TPU v7x, 32 devices: a whole 2x2x4 slice. The times are simulated.
32 devices in a mesh: seq: 8 (over z, x), rep: 4 (over y, core).
Axes of the slice: x: 2, y: 2, z: 4, core: 2. Of those that a mesh axis runs over, the one named last changes fastest.
Arguments:
- start_deter: bfloat16 [64, 512], P(('seq', 'rep')), may hold values from -1 to 1
- post_cat: int32 [64, 64, 32], P(('seq', 'rep')), may hold values from 0 to 31
- embed: bfloat16 [64, 64, 4096], P(('seq', 'rep')), may hold values from -6 to 6
- camera: int32 [64], P(('seq', 'rep')), may hold values from 0 to 1
- start_order: int32 [32, 128], P(('seq', 'rep')), may hold values from 0 to 127, each once within a row
- imag_cat: int32 [2048, 14, 32], P(('seq', 'rep')), may hold values from 0 to 31
- imag_cot: bfloat16 [2048, 15, 512], P(('seq', 'rep')), may hold values from -6 to 6
- stoch_table: bfloat16 [1024, 512], replicated, may hold values from -1 to 1
- stoch_gain: float32 [512], replicated, may hold values from 0.1 to 1.9
- stoch_bias: float32 [512], replicated, may hold values from -3 to 3
- state_weight: bfloat16 [8, 64, 192], replicated, may hold values from -0.25 to 0.25
- input_weight: bfloat16 [512, 1536], replicated, may hold values from -0.25 to 0.25
- cell_gain: float32 [1536], replicated, may hold values from 0.1 to 1.9
- cell_bias: float32 [1536], replicated, may hold values from -3 to 3
- prior_hidden: bfloat16 [512, 512], replicated, may hold values from -0.25 to 0.25
- prior_gain: float32 [512], replicated, may hold values from 0.1 to 1.9
- prior_bias: float32 [512], replicated, may hold values from -3 to 3
- prior_out: bfloat16 [512, 1024], replicated, may hold values from -0.75 to 0.75
- prior_shift: float32 [1024], replicated, may hold values from -3 to 3
- post_deter: bfloat16 [512, 512], replicated, may hold values from -0.09375 to 0.09375
- post_embed: bfloat16 [4096, 512], replicated, may hold values from -0.09375 to 0.09375
- post_gain: float32 [512], replicated, may hold values from 0.1 to 1.9
- post_bias: float32 [512], replicated, may hold values from -3 to 3
- post_out: bfloat16 [512, 1024], replicated, may hold values from -0.75 to 0.75
- post_shift: float32 [1024], replicated, may hold values from -3 to 3
- camera_scale: float32 [2, 4096], replicated, may hold values from 0.1 to 1.9
Outputs:
- imag_deter: float32 [2048, 15, 512], P(('seq', 'rep'))
- embed_grad: float32 [64, 64, 4096], P(('seq', 'rep'))
- start_grad: float32 [64, 512], P(('seq', 'rep'))
- stoch_table_grad: float32 [1024, 512], P('rep')
- stoch_gain_grad: float32 [512], P('rep')
- stoch_bias_grad: float32 [512], P('rep')
- state_weight_grad: float32 [8, 64, 192], P('rep')
- input_weight_grad: float32 [512, 1536], P('rep')
- cell_gain_grad: float32 [1536], P('rep')
- cell_bias_grad: float32 [1536], P('rep')
- prior_hidden_grad: float32 [512, 512], P('rep')
- prior_gain_grad: float32 [512], P('rep')
- prior_bias_grad: float32 [512], P('rep')
- prior_out_grad: float32 [512, 1024], P('rep')
- prior_shift_grad: float32 [1024], P('rep')
- post_deter_grad: float32 [512, 512], P('rep')
- post_embed_grad: float32 [4096, 512], P('rep')
- post_gain_grad: float32 [512], P('rep')
- post_bias_grad: float32 [512], P('rep')
- post_out_grad: float32 [512, 1024], P('rep')
- post_shift_grad: float32 [1024], P('rep')
- camera_scale_grad: float32 [2, 4096], P(None, 'rep')
Inputs may be any that keep to these rules, and one draw needn't show every extreme that they name: `start_order`: each row lists the frames 0 to 127 of one device once each.
All inputs are finite; a program needn't handle non-finite values.
Results may differ from a plain program's by a relative error of at most 0.0095.
Values may be sent and summed in bfloat16 or wider, within the bound.
No kernel may reach another device: no remote copies, remote signals or barrier semaphores. Data moves between devices by JAX's collectives and lax.ppermute only.
A program may use at most 320 MiB of HBM per device.

v0:
```python
import jax
import jax.numpy as jnp
from jax import lax
from jax.sharding import PartitionSpec as P

BLOCKS = 8
GROUPS = 32
CLASSES = 32


epsilon = 1e-05
unimix = 0.01
free_bits = 1.0


def layer_norm(values, factor, offset):
    center = values - jnp.mean(values, -1, keepdims=True)
    spread = jnp.mean(center * center, -1, keepdims=True)
    return center * lax.rsqrt(spread + epsilon) * factor + offset


def norm_silu(values, factor, offset):
    return jax.nn.silu(layer_norm(values, factor, offset))


def gru_update(gate_values, previous, factor, offset):
    row_count = gate_values.shape[0]
    normed = layer_norm(gate_values, factor, offset).reshape(row_count, BLOCKS, 3, -1)
    reset_gate = jax.nn.sigmoid(normed[:, :, 0])
    candidate = jnp.tanh(reset_gate * normed[:, :, 1])
    update_gate = jax.nn.sigmoid(normed[:, :, 2] - 1.0)
    blocked = previous.reshape(row_count, BLOCKS, -1)
    return (update_gate * candidate + (1.0 - update_gate) * blocked).reshape(row_count, -1)


def mixed_probs(logits):
    row_count = logits.shape[0]
    probability = jax.nn.softmax(logits.reshape(row_count, GROUPS, -1), axis=-1)
    return (1.0 - unimix) * probability + unimix / probability.shape[-1]


def summed_losses(post_logits, prior_logits):
    posterior = mixed_probs(post_logits)
    prior_probs = mixed_probs(prior_logits)
    divergence = jnp.sum(posterior * (jnp.log(posterior) - jnp.log(prior_probs)), axis=(1, 2))
    return jnp.sum(1.0 + jax.nn.softplus(divergence - free_bits))


def one_hot(categories):
    matches = categories[..., None] == jnp.arange(CLASSES, dtype=jnp.int32)
    return matches.astype(jnp.bfloat16).reshape(categories.shape[:-1] + (GROUPS * CLASSES,))


def state_part(held_state, state_weight):
    row_count = held_state.shape[0]
    blocked = held_state.reshape(row_count, BLOCKS, -1)
    return jnp.einsum(
        "rbk,bkn->rbn", blocked, state_weight, preferred_element_type=jnp.float32
    ).reshape(row_count, -1)


def state_back(gate_grads, state_weight):
    row_count = gate_grads.shape[0]
    blocked = gate_grads.reshape(row_count, BLOCKS, -1)
    return jnp.einsum(
        "rbn,bkn->rbk", blocked, state_weight, preferred_element_type=jnp.float32
    ).reshape(row_count, -1)


def state_weight_grad(held_state, gate_grads):
    row_count = held_state.shape[0]
    return jnp.einsum(
        "rbk,rbn->bkn",
        held_state.reshape(row_count, BLOCKS, -1),
        gate_grads.reshape(row_count, BLOCKS, -1),
        preferred_element_type=jnp.float32,
    )


def contract_rows(left, right):
    return lax.dot_general(
        left, right, (((0,), (0,)), ((), ())), preferred_element_type=jnp.float32
    )


def times_transpose(left, weight):
    return lax.dot_general(
        left, weight, (((1,), (1,)), ((), ())), preferred_element_type=jnp.float32
    )


def run_forward(start_state, start_held, gate_inputs, state_weight, cell_gain, cell_bias):

    def advance(carry, gate_input):
        current, held_state = carry
        gate_values = gate_input + state_part(held_state, state_weight)
        renewed = gru_update(gate_values, current, cell_gain, cell_bias)
        return ((renewed, renewed.astype(jnp.bfloat16)), (gate_values, renewed))

    return lax.scan(advance, (start_state, start_held), gate_inputs, unroll=8)[1]


def run_backward(arriving_all, gate_all, previous_all, state_weight, cell_gain, cell_bias):

    def retreat(carry, inputs):
        state_grad, gain_grad, bias_grad = carry
        arriving, gate_values, previous = inputs
        pullback = jax.vjp(gru_update, gate_values, previous, cell_gain, cell_bias)[1]
        gate_grad, previous_grad, gain_part, bias_part = pullback(state_grad + arriving)
        gate_low = gate_grad.astype(jnp.bfloat16)
        carried = previous_grad + state_back(gate_low, state_weight)
        return ((carried, gain_grad + gain_part, bias_grad + bias_part), gate_low)

    initial = (
        jnp.zeros(previous_all.shape[1:], jnp.float32),
        jnp.zeros_like(cell_gain),
        jnp.zeros_like(cell_bias),
    )
    return lax.scan(
        retreat, initial, (arriving_all, gate_all, previous_all), reverse=True, unroll=8
    )


def on_device(
    start_deter,
    post_cat,
    embed,
    camera,
    start_order,
    imag_cat,
    imag_cot,
    stoch_table,
    stoch_gain,
    stoch_bias,
    state_weight,
    input_weight,
    cell_gain,
    cell_bias,
    prior_hidden,
    prior_gain,
    prior_bias,
    prior_out,
    prior_shift,
    post_deter,
    post_embed,
    post_gain,
    post_bias,
    post_out,
    post_shift,
    camera_scale,
):
    seq_count, length = (post_cat.shape[0], post_cat.shape[1])
    start_count, horizon = (imag_cot.shape[0], imag_cot.shape[1])
    unit_count = stoch_gain.shape[0]
    frame_rows = seq_count * length
    obs_hot = one_hot(jnp.swapaxes(post_cat, 0, 1).reshape(frame_rows, GROUPS))
    obs_pre = jnp.dot(obs_hot, stoch_table, preferred_element_type=jnp.float32)
    obs_taken = norm_silu(obs_pre, stoch_gain, stoch_bias).astype(jnp.bfloat16)
    obs_inputs = jnp.concatenate(
        [jnp.zeros((seq_count, unit_count), jnp.bfloat16), obs_taken[: frame_rows - seq_count]], 0
    )
    obs_gate_in = jnp.dot(obs_inputs, input_weight, preferred_element_type=jnp.float32).reshape(
        length, seq_count, -1
    )
    start_state = start_deter.astype(jnp.float32)
    obs_gates, obs_states = run_forward(
        start_state, start_deter, obs_gate_in, state_weight, cell_gain, cell_bias
    )
    obs_held = obs_states.reshape(frame_rows, -1).astype(jnp.bfloat16)
    camera_hot = (camera[:, None] == jnp.arange(camera_scale.shape[0], dtype=jnp.int32)).astype(
        jnp.float32
    )
    scale_rows = jnp.sum(camera_hot[:, :, None] * camera_scale[None], axis=1)
    scaled = (embed.astype(jnp.float32) * scale_rows[:, None, :]).astype(jnp.bfloat16)
    scaled_rows = scaled.reshape(frame_rows, -1)
    embed_part = jnp.dot(scaled_rows, post_embed, preferred_element_type=jnp.float32)
    embed_part = jnp.swapaxes(embed_part.reshape(seq_count, length, -1), 0, 1).reshape(
        frame_rows, -1
    )
    prior_pre = jnp.dot(obs_held, prior_hidden, preferred_element_type=jnp.float32)
    prior_act = norm_silu(prior_pre, prior_gain, prior_bias).astype(jnp.bfloat16)
    prior_logits = jnp.dot(prior_act, prior_out, preferred_element_type=jnp.float32) + prior_shift
    post_pre = jnp.dot(obs_held, post_deter, preferred_element_type=jnp.float32) + embed_part
    post_act = norm_silu(post_pre, post_gain, post_bias).astype(jnp.bfloat16)
    post_logits = jnp.dot(post_act, post_out, preferred_element_type=jnp.float32) + post_shift
    loss_pull = jax.vjp(summed_losses, post_logits, prior_logits)[1]
    post_log_grad, prior_log_grad = loss_pull(jnp.ones((), jnp.float32))
    chosen = start_order[0, :start_count]
    frame_index = chosen % length * seq_count + chosen // length
    start_held = jnp.take(obs_held, frame_index, axis=0)
    start_taken = jnp.take(obs_taken, frame_index, axis=0)
    got_held, got_taken = (
        lax.all_to_all(start_held, "seq", split_axis=0, concat_axis=0, tiled=True),
        lax.all_to_all(start_taken, "seq", split_axis=0, concat_axis=0, tiled=True),
    )
    imag_hot = one_hot(jnp.swapaxes(imag_cat, 0, 1).reshape((horizon - 1) * start_count, GROUPS))
    imag_pre = jnp.dot(imag_hot, stoch_table, preferred_element_type=jnp.float32)
    imag_taken = norm_silu(imag_pre, stoch_gain, stoch_bias).astype(jnp.bfloat16)
    imag_inputs = jnp.concatenate([got_taken, imag_taken], 0)
    imag_gate_in = jnp.dot(imag_inputs, input_weight, preferred_element_type=jnp.float32).reshape(
        horizon, start_count, -1
    )
    got_state = got_held.astype(jnp.float32)
    imag_gates, imag_states = run_forward(
        got_state, got_held, imag_gate_in, state_weight, cell_gain, cell_bias
    )
    imag_deter = jnp.swapaxes(imag_states, 0, 1)
    imag_previous = jnp.concatenate([got_state[None], imag_states[:-1]], 0)
    imag_back, imag_gate_low = run_backward(
        jnp.swapaxes(imag_cot, 0, 1).astype(jnp.float32),
        imag_gates,
        imag_previous,
        state_weight,
        cell_gain,
        cell_bias,
    )
    first_grad, imag_gain_grad, imag_bias_grad = imag_back
    imag_gate_rows = imag_gate_low.reshape(horizon * start_count, -1)
    imag_input_grad = times_transpose(imag_gate_rows, input_weight)
    input_grad_sum = contract_rows(imag_inputs, imag_gate_rows)
    imag_held_prev = jnp.concatenate(
        [got_held, imag_states[:-1].reshape((horizon - 1) * start_count, -1).astype(jnp.bfloat16)],
        0,
    )
    state_grad_sum = state_weight_grad(imag_held_prev, imag_gate_rows)
    back_held, back_taken = (
        lax.all_to_all(
            first_grad.astype(jnp.bfloat16), "seq", split_axis=0, concat_axis=0, tiled=True
        ),
        lax.all_to_all(
            imag_input_grad[:start_count].astype(jnp.bfloat16),
            "seq",
            split_axis=0,
            concat_axis=0,
            tiled=True,
        ),
    )
    imag_pull = jax.vjp(norm_silu, imag_pre, stoch_gain, stoch_bias)[1]
    imag_pre_grad, stoch_gain_grad, stoch_bias_grad = imag_pull(imag_input_grad[start_count:])
    table_grad_sum = contract_rows(imag_hot, imag_pre_grad.astype(jnp.bfloat16))
    post_log_low = post_log_grad.astype(jnp.bfloat16)
    post_out_grad = contract_rows(post_act, post_log_low)
    post_shift_grad = jnp.sum(post_log_low.astype(jnp.float32), 0)
    post_pull = jax.vjp(norm_silu, post_pre, post_gain, post_bias)[1]
    post_pre_grad, post_gain_grad, post_bias_grad = post_pull(
        times_transpose(post_log_low, post_out)
    )
    post_pre_low = post_pre_grad.astype(jnp.bfloat16)
    post_deter_grad = contract_rows(obs_held, post_pre_low)
    prior_log_low = prior_log_grad.astype(jnp.bfloat16)
    prior_out_grad = contract_rows(prior_act, prior_log_low)
    prior_shift_grad = jnp.sum(prior_log_low.astype(jnp.float32), 0)
    prior_pull = jax.vjp(norm_silu, prior_pre, prior_gain, prior_bias)[1]
    prior_pre_grad, prior_gain_grad, prior_bias_grad = prior_pull(
        times_transpose(prior_log_low, prior_out)
    )
    prior_pre_low = prior_pre_grad.astype(jnp.bfloat16)
    prior_hidden_grad = contract_rows(obs_held, prior_pre_low)
    held_grad = times_transpose(post_pre_low, post_deter) + times_transpose(
        prior_pre_low, prior_hidden
    )
    held_grad = held_grad.at[frame_index].add(back_held.astype(jnp.float32))
    post_seq = jnp.swapaxes(post_pre_low.reshape(length, seq_count, -1), 0, 1).reshape(
        frame_rows, -1
    )
    post_embed_grad = contract_rows(scaled_rows, post_seq)
    scaled_grad = times_transpose(post_seq, post_embed).reshape(seq_count, length, -1)
    embed_grad = scaled_grad * scale_rows[:, None, :]
    seq_terms = jnp.sum(scaled_grad * embed.astype(jnp.float32), 1)
    camera_scale_grad = jnp.sum(camera_hot[:, :, None] * seq_terms[:, None, :], axis=0)
    obs_previous = jnp.concatenate([start_state[None], obs_states[:-1]], 0)
    obs_back, obs_gate_low = run_backward(
        held_grad.reshape(length, seq_count, -1),
        obs_gates,
        obs_previous,
        state_weight,
        cell_gain,
        cell_bias,
    )
    start_grad, obs_gain_grad, obs_bias_grad = obs_back
    obs_gate_rows = obs_gate_low.reshape(frame_rows, -1)
    obs_input_grad = times_transpose(obs_gate_rows, input_weight)
    input_grad_sum = input_grad_sum + contract_rows(obs_inputs, obs_gate_rows)
    obs_held_prev = jnp.concatenate([start_deter, obs_held[: frame_rows - seq_count]], 0)
    state_grad_sum = state_grad_sum + state_weight_grad(obs_held_prev, obs_gate_rows)
    taken_grad = jnp.concatenate(
        [obs_input_grad[seq_count:], jnp.zeros((seq_count, unit_count), jnp.float32)], 0
    )
    taken_grad = taken_grad.at[frame_index].add(back_taken.astype(jnp.float32))
    obs_pull = jax.vjp(norm_silu, obs_pre, stoch_gain, stoch_bias)[1]
    obs_pre_grad, gain_more, bias_more = obs_pull(taken_grad)
    table_grad_sum = table_grad_sum + contract_rows(obs_hot, obs_pre_grad.astype(jnp.bfloat16))
    gradients = [
        table_grad_sum,
        stoch_gain_grad + gain_more,
        stoch_bias_grad + bias_more,
        state_grad_sum,
        input_grad_sum,
        imag_gain_grad + obs_gain_grad,
        imag_bias_grad + obs_bias_grad,
        prior_hidden_grad,
        prior_gain_grad,
        prior_bias_grad,
        prior_out_grad,
        prior_shift_grad,
        post_deter_grad,
        post_embed_grad,
        post_gain_grad,
        post_bias_grad,
        post_out_grad,
        post_shift_grad,
        camera_scale_grad,
    ]
    split_dims = (0, 0, 0, 0, 0, 0, 0, 0, 0, 0, 0, 0, 0, 0, 0, 0, 0, 0, 1)
    summed = lax.psum(
        (
            gradients[0],
            gradients[1],
            gradients[2],
            gradients[3],
            gradients[4],
            gradients[5],
            gradients[6],
            gradients[7],
            gradients[8],
            gradients[9],
            gradients[10],
            gradients[11],
            gradients[12],
            gradients[13],
            gradients[14],
            gradients[15],
            gradients[16],
            gradients[17],
            gradients[18],
        ),
        ("seq", "rep"),
    )
    rep_index = lax.axis_index("rep")
    rep_count = lax.axis_size("rep")
    kept = []
    for member, axis_dim in zip(summed, split_dims):
        share = member.shape[axis_dim] // rep_count
        kept.append(lax.dynamic_slice_in_dim(member, rep_index * share, share, axis_dim))
    return (imag_deter, embed_grad, start_grad) + tuple(kept)


def solution(mesh):
    in_specs = (
        P(("seq", "rep"), None),
        P(("seq", "rep"), None, None),
        P(("seq", "rep"), None, None),
        P(("seq", "rep")),
        P(("seq", "rep"), None),
        P(("seq", "rep"), None, None),
        P(("seq", "rep"), None, None),
        P(),
        P(),
        P(),
        P(),
        P(),
        P(),
        P(),
        P(),
        P(),
        P(),
        P(),
        P(),
        P(),
        P(),
        P(),
        P(),
        P(),
        P(),
        P(),
    )
    out_specs = (
        P(("seq", "rep"), None, None),
        P(("seq", "rep"), None, None),
        P(("seq", "rep"), None),
        P("rep", None),
        P("rep"),
        P("rep"),
        P("rep", None, None),
        P("rep", None),
        P("rep"),
        P("rep"),
        P("rep", None),
        P("rep"),
        P("rep"),
        P("rep", None),
        P("rep"),
        P("rep", None),
        P("rep", None),
        P("rep"),
        P("rep"),
        P("rep", None),
        P("rep"),
        P(None, "rep"),
    )
    return jax.shard_map(
        on_device, mesh=mesh, in_specs=in_specs, out_specs=out_specs, check_vma=False
    )
```

profile of v0, /device:TPU:0, one launch (start us, length us, event | category | flops | bytes accessed | tf_op | source)
XLA Modules:
  0.0 1699.6 jit_solution(15587871125505432326)
XLA Ops:
  16.4 136.2 %while.56 = (s32[]{:T(128)}, f32[2,512]{1,0:T(2,128)S(1)}, bf16[2,512]{1,0:T(2,128)(2,1)S(1)}, f32[8,8,2,1536]{3,2,1,0:T(2,128)}, f32[8,8,2,512]{3,2,1,0:T(2,128...) while((s32[]{:T(128)}, f32[2,512]{1,0:T(2,128)S(1)}, ...), condition=%wide.region_21.23_spmd, body=%wide.region_4.22_spmd.sunk | while | flops 3547159 | bytes 4703109 | solution.py:100
  158.4 7.6 all-to-all-start.1
  170.8 3.0 fusion.304
  216.2 3.4 convert_reduce_fusion.1
  235.4 2.9 fusion.941
  239.7 5.7 fusion.301
  245.3 4.6 convolution_bitcast_fusion.16
  252.3 12.9 bitcast_compare_fusion
  287.7 6.0 all-to-all-start
  296.6 4.1 all-to-all-done
  300.6 2.9 fusion.380
  314.6 3.4 multiply_add_fusion.26
  330.5 2.9 multiply_add_fusion.39
  343.5 2.9 multiply_add_fusion.38
  358.2 2.9 squeeze.787
  361.1 3.0 multiply_add_fusion.37
  379.1 2.9 multiply_add_fusion.36
  397.2 3.0 multiply_add_fusion.35
  415.3 3.0 multiply_add_fusion.34
  453.5 2.9 multiply_add_fusion.33
  472.1 3.0 multiply_add_fusion.32
  491.3 3.0 multiply_add_fusion.31
  507.4 2.7 squeeze.811
  510.1 3.0 multiply_add_fusion.30
  528.8 3.0 multiply_add_fusion.29
  547.4 3.0 multiply_add_fusion.28
  591.6 2.9 multiply_add_fusion.27
  598.2 7.1 multiply_multiply_fusion.27
  609.3 2.6 copy.1489
  651.1 2.6 copy.1499
  671.5 2.6 copy.1504
  749.6 2.9 fusion.1009
  780.5 2.8 reshape.12078
  874.1 2.6 copy.1554
  895.9 2.8 multiply_reduce_fusion.35
  912.9 7.3 reshape_reshape.16
  920.2 4.9 fusion.1015
  925.1 5.4 fusion.379
  965.1 4.4 all-to-all-start.2
  969.5 4.2 multiply_reduce_fusion.32
  981.3 3.4 copy.1562
  991.1 4.3 fusion.340
  998.8 6.0 all-to-all-start.3
  1007.3 189.0 %while.57 = (s32[]{:T(128)}, f32[2,512]{1,0:T(2,128)S(1)}, f32[1536]{0:T(1024)S(1)}, f32[1536]{0:T(1024)S(1)}, bf16[8,8,2,1536]{3,2,1,0:T(2,128)(2,1)S(1)}, /*in...) while((s32[]{:T(128)}, f32[2,512]{1,0:T(2,128)S(1)}, ...), condition=%wide.wide.region_148.150_spmd.clone, body=%wide.wide.region_99.149_spmd.clone.sunk | while | flops 4436090 | bytes 6275032 | solution.py:119
  1202.8 4.3 convolution_add_fusion
  1228.2 109.8 %all-reduce.76.cloned.1.call-done = (f32[512]{0:T(512)}, f32[512]{0:T(512)}, f32[1536]{0:T(1024)}, f32[1536]{0:T(1024)}, f32[512]{0:T(512)}, /*index=5*/f32[512]...) async-done(((f32[512]{0:T(512)}, f32[512]{0:T(512)}, f32[1536]{0:T(1024)}, f32[1536]{0:T(1024)}, f32[512]{0:T(512)}, ...) | async-done | bytes 65552 | tf_op jit(solution)/shard_map/psum | solution.py:315
  1352.0 324.8 %all-reduce.78.cloned.1.call-done = (f32[1024,512]{1,0:T(8,128)}, f32[8,64,192]{2,1,0:T(8,128)}, f32[512,1536]{1,0:T(8,128)}, f32[512,512]{1,0:T(8,128)}, f32[51...) async-done(((f32[1024,512]{1,0:T(8,128)}, f32[8,64,192]{2,1,0:T(8,128)}, f32[512,1536]{1,0:T(8,128)}, f32[512,512]{1,0:T(8,128)}, ...) | async-done | bytes 20316176 | tf_op jit(solution)/shard_map/psum | solution.py:315
  1686.0 3.1 constant_dynamic-slice_fusion.34
  (4962 shorter events, 1064.6 us)
Async XLA Ops:
  152.6 15.6 copy-start.201
  152.6 18.2 %copy-start.24 = (bf16[2,64,4096]{2,1,0:T(8,128)(2,1)S(1)}, bf16[2,64,4096]{2,1,0:T(8,128)(2,1)}, u32[]{:S(2)}) copy-start(bf16[2,64,4096]{2,1,0:T(8,128)(2,1)} %param.34) | copy-start | bytes 3145732
  158.4 129.3 %all-to-all-start.1 = ((bf16[8,8,512]{2,1,0:T(8,128)(2,1)}), bf16[8,8,512]{2,1,0:T(8,128)(2,1)}, u32[]{:S(2)}, u32[]{:S(2)}) async-start(bf16[8,8,512]{2,1,0:T(8,128)(2,1)} %get-tuple-element.1011), calls=%async_computation.1 | async-start | bytes 131072 | tf_op jit(solution)/shard_map/all_to_all | solution.py:193
  250.0 15.2 copy-start.244
  270.1 9.4 copy-start.279
  271.1 9.2 copy-start.278
  271.2 10.0 copy-start.277
  272.0 10.0 copy-start.276
  273.7 9.0 copy-start.275
  287.7 12.9 all-to-all-start
  294.7 23.3 %copy-start.147 = (bf16[64,8,64]{2,1,0:T(8,128)(2,1)}, bf16[64,8,64]{2,1,0:T(8,128)(2,1)S(1)}, u32[]{:S(2)}) copy-start(bf16[64,8,64]{2,1,0:T(8,128)(2,1)S(1)} %reshape.12023) | copy-start | bytes 196612
  308.9 9.1 copy-start.28
  319.0 14.4 copy-start.121
  965.1 33.7 %all-to-all-start.2 = ((bf16[8,8,512]{2,1,0:T(8,128)(2,1)}), bf16[8,8,512]{2,1,0:T(8,128)(2,1)}, u32[]{:S(2)}, u32[]{:S(2)}) async-start(bf16[8,8,512]{2,1,0:T(8,128)(2,1)} %convert_element_type.757), calls=%async_computation.2 | async-start | bytes 131072 | tf_op jit(solution)/shard_map/all_to_all | solution.py:227
  981.2 9.1 copy-start.413
  981.2 9.0 copy-start.414
  981.2 9.0 copy-start.416
  981.2 9.0 copy-start.418
  981.2 9.0 copy-start.420
  981.2 9.0 copy-start.422
  981.2 9.0 copy-start.424
  981.3 9.0 copy-start.426
  981.3 9.0 copy-start.428
  981.3 9.0 copy-start.430
  981.3 9.0 copy-start.432
  981.3 9.0 copy-start.433
  981.3 9.0 copy-start.435
  981.3 9.0 copy-start.437
  981.3 9.0 copy-start.439
  981.3 9.7 copy-start.271
  995.4 9.4 copy-start.243
  995.4 11.9 copy-start.27
  995.4 11.9 copy-start.341
  995.4 11.9 copy-start.344
  995.4 11.9 copy-start.399
  998.8 201.9 %all-to-all-start.3 = ((bf16[8,8,512]{2,1,0:T(8,128)(2,1)}), bf16[8,8,512]{2,1,0:T(8,128)(2,1)}, u32[]{:S(2)}, u32[]{:S(2)}) async-start(bf16[8,8,512]{2,1,0:T(8,128)(2,1)} %fusion.901), calls=%async_computation.3 | async-start | bytes 131072 | tf_op jit(solution)/shard_map/all_to_all | solution.py:230
  1004.8 333.2 %all-reduce.76.cloned.1.call-start = ((), (), s32[]{:S(2)}) async-start(), calls=%async_computation.4 | async-start | bytes 139264 | tf_op jit(solution)/shard_map/psum | solution.py:315
  1211.5 465.3 %all-reduce.78.cloned.1.call-start = ((), (), s32[]{:S(2)}) async-start(), calls=%async_computation.5 | async-start | bytes 40894464 | tf_op jit(solution)/shard_map/psum | solution.py:315
  1212.7 9.4 copy-start.223
  1212.7 10.1 copy-start.225
  1213.6 9.9 copy-start.227
  1213.7 10.4 copy-start.229
  1213.8 11.1 copy-start.231
  1214.5 11.0 copy-start.233
  1214.5 11.6 copy-start.235
  1216.4 10.4 copy-start.236
  1218.1 9.3 copy-start.338
  1218.2 9.3 copy-start.339
  (581 other events, 2004.6 us)
Sparse Core Ops, SparseCore 0:
  1211.7 126.2 all-reduce.75
  1346.1 330.7 all-reduce.77
where the time goes:
time: 1710 us; the launch traced here: 1700 us
  local copies, waits for them, and re-layouts  658 us (38%)
  other arithmetic  445 us (26%)
  waiting for transfers between devices  439 us (26%)
  matrix products  107 us (6%)
  starting transfers between devices  24 us (1%)
  between operations  21 us (1%)
    psum x2, waiting for transfers between devices, on_device(): lax.psum((gradients[0], gradients[1], gradients[2], gradients[3], gradien...  435 us
    reshape x222, local copies, waits for them, and re-layouts, gru_update(): layer_norm(gate_values, factor, offset).reshape(row_count, BLOCKS, 3, -1)  85.5 us
    reduce_sum x159, other arithmetic, layer_norm(): return center * lax.rsqrt(spread + epsilon) * factor + offset  84.2 us
    reshape x222, local copies, waits for them, and re-layouts, state_part(): return jnp.einsum('rbk,bkn->rbn', blocked, state_weight, preferred_elemen...  78.3 us
    unnamed x1260, local copies, waits for them, and re-layouts  75.7 us
    add_any x93, local copies, waits for them, and re-layouts, gru_update(): reset_gate = jax.nn.sigmoid(normed[:, :, 0])  69.1 us
    squeeze x92, local copies, waits for them, and re-layouts, run_forward(): lax.scan(advance, (start_state, start_held), gate_inputs, unroll=8)[1]  67.5 us
    add x88, other arithmetic, layer_norm(): return center * lax.rsqrt(spread + epsilon) * factor + offset  52.4 us

commit v1 on v0

v1 whole, which is shorter than its diff:
```python
import jax
import jax.numpy as jnp
from jax import lax
from jax.experimental import pallas as pl
from jax.experimental.pallas import tpu as pltpu
from jax.sharding import PartitionSpec as P

BLOCKS = 8
GROUPS = 32
CLASSES = 32
PAIRS = BLOCKS // 2
LANES = 128
GATE = 3 * LANES

epsilon = 1e-05
unimix = 0.01
free_bits = 1.0

f32 = jnp.float32
bf16 = jnp.bfloat16


def iota(shape, axis):
    return lax.broadcasted_iota(jnp.int32, shape, axis)


def mm(left, right):
    return jnp.dot(left, right, preferred_element_type=f32)


def mm_nt(left, right):
    return lax.dot_general(left, right, (((1,), (1,)), ((), ())), preferred_element_type=f32)


def mm_tn(left, right):
    return lax.dot_general(left, right, (((0,), (0,)), ((), ())), preferred_element_type=f32)


def sigmoid(values):
    return 0.5 * jnp.tanh(0.5 * values) + 0.5


def row_mean(values):
    return jnp.sum(values, -1, keepdims=True) * (1.0 / values.shape[-1])


def hot_rows(columns):
    categories = jnp.concatenate([part.astype(f32).T for part in columns], 0).astype(bf16)
    count = categories.shape[0]
    width = GROUPS * CLASSES
    spread = (iota((GROUPS, width), 1) // CLASSES == iota((GROUPS, width), 0)).astype(f32)
    wide = mm(categories, spread.astype(bf16))
    own = (iota((count, width), 1) % CLASSES).astype(f32)
    return jnp.where(wide == own, 1.0, 0.0).astype(bf16)


def normed(values):
    center = values - row_mean(values)
    scale = lax.rsqrt(row_mean(center * center) + epsilon)
    return center * scale, scale


def norm_silu(values, factor, offset):
    act = normed(values)[0] * factor + offset
    return act * sigmoid(act)


def norm_silu_back(values, factor, offset, grad):
    unit, scale = normed(values)
    act = unit * factor + offset
    gate = sigmoid(act)
    act_grad = grad * (gate + act * gate * (1.0 - gate))
    unit_grad = act_grad * factor
    pre_grad = scale * (unit_grad - row_mean(unit_grad) - unit * row_mean(unit_grad * unit))
    return (
        pre_grad,
        jnp.sum(act_grad * unit, 0, keepdims=True),
        jnp.sum(act_grad, 0, keepdims=True),
    )


def pick_columns(chosen, count):
    return jnp.where(iota((count, chosen.shape[1]), 0) == chosen, 1.0, 0.0).astype(bf16)


def column_order():
    source, target = iota((GATE, GATE), 0), iota((GATE, GATE), 1)
    half = LANES // 2
    moved = source // half % 3 * LANES + source // (3 * half) * half + source % half
    return jnp.where(moved == target, 1.0, 0.0).astype(bf16)


def pair_row(ref, pair):
    half = LANES // 2
    return jnp.concatenate(
        [
            ref[:, pair * GATE + (3 * e + p) * half : pair * GATE + (3 * e + p + 1) * half]
            for p in range(3)
            for e in range(2)
        ],
        1,
    )


def plain_row(row):
    half = LANES // 2
    return jnp.concatenate(
        [
            row[:, (2 * p + e) * half : (2 * p + e + 1) * half]
            for e in range(2)
            for p in range(3)
        ],
        1,
    )


def group_sum(values):
    values = values + pltpu.roll(values, 4, 0)
    return values + pltpu.roll(values, 2, 0)


def lanes_of(pair):
    return slice(pair * LANES, (pair + 1) * LANES)


def gates_of(pair):
    return slice(pair * GATE, (pair + 1) * GATE)


def scale_row(camera_ref, camera_scale_ref, s, columns):
    row = None
    for c in range(camera_scale_ref.shape[0]):
        part = jnp.where(camera_ref[s] == c, camera_scale_ref[c : c + 1, columns], 0.0)
        row = part if row is None else row + part
    return row


def observe_kernel(
    cat_ref,
    table_ref,
    stoch_gain_ref,
    stoch_bias_ref,
    input_ref,
    weight_ref,
    cell_gain_ref,
    cell_bias_ref,
    start_ref,
    order_ref,
    held_ref,
    taken_ref,
    pre_ref,
    gates_ref,
    states_ref,
    sent_ref,
    ordered_ref,
    state_ref,
    cell_ref,
    inputs_ref,
):
    frames, width = held_ref.shape
    length = frames // 2
    half = LANES // 2
    pre = mm(hot_rows([cat_ref[s] for s in range(2)]), table_ref[...])
    pre_ref[...] = pre
    taken = norm_silu(pre, stoch_gain_ref[...], stoch_bias_ref[...]).astype(bf16)
    taken_ref[...] = taken
    order = column_order()
    for pair in range(PAIRS):
        columns = mm(input_ref[:, gates_of(pair)], order).astype(bf16)
        ordered_ref[:, gates_of(pair)] = columns
        values = mm(taken, columns)
        for p in range(3):
            at = p * PAIRS * frames + pair * frames
            inputs_ref[at : at + frames, :] = values[:, lanes_of(p)]
    source, target = iota((3 * half, GATE), 0), iota((3 * half, GATE), 1)
    same = (source // half == target // LANES) & (source % half == target % half)
    weights = mm(weight_ref[...], jnp.where(same, 1.0, 0.0).astype(bf16))
    own = iota(weights.shape, 0) // half % 2 == iota(weights.shape, 1) // half % 2
    state_ref[...] = jnp.where(own, weights, 0.0).astype(bf16)
    gain_rows = [pair_row(cell_gain_ref, pair) for pair in range(PAIRS)]
    bias_rows = [pair_row(cell_bias_ref, pair) for pair in range(PAIRS)]
    cell_ref[...] = jnp.concatenate(
        [jnp.concatenate(gain_rows, 1), jnp.concatenate(bias_rows, 1)], 0
    )
    row_pair = iota((8, LANES), 0) // 2
    part = iota((8, GATE), 1) // LANES
    smaller = jnp.where(part == 1, 1.0, 0.5)
    gain = jnp.concatenate([row for row in gain_rows for _ in range(2)], 0) * smaller
    bias = jnp.concatenate([row for row in bias_rows for _ in range(2)], 0)
    bias = (bias - jnp.where(part == 2, 1.0, 0.0)) * smaller
    start = jnp.concatenate(
        [start_ref[:, lanes_of(pair)].astype(f32) for pair in range(PAIRS)], 0
    )
    scale = 1.0 / (PAIRS * GATE)

    def advance(step, state, first=False):
        wide = jnp.concatenate([jnp.where(row_pair == j, state, 0.0) for j in range(PAIRS)], 1)
        values = mm(wide.astype(bf16), state_ref[...])
        parts = [values[:, lanes_of(p)] for p in range(3)]
        for p in range(3):
            at = p * PAIRS * frames + step
            if not first:
                parts[p] = parts[p] + inputs_ref[pl.ds(at - 1, 8, stride=length), :]
            gates_ref[pl.ds(at, 8, stride=length), :] = parts[p]
        total = parts[0] + parts[1] + parts[2]
        square = parts[0] * parts[0] + parts[1] * parts[1] + parts[2] * parts[2]
        mean = jnp.sum(group_sum(total), 1, keepdims=True) * scale
        spread = jnp.sum(group_sum(square), 1, keepdims=True) * scale - mean * mean
        factor = lax.rsqrt(jnp.maximum(spread, 0.0) + epsilon)
        units = [
            (parts[p] - mean) * (factor * gain[:, lanes_of(p)]) + bias[:, lanes_of(p)]
            for p in range(3)
        ]
        reset = 0.5 * jnp.tanh(units[0]) + 0.5
        update = 0.5 * jnp.tanh(units[2]) + 0.5
        renewed = state + update * (jnp.tanh(reset * units[1]) - state)
        states_ref[pl.ds(step, 8, stride=length), :] = renewed
        return renewed

    for ref in (taken_ref, pre_ref, ordered_ref, state_ref, cell_ref):
        ref.flush()
    state = advance(0, start, True)
    lax.fori_loop(1, length, advance, state, unroll=7)
    gates_ref.flush()
    states_ref.flush()
    for pair in range(PAIRS):
        held_ref[:, lanes_of(pair)] = states_ref[pair * frames : (pair + 1) * frames, :].astype(
            bf16
        )
    chosen = pick_columns(order_ref[:, : sent_ref.shape[0]], frames)
    held_ref.flush()
    sent_ref[:, :width] = mm_tn(chosen, held_ref[...]).astype(bf16)
    sent_ref[:, width:] = mm_tn(chosen, taken).astype(bf16)


def mixed_probs(logits):
    shifted = jnp.exp(logits - jnp.max(logits, 1, keepdims=True))
    probability = shifted / jnp.sum(shifted, 1, keepdims=True)
    return probability, (1.0 - unimix) * probability + unimix / CLASSES


def softmax_back(probability, grad):
    grad = (1.0 - unimix) * grad
    return probability * (grad - jnp.sum(probability * grad, 1, keepdims=True))


def heads_kernel(
    core_ref,
    camera_ref,
    held_ref,
    embed_ref,
    camera_scale_ref,
    prior_hidden_ref,
    prior_gain_ref,
    prior_bias_ref,
    prior_out_ref,
    prior_shift_ref,
    post_deter_ref,
    post_embed_ref,
    post_gain_ref,
    post_bias_ref,
    post_out_ref,
    post_shift_ref,
    post_low_ref,
    prior_low_ref,
    small_ref,
    keep_ref,
    send_ref,
    post_act_ref,
    prior_act_ref,
    scaled_ref,
):
    frames, width = held_ref.shape
    features = embed_ref.shape[1]
    length = frames // 2
    held = held_ref[...]
    for s in range(2):
        rows = slice(s * length, (s + 1) * length)
        scale = scale_row(camera_ref, camera_scale_ref, s, slice(0, features))
        scaled_ref[rows, :] = (embed_ref[rows, :].astype(f32) * scale).astype(bf16)
    post_pre = mm(held, post_deter_ref[...]) + mm(scaled_ref[...], post_embed_ref[...])
    prior_pre = mm(held, prior_hidden_ref[...])
    post_act = norm_silu(post_pre, post_gain_ref[...], post_bias_ref[...]).astype(bf16)
    prior_act = norm_silu(prior_pre, prior_gain_ref[...], prior_bias_ref[...]).astype(bf16)
    post_logits = mm(post_act, post_out_ref[...]) + post_shift_ref[...]
    prior_logits = mm(prior_act, prior_out_ref[...]) + prior_shift_ref[...]
    split = (GROUPS, CLASSES, frames)
    post_prob, post_mix = mixed_probs(post_logits.T.reshape(split))
    prior_prob, prior_mix = mixed_probs(prior_logits.T.reshape(split))
    ratio = jnp.log(post_mix) - jnp.log(prior_mix)
    divergence = jnp.sum(jnp.sum(post_mix * ratio, 0, keepdims=True), 1, keepdims=True)
    slope = sigmoid(divergence - free_bits)
    post_log = softmax_back(post_prob, slope * (ratio + 1.0))
    prior_log = softmax_back(prior_prob, -slope * (post_mix / prior_mix))
    post_log = post_log.reshape(GROUPS * CLASSES, frames).T.astype(bf16)
    prior_log = prior_log.reshape(GROUPS * CLASSES, frames).T.astype(bf16)
    post_low, post_gain_grad, post_bias_grad = norm_silu_back(
        post_pre, post_gain_ref[...], post_bias_ref[...], mm_nt(post_log, post_out_ref[...])
    )
    prior_low, prior_gain_grad, prior_bias_grad = norm_silu_back(
        prior_pre, prior_gain_ref[...], prior_bias_ref[...], mm_nt(prior_log, prior_out_ref[...])
    )
    post_low, prior_low = post_low.astype(bf16), prior_low.astype(bf16)
    post_low_ref[...] = post_low
    prior_low_ref[...] = prior_low
    post_low_ref.flush()
    prior_low_ref.flush()
    small_ref[...] = jnp.concatenate(
        [
            post_gain_grad,
            post_bias_grad,
            prior_gain_grad,
            prior_bias_grad,
            jnp.sum(post_log.astype(f32), 0, keepdims=True),
            jnp.sum(prior_log.astype(f32), 0, keepdims=True),
        ],
        1,
    )
    post_act_ref[...] = post_act
    prior_act_ref[...] = prior_act
    products = (
        (held_ref, post_low),
        (held_ref, prior_low),
        (post_act_ref, post_log[:, :width]),
        (post_act_ref, post_log[:, width:]),
        (prior_act_ref, prior_log[:, :width]),
        (prior_act_ref, prior_log[:, width:]),
    )
    shares = keep_ref.shape[0] // 2
    unit_rows, embed_rows = width // shares, features // shares
    small, large = unit_rows // 4, embed_rows // 4
    for slot, ref in ((1, send_ref), (0, keep_ref)):
        parity = core_ref[0] ^ slot
        for y in range(shares // 2):
            share = 2 * y + parity
            places = [block_place(parity, y, block) for block in range(4)]
            for block in range(4):
                at = pl.multiple_of(share * embed_rows + block * large, large)
                grad = mm_tn(scaled_ref[:, pl.ds(at, large)], post_low)
                ref[places[block], :large, :] = grad.astype(bf16)
            at = pl.multiple_of(share * unit_rows, unit_rows)
            for index, (left, right) in enumerate(products):
                grad = mm_tn(left[:, pl.ds(at, unit_rows)], right).astype(bf16)
                first = large + index * small
                for block in range(4):
                    ref[places[block], first : first + small, :] = grad[
                        block * small : (block + 1) * small
                    ]
        ref.flush()


def block_place(parity, y, block):
    low_bit, next_bit = block // 2, block % 2
    return jnp.where(
        parity == 0, 4 * y + 2 * low_bit + next_bit, 4 * next_bit + 2 * y + low_bit
    )


def embed_back_kernel(
    camera_ref,
    embed_ref,
    camera_scale_ref,
    post_low_ref,
    prior_low_ref,
    post_embed_ref,
    post_deter_ref,
    prior_hidden_ref,
    held_grad_ref,
    embed_grad_ref,
    camera_grad_ref,
):
    frames, features = embed_ref.shape
    length = frames // 2
    cameras = camera_scale_ref.shape[0]
    held_grad_ref[...] = mm_nt(post_low_ref[...], post_deter_ref[...]) + mm_nt(
        prior_low_ref[...], prior_hidden_ref[...]
    )
    wide = features // 4
    for q in range(4):
        columns = slice(q * wide, (q + 1) * wide)
        scaled_grad = mm_nt(post_low_ref[...], post_embed_ref[columns, :])
        terms = [jnp.zeros((1, wide), f32) for _ in range(cameras)]
        for s in range(2):
            rows = slice(s * length, (s + 1) * length)
            part = scaled_grad[rows]
            scale = scale_row(camera_ref, camera_scale_ref, s, columns)
            embed_grad_ref[rows, columns] = part * scale
            term = jnp.sum(part * embed_ref[rows, columns].astype(f32), 0, keepdims=True)
            for c in range(cameras):
                terms[c] = terms[c] + jnp.where(camera_ref[s] == c, term, 0.0)
        camera_grad_ref[:, columns] = jnp.concatenate(terms, 0)


def cell_gates(units, cell_ref, pair):
    scaled = units * cell_ref[:1, gates_of(pair)] + cell_ref[1:, gates_of(pair)]
    reset = sigmoid(scaled[:, :LANES])
    middle = scaled[:, LANES : 2 * LANES]
    return reset, middle, jnp.tanh(reset * middle), sigmoid(scaled[:, 2 * LANES :] - 1.0)


def rollout_kernel(
    got_ref,
    cat_ref,
    table_ref,
    stoch_gain_ref,
    stoch_bias_ref,
    ordered_ref,
    state_ref,
    cell_ref,
    states_ref,
    inputs_ref,
    held_ref,
    pre_ref,
    unit_ref,
    scale_ref,
):
    horizon, count, width = states_ref.shape
    inputs_ref[:count, :] = got_ref[:, width:]
    for at in range(0, horizon - 1, 2):
        rows = slice(at * count, (at + 2) * count)
        pre = mm(hot_rows([cat_ref[at], cat_ref[at + 1]]), table_ref[...])
        pre_ref[rows, :] = pre
        inputs_ref[(at + 1) * count : (at + 3) * count, :] = norm_silu(
            pre, stoch_gain_ref[...], stoch_bias_ref[...]
        ).astype(bf16)
    chunk = 3 * count
    for at in range(0, horizon * count, chunk):
        rows = slice(at, at + chunk)
        unit_ref[rows, :] = mm(inputs_ref[rows, :], ordered_ref[...])
    norm = 1.0 / (PAIRS * GATE)

    def advance(step, state):
        rows = pl.ds(pl.multiple_of(step * count, count), count)
        held = state.astype(bf16)
        held_ref[rows, :] = held
        values = []
        total = jnp.zeros((count, LANES), f32)
        square = jnp.zeros((count, LANES), f32)
        for pair in range(PAIRS):
            value = unit_ref[rows, gates_of(pair)] + mm(
                held[:, lanes_of(pair)], state_ref[lanes_of(pair), :]
            )
            values.append(value)
            for p in range(3):
                piece = value[:, lanes_of(p)]
                total = total + piece
                square = square + piece * piece
        mean = jnp.sum(total, 1, keepdims=True) * norm
        spread = jnp.sum(square, 1, keepdims=True) * norm - mean * mean
        factor = lax.rsqrt(jnp.maximum(spread, 0.0) + epsilon)
        scale_ref[rows, :] = jnp.broadcast_to(factor, (count, LANES))
        fresh = []
        for pair in range(PAIRS):
            units = (values[pair] - mean) * factor
            unit_ref[rows, gates_of(pair)] = units
            _, _, candidate, update = cell_gates(units, cell_ref, pair)
            old = state[:, lanes_of(pair)]
            fresh.append(old + update * (candidate - old))
        renewed = jnp.concatenate(fresh, 1)
        states_ref[step] = renewed
        return renewed

    inputs_ref.flush()
    pre_ref.flush()
    ready(state_ref, cell_ref)
    lax.fori_loop(0, horizon, advance, got_ref[:, :width].astype(f32))


def rollout_back_kernel(
    got_ref,
    states_ref,
    unit_ref,
    scale_ref,
    cot_ref,
    ordered_ref,
    state_ref,
    cell_ref,
    back_ref,
    gate_grad_ref,
    cell_grad_ref,
    part_ref,
    gain_grad_ref,
    bias_grad_ref,
):
    horizon, count, width = states_ref.shape
    norm = 1.0 / (PAIRS * GATE)
    first = got_ref[:, :width].astype(f32)
    gain_grad_ref[...] = jnp.zeros_like(gain_grad_ref)
    bias_grad_ref[...] = jnp.zeros_like(bias_grad_ref)

    def retreat(index, carry):
        step = horizon - 1 - index
        rows = pl.ds(pl.multiple_of(step * count, count), count)
        before = states_ref[jnp.maximum(step - 1, 0)]
        before = jnp.where(step == 0, first, before)
        grads = cot_ref[step].astype(f32) + carry
        low = jnp.zeros((count, LANES), f32)
        high = jnp.zeros((count, LANES), f32)
        kept = []
        for pair in range(PAIRS):
            units = unit_ref[rows, gates_of(pair)]
            reset, middle, candidate, update = cell_gates(units, cell_ref, pair)
            grad = grads[:, lanes_of(pair)]
            rest = 1.0 - update
            inner = grad * update * (1.0 - candidate * candidate)
            parts = jnp.concatenate(
                [
                    inner * middle * (reset * (1.0 - reset)),
                    inner * reset,
                    grad * (candidate - before[:, lanes_of(pair)]) * (update * rest),
                ],
                1,
            )
            weighted = parts * units
            gain_grad_ref[:, gates_of(pair)] += jnp.sum(weighted.reshape(count // 8, 8, GATE), 0)
            bias_grad_ref[:, gates_of(pair)] += jnp.sum(parts.reshape(count // 8, 8, GATE), 0)
            parts = parts * cell_ref[:1, gates_of(pair)]
            weighted = parts * units
            for p in range(3):
                low = low + parts[:, lanes_of(p)]
                high = high + weighted[:, lanes_of(p)]
            part_ref[:, gates_of(pair)] = parts
            kept.append(grad * rest)
        low = jnp.sum(low, 1, keepdims=True) * norm
        high = jnp.sum(high, 1, keepdims=True) * norm
        factor = scale_ref[rows, :][:, :1]
        carried = []
        for pair in range(PAIRS):
            units = unit_ref[rows, gates_of(pair)]
            grad = (factor * (part_ref[:, gates_of(pair)] - low - units * high)).astype(bf16)
            gate_grad_ref[rows, gates_of(pair)] = grad
            carried.append(kept[pair] + mm_nt(grad, state_ref[lanes_of(pair), :]))
        return jnp.concatenate(carried, 1)

    ready(states_ref, unit_ref, scale_ref, cot_ref, state_ref, cell_ref)
    carry = lax.fori_loop(0, horizon, retreat, jnp.zeros((count, width), f32))
    back_ref[:, :width] = carry.astype(bf16)
    back_ref[:, width:] = mm_nt(gate_grad_ref[:count, :], ordered_ref[...]).astype(bf16)
    cell_grad_ref[...] = jnp.concatenate(
        [
            jnp.sum(gain_grad_ref[...], 0, keepdims=True),
            jnp.sum(bias_grad_ref[...], 0, keepdims=True),
        ],
        0,
    )


def rollout_grads_kernel(
    gate_grad_ref,
    inputs_ref,
    held_ref,
    pre_ref,
    cat_ref,
    ordered_ref,
    stoch_gain_ref,
    stoch_bias_ref,
    input_grad_ref,
    state_grad_ref,
    table_grad_ref,
    stoch_grad_ref,
):
    for pair in range(PAIRS):
        grads = gate_grad_ref[:, gates_of(pair)]
        input_grad_ref[:, gates_of(pair)] = mm_tn(inputs_ref[...], grads)
        state_grad_ref[pair] = mm_tn(held_ref[:, lanes_of(pair)], grads)
    steps, _, count = cat_ref.shape
    table_grad_ref[...] = jnp.zeros(table_grad_ref.shape, f32)
    gain_sum = jnp.zeros(stoch_gain_ref.shape, f32)
    bias_sum = jnp.zeros(stoch_bias_ref.shape, f32)
    for at in range(0, steps, 2):
        rows = slice(at * count, (at + 2) * count)
        grad = mm_nt(gate_grad_ref[(at + 1) * count : (at + 3) * count, :], ordered_ref[...])
        low, gain_grad, bias_grad = norm_silu_back(
            pre_ref[rows, :], stoch_gain_ref[...], stoch_bias_ref[...], grad
        )
        gain_sum = gain_sum + gain_grad
        bias_sum = bias_sum + bias_grad
        table_grad_ref[...] += mm_tn(
            hot_rows([cat_ref[at], cat_ref[at + 1]]), low.astype(bf16)
        )
    stoch_grad_ref[...] = jnp.concatenate([gain_sum, bias_sum], 1)


def observe_back_kernel(
    core_ref,
    held_grad_ref,
    back_ref,
    order_ref,
    cat_ref,
    taken_ref,
    pre_ref,
    gates_ref,
    states_ref,
    start_ref,
    stoch_gain_ref,
    stoch_bias_ref,
    ordered_ref,
    state_ref,
    cell_ref,
    input_part_ref,
    state_part_ref,
    table_part_ref,
    stoch_part_ref,
    cell_part_ref,
    small_ref,
    camera_grad_ref,
    start_grad_ref,
    keep_ref,
    send_ref,
    grads_ref,
    turned_ref,
    arriving_ref,
    slope_ref,
    factor_ref,
    unit_ref,
    mean_ref,
    cross_ref,
    rest_ref,
    flat_ref,
    lean_ref,
    scale_ref,
    grad_ref,
    low_ref,
    high_ref,
    previous_ref,
):
    frames, width = held_grad_ref.shape
    length = frames // 2
    norm = 1.0 / (PAIRS * GATE)
    chosen = pick_columns(order_ref[:, : back_ref.shape[0]], frames)
    held_grad = held_grad_ref[...] + mm(chosen, back_ref[:, :width])
    turned_ref[...] = state_ref[...].astype(f32).T.astype(bf16)
    start = jnp.concatenate(
        [start_ref[:, lanes_of(pair)].astype(f32) for pair in range(PAIRS)], 0
    )
    for pair in range(PAIRS):
        arriving_ref[pair * frames : (pair + 1) * frames, :] = held_grad[:, lanes_of(pair)]
    long = PAIRS * frames
    for s in range(2):
        blocks = [
            slice((2 * pair + s) * length, (2 * pair + s + 1) * length) for pair in range(PAIRS)
        ]
        total = jnp.zeros((length, LANES), f32)
        for rows in blocks:
            for p in range(3):
                total = total + gates_ref[p * long + rows.start : p * long + rows.stop, :]
        mean = jnp.sum(total, 1, keepdims=True) * norm
        square = jnp.zeros((length, LANES), f32)
        for rows in blocks:
            for p in range(3):
                center = gates_ref[p * long + rows.start : p * long + rows.stop, :] - mean
                square = square + center * center
        scale = lax.rsqrt(jnp.sum(square, 1, keepdims=True) * norm + epsilon)
        for pair, rows in enumerate(blocks):
            gain = cell_ref[:1, gates_of(pair)]
            units = jnp.concatenate(
                [gates_ref[p * long + rows.start : p * long + rows.stop, :] for p in range(3)], 1
            )
            units = (units - mean) * scale
            reset, middle, candidate, update = cell_gates(units, cell_ref, pair)
            row = 2 * pair + s
            previous = jnp.where(
                iota((length, LANES), 0) == 0,
                start[row : row + 1, :],
                pltpu.roll(states_ref[rows, :], 1, 0),
            )
            previous_ref[rows, :] = previous
            inner = update * (1.0 - candidate * candidate)
            slope = jnp.concatenate(
                [
                    inner * middle * (reset * (1.0 - reset)),
                    inner * reset,
                    (candidate - previous) * (update * (1.0 - update)),
                ],
                1,
            )
            slope_ref[rows, :] = slope
            slope = slope * gain
            weighted = slope * units
            mean_ref[rows, :] = norm * (
                slope[:, :LANES] + slope[:, LANES : 2 * LANES] + slope[:, 2 * LANES :]
            )
            cross_ref[rows, :] = norm * (
                weighted[:, :LANES] + weighted[:, LANES : 2 * LANES] + weighted[:, 2 * LANES :]
            )
            for p in range(3):
                factor_ref[p * long + rows.start : p * long + rows.stop, :] = (
                    scale * slope[:, lanes_of(p)]
                )
            unit_ref[rows, :] = scale * units
            rest_ref[rows, :] = 1.0 - update
            scale_ref[rows, :] = jnp.broadcast_to(scale, (length, LANES))
            weight = state_ref[lanes_of(pair), :]
            flat_ref[rows, :] = scale * mm_nt(jnp.ones((8, GATE), bf16), weight)[:1, :]
            lean_ref[rows, :] = mm_nt((scale * units).astype(bf16), weight)
    row_pair = iota((8, LANES), 0) // 2

    def retreat(index, carry):
        step = length - 1 - index
        rows = pl.ds(step, 8, stride=length)
        grad = arriving_ref[rows, :] + carry
        wide = jnp.concatenate(
            [grad * factor_ref[pl.ds(p * long + step, 8, stride=length), :] for p in range(3)], 1
        )
        turned = mm(wide.astype(bf16), turned_ref[...])
        low = jnp.sum(group_sum(grad * mean_ref[rows, :]), 1, keepdims=True)
        high = jnp.sum(group_sum(grad * cross_ref[rows, :]), 1, keepdims=True)
        grad_ref[rows, :] = grad
        low_ref[rows, :] = jnp.broadcast_to(low, (8, LANES))
        high_ref[rows, :] = jnp.broadcast_to(high, (8, LANES))
        kept = grad * rest_ref[rows, :] - low * flat_ref[rows, :] - high * lean_ref[rows, :]
        for pair in range(PAIRS):
            kept = kept + jnp.where(row_pair == pair, turned[:, lanes_of(pair)], 0.0)
        return kept

    carry = lax.fori_loop(0, length, retreat, jnp.zeros((8, LANES), f32), unroll=8)
    for pair in range(PAIRS):
        start_grad_ref[:, lanes_of(pair)] = carry[2 * pair : 2 * pair + 2, :]
    frame = iota((frames, width), 0) % length
    earlier = jnp.where(frame == 0, 0.0, pltpu.roll(taken_ref[...].astype(f32), 1, 0)).astype(bf16)
    input_grad = jnp.zeros((frames, width), f32)
    gains, biases, inputs = [], [], []
    order = column_order()
    shares = grads_ref.shape[0]
    unit_rows = width // shares
    for pair in range(PAIRS):
        rows = slice(pair * frames, (pair + 1) * frames)
        grad = jnp.concatenate([grad_ref[rows, :]] * 3, 1)
        gate_grad = grad * slope_ref[rows, :]
        biases.append(jnp.sum(gate_grad, 0, keepdims=True))
        scale = scale_ref[rows, :][:, :1]
        units = unit_ref[rows, :]
        gains.append(jnp.sum(gate_grad * (units / scale), 0, keepdims=True))
        low = low_ref[rows, :][:, :1]
        high = high_ref[rows, :][:, :1]
        factors = jnp.concatenate(
            [factor_ref[p * long + rows.start : p * long + rows.stop, :] for p in range(3)], 1
        )
        gate_low = (grad * factors - low * scale - high * units).astype(bf16)
        columns = ordered_ref[:, gates_of(pair)]
        input_grad = input_grad + mm_nt(gate_low, columns)
        weight_grad = mm_tn(earlier, gate_low) + input_part_ref[:, gates_of(pair)]
        inputs.append(mm_nt(weight_grad.astype(bf16), order).astype(bf16))
        state_grad = mm_tn(previous_ref[rows, :].astype(bf16), gate_low) + state_part_ref[pair]
        half = LANES // 2
        upper = iota((half, GATE), 1) % LANES < half
        folded = jnp.where(upper, state_grad[:half], state_grad[half:])
        at = 3 * unit_rows + 2 * unit_rows
        grads_ref[pair, at : at + half, :GATE] = folded.astype(bf16)
        grads_ref[pair, at : at + half, GATE:] = jnp.zeros((half, width - GATE), bf16)
    weights = jnp.concatenate(inputs, 1)
    for q in range(shares):
        for c in range(3):
            grads_ref[q, c * unit_rows : (c + 1) * unit_rows, :] = weights[
                q * unit_rows : (q + 1) * unit_rows, c * width : (c + 1) * width
            ]
    taken_grad = jnp.where(
        frame == length - 1, 0.0, pltpu.roll(input_grad, frames - 1, 0)
    ) + mm(chosen, back_ref[:, width:])
    low, gain_grad, bias_grad = norm_silu_back(
        pre_ref[...], stoch_gain_ref[...], stoch_bias_ref[...], taken_grad
    )
    stoch = jnp.concatenate([gain_grad, bias_grad], 1) + stoch_part_ref[...]
    hot = hot_rows([cat_ref[s] for s in range(2)])
    table_grad = mm_tn(hot, low.astype(bf16)) + table_part_ref[...]
    rows = table_grad.shape[0] // shares
    vector_row = 5 * unit_rows + LANES // 2
    classes = GROUPS * CLASSES
    wide = camera_grad_ref.shape[1] // shares
    for q in range(shares):
        grads_ref[q, 3 * unit_rows : 3 * unit_rows + rows, :] = table_grad[
            q * rows : (q + 1) * rows
        ].astype(bf16)
        unit = slice(q * unit_rows, (q + 1) * unit_rows)
        logit = slice(q * classes // shares, (q + 1) * classes // shares)
        units = [stoch[:, unit], stoch[:, width + unit.start : width + unit.stop]]
        units += [
            small_ref[:, k * width + unit.start : k * width + unit.stop] for k in range(4)
        ]
        logits = [
            small_ref[
                :, 4 * width + k * classes + logit.start : 4 * width + k * classes + logit.stop
            ]
            for k in range(2)
        ]
        cells = [
            plain_row(kind[q] + cell_part_ref[k : k + 1, gates_of(q)])
            for k, kind in enumerate((gains, biases))
        ]
        pad = jnp.zeros((1, width - GATE), f32)
        rows_out = [
            jnp.concatenate(units[:4], 1),
            jnp.concatenate(units[4:] + logits[:1], 1),
            jnp.concatenate(logits[1:] + [jnp.zeros((1, width - logits[1].shape[1]), f32)], 1),
        ]
        rows_out += [jnp.concatenate([cell, pad], 1) for cell in cells]
        for c in range(camera_grad_ref.shape[0]):
            for at in range(q * wide, (q + 1) * wide, width):
                rows_out.append(camera_grad_ref[c : c + 1, at : at + width])
        rows_out.append(jnp.zeros((grads_ref.shape[1] - vector_row - len(rows_out), width), f32))
        grads_ref[q, vector_row:, :] = jnp.concatenate(rows_out, 0).astype(bf16)
    block = keep_ref.shape[1]
    for slot, ref in ((0, keep_ref), (1, send_ref)):
        parity = core_ref[0] ^ slot
        for y in range(shares // 2):
            for index in range(4):
                at = index * block
                ref[block_place(parity, y, index)] = grads_ref[
                    2 * y + parity, at : at + block, :
                ]


def place_blocks(where_ref, own_ref, got_ref, full_ref):
    block = own_ref.shape[0] // 2
    parity, bit = where_ref[0], where_ref[1]
    for side in range(2):
        for inner in range(2):
            rows = slice(inner * block, (inner + 1) * block)
            piece = jnp.where(bit == side, own_ref[rows, :], got_ref[rows, :]).astype(f32)
            place = jnp.where(parity == 0, 2 * side + inner, 2 * inner + side)
            full_ref[pl.ds(pl.multiple_of(place * block, block), block), :] = piece


def finish_heads_kernel(
    where_ref,
    own_ref,
    got_ref,
    post_embed_ref,
    post_deter_ref,
    prior_hidden_ref,
    post_out_ref,
    prior_out_ref,
    full_ref,
):
    place_blocks(where_ref, own_ref, got_ref, full_ref)
    block = full_ref.shape[0] // 4
    width = own_ref.shape[1]
    large, small = post_embed_ref.shape[0] // 4, post_deter_ref.shape[0] // 4
    for index in range(4):
        at = index * block
        post_embed_ref[index * large : (index + 1) * large, :] = full_ref[at : at + large, :]
        rows = slice(index * small, (index + 1) * small)
        for member, (ref, column) in enumerate(
            (
                (post_deter_ref, 0),
                (prior_hidden_ref, 0),
                (post_out_ref, 0),
                (post_out_ref, width),
                (prior_out_ref, 0),
                (prior_out_ref, width),
            )
        ):
            first = at + large + member * small
            ref[rows, column : column + width] = full_ref[first : first + small, :]


def finish_kernel(where_ref, own_ref, got_ref, *refs):
    outs, full_ref = refs[:-1], refs[-1]
    width = own_ref.shape[1]
    place_blocks(where_ref, own_ref, got_ref, full_ref)
    input_ref, table_ref, state_ref = outs[:3]
    unit_rows = input_ref.shape[0]
    for c in range(3):
        input_ref[:, c * width : (c + 1) * width] = full_ref[c * unit_rows : (c + 1) * unit_rows, :]
    at = 3 * unit_rows
    table_ref[...] = full_ref[at : at + table_ref.shape[0], :]
    at += table_ref.shape[0]
    half = state_ref.shape[1]
    folded = full_ref[at : at + half, :]
    for e in range(2):
        state_ref[e] = jnp.concatenate(
            [folded[:, (2 * p + e) * half : (2 * p + e + 1) * half] for p in range(3)], 1
        )
    at += half
    units = outs[3:9]
    for k, ref in enumerate(units):
        ref[...] = full_ref[
            at + k // 4 : at + k // 4 + 1, k % 4 * unit_rows : (k % 4 + 1) * unit_rows
        ]
    size = outs[9].shape[1]
    outs[9][...] = full_ref[at + 1 : at + 2, size:]
    outs[10][...] = full_ref[at + 2 : at + 3, :size]
    outs[11][...] = full_ref[at + 3 : at + 4, :GATE]
    outs[12][...] = full_ref[at + 4 : at + 5, :GATE]
    row = at + 5
    camera_ref = outs[13]
    for c in range(camera_ref.shape[0]):
        for column in range(0, camera_ref.shape[1], width):
            camera_ref[c : c + 1, column : column + width] = full_ref[row : row + 1, :]
            row += 1


def struct(shape, dtype):
    return jax.ShapeDtypeStruct(shape, dtype)


class Incoming:
    def __init__(self, ref, copy):
        self.ref, self.copy, self.shape = ref, copy, ref.shape
        copy.start()

    def ready(self):
        if self.copy is not None:
            self.copy.wait()
            self.copy = None

    def __getitem__(self, index):
        self.ready()
        return self.ref[index]


class Outgoing:
    def __init__(self, ref, copy):
        self.ref, self.copy, self.shape, self.started = ref, copy, ref.shape, False

    def __getitem__(self, index):
        return self.ref[index]

    def __setitem__(self, index, value):
        self.ref[index] = value

    def flush(self):
        if not self.started:
            self.copy.start()
            self.started = True


def ready(*refs):
    for ref in refs:
        if isinstance(ref, Incoming):
            ref.ready()


def call(kernel, name, outs, ins, mib, scratch=(), scalars=0, after=(), near_in=(), near_out=()):
    count, total = len(ins), len(ins) + len(after) + len(outs)
    far_in = [k for k in range(scalars, count) if k not in near_in]
    far_out = [k for k in range(len(outs)) if k not in near_out]
    near = pl.BlockSpec(memory_space=pltpu.VMEM)
    far = pl.BlockSpec(memory_space=pltpu.HBM)

    def body(*refs):
        given, made = list(refs[:count]), list(refs[count + len(after) : total])
        places = refs[total : total + len(far_in) + len(far_out)]
        rest = refs[total + len(far_in) + len(far_out) : -1]
        marks = refs[-1]
        for at, k in enumerate(far_in):
            copy = pltpu.make_async_copy(given[k], places[at], marks.at[at])
            given[k] = Incoming(places[at], copy)
        for at, k in enumerate(far_out, len(far_in)):
            copy = pltpu.make_async_copy(places[at], made[k], marks.at[at])
            made[k] = Outgoing(places[at], copy)
        kernel(*given, *made, *rest)
        ready(*given)
        for k in far_out:
            made[k].flush()
        for k in far_out:
            made[k].copy.wait()

    return pl.pallas_call(
        body,
        out_shape=tuple(
            pltpu.HBM(out.shape, out.dtype) if k in far_out else out for k, out in enumerate(outs)
        ),
        in_specs=[pl.BlockSpec(memory_space=pltpu.SMEM)] * scalars
        + [far if k in far_in else near for k in range(scalars, count)]
        + [pl.BlockSpec(memory_space=pl.ANY)] * len(after),
        out_specs=tuple(far if k in far_out else near for k in range(len(outs))),
        scratch_shapes=[pltpu.VMEM(ins[k].shape, ins[k].dtype) for k in far_in]
        + [pltpu.VMEM(outs[k].shape, outs[k].dtype) for k in far_out]
        + list(scratch)
        + [pltpu.SemaphoreType.DMA((len(far_in) + len(far_out),))],
        compiler_params=pltpu.CompilerParams(vmem_limit_bytes=mib * 1024 * 1024),
        name=name,
    )(
        *[
            pltpu.with_memory_space_constraint(member, pltpu.HBM) if k in far_in else member
            for k, member in enumerate(ins)
        ],
        *after,
    )


def linear_bits(bits):
    own = bits[0]
    rep_count = lax.axis_size("rep")
    index = lax.axis_index("seq") * rep_count + lax.axis_index("rep")
    if bits[0] != bits[1]:
        own = jnp.where(index & 1 == 0, bits[0], bits[1])
    return (index >> own) & 1


def swap(values, bits):
    count = lax.axis_size("seq") * lax.axis_size("rep")
    return lax.ppermute(
        values, ("seq", "rep"), [(i, i ^ (1 << bits[i & 1])) for i in range(count)]
    )


def added(left, right):
    return (left.astype(f32) + right.astype(f32)).astype(bf16)


def folded(keep, got, bits):
    own = linear_bits(bits)
    half = keep.shape[0] // 2
    return [
        added(
            lax.dynamic_slice_in_dim(keep, side * half, half, 0),
            lax.dynamic_slice_in_dim(got, side * half, half, 0),
        )
        for side in (1 - own, own)
    ]


def doubled(values, bits):
    got = swap(values, bits)
    own = linear_bits(bits)
    return jnp.where(
        own == 0, jnp.concatenate([values, got], 0), jnp.concatenate([got, values], 0)
    )


def on_device(
    start_deter,
    post_cat,
    embed,
    camera,
    start_order,
    imag_cat,
    imag_cot,
    stoch_table,
    stoch_gain,
    stoch_bias,
    state_weight,
    input_weight,
    cell_gain,
    cell_bias,
    prior_hidden,
    prior_gain,
    prior_bias,
    prior_out,
    prior_shift,
    post_deter,
    post_embed,
    post_gain,
    post_bias,
    post_out,
    post_shift,
    camera_scale,
):
    seq_count, length = post_cat.shape[:2]
    frames = seq_count * length
    count, horizon, width = imag_cot.shape
    features = embed.shape[-1]
    shares = lax.axis_size("rep")
    rep_bits = shares.bit_length() - 1
    seq_bits = lax.axis_size("seq").bit_length() - 1
    half = LANES // 2
    gate_count = 3 * width
    classes = GROUPS * CLASSES
    rows = horizon * count
    long = PAIRS * frames
    unit_rows = width // shares
    core = (lax.axis_index("rep") & 1).astype(jnp.int32).reshape(1)
    row = lambda vector: vector.reshape(1, -1)
    cat = jnp.swapaxes(post_cat, 1, 2)
    later_cat = jnp.transpose(imag_cat, (1, 2, 0))
    stoch_rows = (row(stoch_gain), row(stoch_bias))
    embed_rows = embed.reshape(frames, features)

    low_bit, next_bit = rep_bits, rep_bits + 1
    deeper = [(rep_bits + bit,) * 2 for bit in range(2, seq_bits)]
    outer, inner = (low_bit, next_bit), (next_bit, low_bit)
    stages = [(1, next_bit), (low_bit, 1), inner] + deeper

    held, taken, obs_pre, obs_gates, obs_states, sent, ordered, state, cell = call(
        observe_kernel,
        "observe",
        [
            struct((frames, width), bf16),
            struct((frames, width), bf16),
            struct((frames, width), f32),
            struct((3 * long, LANES), f32),
            struct((long, LANES), f32),
            struct((count, 2 * width), bf16),
            struct((width, gate_count), bf16),
            struct((width, GATE), bf16),
            struct((2, gate_count), f32),
        ],
        (
            cat,
            stoch_table,
            *stoch_rows,
            input_weight,
            state_weight.reshape(width, 3 * half),
            row(cell_gain),
            row(cell_bias),
            start_deter,
            start_order,
        ),
        18,
        scratch=[pltpu.VMEM((3 * long, LANES), f32)],
    )
    got = lax.all_to_all(sent, "seq", split_axis=0, concat_axis=0, tiled=True)

    square = struct((frames, width), bf16)
    embed_rows_count = features // shares
    head_rows = embed_rows_count + 6 * unit_rows
    blocks = struct((2 * shares, head_rows // 4, width), bf16)
    post_low, prior_low, head_small, keep, send = call(
        heads_kernel,
        "heads",
        [square, square, struct((1, 4 * width + 2 * classes), f32), blocks, blocks],
        (
            core,
            camera,
            held,
            embed_rows,
            camera_scale,
            prior_hidden,
            row(prior_gain),
            row(prior_bias),
            prior_out,
            row(prior_shift),
            post_deter,
            post_embed,
            row(post_gain),
            row(post_bias),
            post_out,
            row(post_shift),
        ),
        34,
        scratch=[
            pltpu.VMEM((frames, width), bf16),
            pltpu.VMEM((frames, width), bf16),
            pltpu.VMEM((frames, features), bf16),
        ],
        scalars=2,
    )
    flat = (shares * head_rows // 2, width)
    arrived = swap(send.reshape(flat), (0, 0))
    send, keep = folded(keep.reshape(flat), arrived, stages[0])
    arrived = swap(send, stages[0])

    states, imag_inputs, imag_held, imag_pre, units, scales = call(
        rollout_kernel,
        "rollout",
        [
            struct((horizon, count, width), f32),
            struct((rows, width), bf16),
            struct((rows, width), bf16),
            struct((rows - count, width), f32),
            struct((rows, gate_count), f32),
            struct((rows, LANES), f32),
        ],
        (got, later_cat, stoch_table, *stoch_rows, ordered, state, cell),
        24,
        near_out=(4, 5),
        after=(send,),
    )
    imag_deter = jnp.swapaxes(states, 0, 1)
    keep, scales = lax.optimization_barrier((keep, scales))
    send, keep = folded(keep, arrived, stages[1])
    arrived = swap(send, stages[1])
    back, gate_grads, cell_part = call(
        rollout_back_kernel,
        "rollout_back",
        [
            struct((count, 2 * width), bf16),
            struct((rows, gate_count), bf16),
            struct((2, gate_count), f32),
        ],
        (got, states, units, scales, jnp.swapaxes(imag_cot, 0, 1), ordered, state, cell),
        24,
        scratch=[
            pltpu.VMEM((count, gate_count), f32),
            pltpu.VMEM((8, gate_count), f32),
            pltpu.VMEM((8, gate_count), f32),
        ],
        near_in=(2, 3),
        after=(send,),
    )
    returned = lax.all_to_all(back, "seq", split_axis=0, concat_axis=0, tiled=True)
    keep, cell_part = lax.optimization_barrier((keep, cell_part))
    send, keep = folded(keep, arrived, stages[2])
    arrived = swap(send, stages[2])

    input_part, state_part, table_part, stoch_part = call(
        rollout_grads_kernel,
        "rollout_grads",
        [
            struct((width, gate_count), f32),
            struct((PAIRS, LANES, GATE), f32),
            struct(stoch_table.shape, f32),
            struct((1, 2 * width), f32),
        ],
        (gate_grads, imag_inputs, imag_held, imag_pre, later_cat, ordered, *stoch_rows),
        22,
        after=(send,),
    )
    keep, stoch_part = lax.optimization_barrier((keep, stoch_part))
    for bits in deeper:
        send, keep = folded(keep, arrived, bits)
        arrived = swap(send, bits)
    held_grad, embed_grad, camera_grad = call(
        embed_back_kernel,
        "embed_back",
        [
            struct((frames, width), f32),
            struct((frames, features), f32),
            struct(camera_scale.shape, f32),
        ],
        (
            camera,
            embed_rows,
            camera_scale,
            post_low,
            prior_low,
            post_embed,
            post_deter,
            prior_hidden,
        ),
        18,
        scalars=1,
        after=(send,),
    )
    keep, camera_grad = lax.optimization_barrier((keep, camera_grad))
    piece = added(keep, arrived)
    for bits in reversed(deeper):
        piece = doubled(piece, bits)
    head_piece = doubled(piece, inner)
    head_other = swap(head_piece, outer)

    tail_rows = 768
    blocks = struct((2 * shares, tail_rows // 4, width), bf16)
    start_grad, tail_keep, tail_send = call(
        observe_back_kernel,
        "observe_back",
        [struct((seq_count, width), f32), blocks, blocks],
        (
            core,
            held_grad,
            returned,
            start_order,
            cat,
            taken,
            obs_pre,
            obs_gates,
            obs_states,
            start_deter,
            *stoch_rows,
            ordered,
            state,
            cell,
            input_part,
            state_part,
            table_part,
            stoch_part,
            cell_part,
            head_small,
            camera_grad,
        ),
        30,
        scratch=[
            pltpu.VMEM((shares, tail_rows, width), bf16),
            pltpu.VMEM((GATE, PAIRS * LANES), bf16),
            pltpu.VMEM((long, LANES), f32),
            pltpu.VMEM((long, GATE), f32),
            pltpu.VMEM((3 * long, LANES), f32),
            pltpu.VMEM((long, GATE), f32),
        ]
        + [pltpu.VMEM((long, LANES), f32)] * 10,
        scalars=1,
    )
    full = (2 * tail_rows, width)
    keep = tail_keep.reshape(full)
    arrived = swap(tail_send.reshape(full), (0, 0))
    for bits in stages:
        send, keep = folded(keep, arrived, bits)
        arrived = swap(send, bits)
    piece = added(keep, arrived)
    for bits in reversed([inner] + deeper):
        piece = doubled(piece, bits)
    other = swap(piece, outer)
    where = jnp.concatenate([core, linear_bits(outer).astype(jnp.int32).reshape(1)])
    unit = struct((1, unit_rows), f32)
    logit = struct((1, classes // shares), f32)
    gate = struct((1, GATE), f32)
    finished = call(
        finish_kernel,
        "finish",
        [
            struct((unit_rows, gate_count), f32),
            struct((stoch_table.shape[0] // shares, width), f32),
            struct((2, half, 3 * half), f32),
            *[unit] * 6,
            logit,
            logit,
            gate,
            gate,
            struct((camera_scale.shape[0], features // shares), f32),
        ],
        (where, piece, other),
        12,
        scratch=[pltpu.VMEM((tail_rows, width), f32)],
        scalars=1,
    )
    small_rows = struct((unit_rows, width), f32)
    wide_rows = struct((unit_rows, classes), f32)
    post_embed_grad, post_deter_grad, prior_hidden_grad, post_out_grad, prior_out_grad = call(
        finish_heads_kernel,
        "finish_heads",
        [struct((embed_rows_count, width), f32), small_rows, small_rows, wide_rows, wide_rows],
        (where, head_piece, head_other),
        16,
        scratch=[pltpu.VMEM((head_rows, width), f32)],
        scalars=1,
    )
    input_weight_grad, stoch_table_grad, state_weight_grad = finished[:3]
    (
        stoch_gain_grad,
        stoch_bias_grad,
        post_gain_grad,
        post_bias_grad,
        prior_gain_grad,
        prior_bias_grad,
        post_shift_grad,
        prior_shift_grad,
        cell_gain_grad,
        cell_bias_grad,
    ) = [member.reshape(-1) for member in finished[3:13]]
    return (
        imag_deter,
        embed_grad.reshape(embed.shape),
        start_grad,
        stoch_table_grad,
        stoch_gain_grad,
        stoch_bias_grad,
        state_weight_grad,
        input_weight_grad,
        cell_gain_grad,
        cell_bias_grad,
        prior_hidden_grad,
        prior_gain_grad,
        prior_bias_grad,
        prior_out_grad,
        prior_shift_grad,
        post_deter_grad,
        post_embed_grad,
        post_gain_grad,
        post_bias_grad,
        post_out_grad,
        post_shift_grad,
        finished[13],
    )


def solution(mesh):
    both = ("seq", "rep")
    in_specs = (
        P(both, None),
        P(both, None, None),
        P(both, None, None),
        P(both),
        P(both, None),
        P(both, None, None),
        P(both, None, None),
    ) + (P(),) * 19
    rows, flat = P("rep", None), P("rep")
    out_specs = (
        P(both, None, None),
        P(both, None, None),
        P(both, None),
        rows,
        flat,
        flat,
        P("rep", None, None),
        rows,
        flat,
        flat,
        rows,
        flat,
        flat,
        rows,
        flat,
        rows,
        rows,
        flat,
        flat,
        rows,
        flat,
        P(None, "rep"),
    )
    return jax.shard_map(
        on_device, mesh=mesh, in_specs=in_specs, out_specs=out_specs, check_vma=False
    )
```

time: 1710 us -> 236 us (0.14)
  local copies, waits for them, and re-layouts: 658 us -> 10.8 us
  other arithmetic: 445 us -> 14.2 us
  waiting for transfers between devices: 439 us -> 51.1 us
  Pallas kernels: 0 us -> 109 us
  matrix products: 107 us -> 0 us
  starting transfers between devices: 24 us -> 49 us
  between operations: 21 us -> 0.92 us
    psum x2 -> x0, waiting for transfers between devices: 435 us -> none  [on_device(): lax.psum((gradients[0], gradients[1], gradients[2], gradients[3], gradien...]
    reshape x643 -> x2, local copies, waits for them, and re-layouts: 190 us -> 2.59 us  [on_device(): row = lambda vector: vector.reshape(1, -1)]
    reduce_sum x404 -> x0, other arithmetic: 168 us -> none  [the longest x159 84.2 us: layer_norm(): return center * lax.rsqrt(spread + epsilon) * factor + offset]
    pallas_call x0 -> x9, Pallas kernels: none -> 109 us  [call(): pl.pallas_call(body, out_shape=tuple((pltpu.HBM(out.shape, out.dtype) if...]
    dot_general x185 -> x0, matrix products: 107 us -> none  [the longest x79 29.8 us: state_back(): jnp.einsum('rbn,bkn->rbk', blocked, state_weight, preferred_element_type=...]
    add x187 -> x0, other arithmetic: 105 us -> none  [the longest x88 52.4 us: layer_norm(): return center * lax.rsqrt(spread + epsilon) * factor + offset]
    squeeze x300 -> x0, local copies, waits for them, and re-layouts: 98.5 us -> none  [the longest x92 67.5 us: run_forward(): lax.scan(advance, (start_state, start_held), gate_inputs, unroll=8)[1]]
    add_any x93 -> x0, local copies, waits for them, and re-layouts: 69.1 us -> none  [gru_update(): reset_gate = jax.nn.sigmoid(normed[:, :, 0])]
where the time goes in v1:
time: 236 us; the launch traced here: 235 us
  Pallas kernels  109 us (46%)
  waiting for transfers between devices  51.1 us (22%)
  starting transfers between devices  49 us (21%)
  other arithmetic  14.2 us (6%)
  local copies, waits for them, and re-layouts  10.8 us (5%)
    pallas_call x9, Pallas kernels, call(): pl.pallas_call(body, out_shape=tuple((pltpu.HBM(out.shape, out.dtype) if...  109 us
    ppermute x16, waiting for transfers between devices, swap(): lax.ppermute(values, ('seq', 'rep'), [(i, i ^ 1 << bits[i & 1]) for i in...  42.9 us
    ppermute x16, starting transfers between devices, swap(): lax.ppermute(values, ('seq', 'rep'), [(i, i ^ 1 << bits[i & 1]) for i in...  39.8 us
    convert_element_type x10, other arithmetic, added(): return (left.astype(f32) + right.astype(f32)).astype(bf16)  10.9 us
    all_to_all x1, waiting for transfers between devices, on_device(): got = lax.all_to_all(sent, 'seq', split_axis=0, concat_axis=0, tiled=True)  8.29 us
    unnamed x20, local copies, waits for them, and re-layouts  8.2 us
    all_to_all x1, starting transfers between devices, on_device(): got = lax.all_to_all(sent, 'seq', split_axis=0, concat_axis=0, tiled=True)  5.81 us
  transfers between devices with their start and end apart: 18, of which 12 were waited for; matrix products, arithmetic and copies ran while one was open for 1% of the time, Pallas kernels for 23%

profile of v1, /device:TPU:0, one launch (start us, length us, event | category | flops | bytes accessed | tf_op | source)
XLA Modules:
  0.0 235.4 jit_solution(17683961409972526295)
XLA Ops:
  0.7 1.3 reshape.138.refs_6_
  2.0 1.3 reshape.139.refs_7_
  3.3 21.7 %observe.1 = (bf16[128,512]{1,0:T(8,128)(2,1)}, bf16[128,512]{1,0:T(8,128)(2,1)}, f32[128,512]{1,0:T(8,128)}, f32[1536,128]{1,0:T(8,128)}, f32[512,128]{1,0:T(8,...) custom-call(s32[2,32,64]{2,1,0:T(8,128)} %bitcast.45, ...), custom_call_target="tpu_custom_call" | custom-call | tf_op jit(solution)/shard_map/observe/pallas_call | solution.py:959
  25.0 12.4 %heads.1 = (bf16[128,512]{1,0:T(8,128)(2,1)}, bf16[128,512]{1,0:T(8,128)(2,1)}, f32[1,4096]{1,0:T(1,128)}, bf16[8,448,512]{2,1,0:T(8,128)(2,1)}, bf16[8,448,512]{2,1,0:T(8,128)(2,1)}) custom-call(s32[1]{0:T(128)} %bitcast.7.refs_0_, s32[2]{0:T(128)S(1)} %copy-done.2, bf16[128,512]{1,0:T(8,128)(2,1)} %get-tuple-element.86.refs_2_, ...), custom_call_target="tpu_custom_call" | custom-call | tf_op jit(solution)/shard_map/heads/pallas_call | solution.py:959
  37.9 6.4 %collective-permute-done = bf16[3584,512]{1,0:T(8,128)(2,1)} collective-permute-done((bf16[3584,512]{1,0:T(8,128)(2,1)}, bf16[3584,512]{1,0:T(8,128)(2,1)}, u32[]{:S(2)}, u32[]{:S(2)}) %collective-permute-start) | collective-permute-done | bytes 3670048 | tf_op jit(solution)/shard_map/ppermute | solution.py:994
  44.2 5.4 %add_convert_fusion = (bf16[1792,512]{1,0:T(8,128)(2,1)}, bf16[1792,512]{1,0:T(8,128)(2,1)S(1)}) fusion(bf16[3584,512]{1,0:T(8,128)(2,1)} %collective-permute-done, s32[]{:T(128)S(6)} %select_n.116, bf16[3584,512]{1,0:T(8,128)(2,1)} %bitcast.35, s32[]{:T(128)S(6)} %select_n.115), kind=kLoop, calls=%fused_computation | loop fusion | flops 7340032 | bytes 11010056 | tf_op jit(solution)/shard_map/convert_element_type | solution.py:1000
  49.7 2.9 %collective-permute-start.1 = (bf16[1792,512]{1,0:T(8,128)(2,1)S(1)}, bf16[1792,512]{1,0:T(8,128)(2,1)}, u32[]{:S(2)}, u32[]{:S(2)}) collective-permute-start(bf16[1792,512]{1,0:T(8,128)(2,1)S(1)} %get-tuple-element.143.refs_8_), channel_id=1, source_target_pairs={{0,2},{1,9},{2,0},{3,11},{4,6},{5,13},{6,4},{7,15},{8,10},{9,1},{1... | collective-permute-start | bytes 5505032 | tf_op jit(solution)/shard_map/ppermute | solution.py:994
  52.6 5.8 %all-to-all-start = ((bf16[8,8,1024]{2,1,0:T(8,128)(2,1)}), bf16[8,8,1024]{2,1,0:T(8,128)(2,1)S(1)}, u32[]{:S(2)}, u32[]{:S(2)}) async-start(bf16[8,8,1024]{2,1,0:T(8,128)(2,1)} %bitcast.4), calls=%async_computation | async-start | bytes 262144 | tf_op jit(solution)/shard_map/all_to_all | solution.py:1104
  58.4 8.3 %all-to-all-done = bf16[8,8,1024]{2,1,0:T(8,128)(2,1)S(1)} async-done(((bf16[8,8,1024]{2,1,0:T(8,128)(2,1)}), bf16[8,8,1024]{2,1,0:T(8,128)(2,1)S(1)}, u32[]{:S(2)}, u32[]{:S(2)}) %all-to-all-start) | async-done | bytes 131104 | tf_op jit(solution)/shard_map/all_to_all | solution.py:1104
  66.7 0.7 copy-done.6
  67.3 13.8 %rollout.1 = (f32[15,64,512]{2,1,0:T(8,128)}, bf16[960,512]{1,0:T(8,128)(2,1)}, bf16[960,512]{1,0:T(8,128)(2,1)}, f32[896,512]{1,0:T(8,128)}, f32[960,1536]{1,0:T(8,128)S(1)}, /*index=5*/f32[960,128]{1,0:T(8,128)S(1)}) custom-call(bf16[64,1024]{1,0:T(8,128)(2,1)} %bitcast.38, s32[14,32,64]{2,1,0:T(8,128)} %bitcast.41, bf16[1024,512]{1,0:T(8,128)(2,1)} %refs_2_.2, ...), custom_call_target="tpu_custom_call" | custom-call | tf_op jit(solution)/shard_map/rollout/pallas_call | solution.py:959
  81.1 2.5 %copy-done = f32[960,1536]{1,0:T(8,128)} copy-done((f32[960,1536]{1,0:T(8,128)}, f32[960,1536]{1,0:T(8,128)S(1)}, u32[]{:S(2)}) %copy-start) | copy-done | bytes 5898264
  83.6 2.0 add_convert_fusion.3
  85.7 2.7 %copy-done.1 = f32[960,1536]{1,0:T(8,128)S(1)} copy-done((f32[960,1536]{1,0:T(8,128)S(1)}, f32[960,1536]{1,0:T(8,128)}, u32[]{:S(2)}) %copy-start.1) | copy-done | bytes 5898264
  88.4 13.3 %rollout_back.1 = (bf16[64,1024]{1,0:T(8,128)(2,1)}, bf16[960,1536]{1,0:T(8,128)(2,1)}, f32[2,1536]{1,0:T(2,128)}) custom-call(bf16[64,1024]{1,0:T(8,128)(2,1)} %bitcast.39, f32[15,64,512]{2,1,0:T(8,128)} %get-tuple-element.89.refs_1_, f32[960,1536]{1,0:T(8,128)S(1)} %copy-done.1, f32[960,128]{1,0:T(8,128)S(1)} %get-tuple-element.95.refs_3_, ...), custom_call_target="tpu_custom_call" | custom-call | tf_op jit(solution)/shard_map/rollout_back/pallas_call | solution.py:959
  102.0 1.5 collective-permute-start.3
  103.5 3.4 %all-to-all-start.1 = ((bf16[8,8,1024]{2,1,0:T(8,128)(2,1)}), bf16[8,8,1024]{2,1,0:T(8,128)(2,1)S(1)}, u32[]{:S(2)}, u32[]{:S(2)}) async-start(bf16[8,8,1024]{2,1,0:T(8,128)(2,1)} %bitcast.20), calls=%async_computation.1 | async-start | bytes 262144 | tf_op jit(solution)/shard_map/all_to_all | solution.py:1183
  106.9 14.8 %rollout_grads.1 = (f32[512,1536]{1,0:T(8,128)}, f32[4,128,384]{2,1,0:T(8,128)}, f32[1024,512]{1,0:T(8,128)}, f32[1,1024]{1,0:T(1,128)}) custom-call(bf16[960,1536]{1,0:T(8,128)(2,1)} %get-tuple-element.98.refs_0_, bf16[960,512]{1,0:T(8,128)(2,1)} %get-tuple-element.99.refs_1_, bf16[960,512]{1,0:T(8,128)(2,1)} %get-tuple-element.100.refs_2_, ...), custom_call_target="tpu_custom_call" | custom-call | tf_op jit(solution)/shard_map/rollout_grads/pallas_call | solution.py:959
  121.8 6.9 %embed_back.1 = (f32[128,512]{1,0:T(8,128)}, f32[128,4096]{1,0:T(8,128)}, f32[2,4096]{1,0:T(2,128)}) custom-call(s32[2]{0:T(128)S(1)} %copy-done.2, bf16[128,4096]{1,0:T(8,128)(2,1)} %bitcast.34, f32[2,4096]{1,0:T(2,128)} %refs_2_.3, bf16[128,512]{1,0:T(8,128)(2,1)} %get-tuple-element.90.refs_3_, bf16[128,512]{1,0:T(8,128)(2,1)} %get-tuple-element.91.refs_4_, ...), custom_call_target="tpu_custom_call" | custom-call | tf_op jit(solution)/shard_map/embed_back/pallas_call | solution.py:959
  128.8 0.6 copy-done.8
  129.4 18.9 %observe_back.1 = (f32[2,512]{1,0:T(2,128)}, bf16[8,192,512]{2,1,0:T(8,128)(2,1)}, bf16[8,192,512]{2,1,0:T(8,128)(2,1)}) custom-call(s32[1]{0:T(128)} %bitcast.7.refs_0_, f32[128,512]{1,0:T(8,128)} %get-tuple-element.105.refs_1_, bf16[64,1024]{1,0:T(8,128)(2,1)} %bitcast.43, s32[1,128]{1,0:T(1,128)} %refs_3_.1, s32[2,32,64]{2,1,0:T(8,128)} %bitcast.46, ...), custom_call_target="tpu_custom_call" | custom-call | tf_op jit(solution)/shard_map/observe_back/pallas_call | solution.py:959
  148.4 11.8 %collective-permute-start.4 = (bf16[1536,512]{1,0:T(8,128)(2,1)}, bf16[1536,512]{1,0:T(8,128)(2,1)S(1)}, u32[]{:S(2)}, u32[]{:S(2)}) collective-permute-start(bf16[1536,512]{1,0:T(8,128)(2,1)} %bitcast.63), channel_id=1, source_target_pairs={{0,1},{1,0},{2,3},{3,2},{4,5},{5,4},{6,7},{7,6},{8,9},{9,8},{10,11... | collective-permute-start | bytes 4718600 | tf_op jit(solution)/shard_map/ppermute | solution.py:994
  160.2 3.2 %collective-permute-done.4 = bf16[1536,512]{1,0:T(8,128)(2,1)S(1)} collective-permute-done((bf16[1536,512]{1,0:T(8,128)(2,1)}, bf16[1536,512]{1,0:T(8,128)(2,1)S(1)}, u32[]{:S(2)}, u32[]{:S(2)}) %collective-permute-start.4) | collective-permute-done | bytes 1572896 | tf_op jit(solution)/shard_map/ppermute | solution.py:994
  163.5 2.7 %add_convert_fusion.5 = (bf16[768,512]{1,0:T(8,128)(2,1)S(1)}, bf16[768,512]{1,0:T(8,128)(2,1)}) fusion(bf16[1536,512]{1,0:T(8,128)(2,1)S(1)} %collective-permute-done.4, s32[]{:T(128)S(6)} %select_n.128, bf16[1536,512]{1,0:T(8,128)(2,1)} %bitcast.37, s32[]{:T(128)S(6)} %select_n.130), kind=kLoop, calls=%fused_computation.5 | loop fusion | flops 3145728 | bytes 4718600 | tf_op jit(solution)/shard_map/convert_element_type | solution.py:1000
  166.7 2.6 %collective-permute-start.12 = (bf16[224,512]{1,0:T(8,128)(2,1)S(1)}, bf16[224,512]{1,0:T(8,128)(2,1)S(1)}, u32[]{:S(2)}, u32[]{:S(2)}) collective-permute-start(bf16[224,512]{1,0:T(8,128)(2,1)S(1)} %get-tuple-element.153.refs_8_), channel_id=1, source_target_pairs={{0,16},{1,17},{2,18},{3,19},{4,20},{5,21},{6,22},{7,23},{8,24},{9,... | collective-permute-start | bytes 688136 | tf_op jit(solution)/shard_map/ppermute | solution.py:994
  169.3 9.1 %collective-permute-done.5 = bf16[768,512]{1,0:T(8,128)(2,1)S(1)} collective-permute-done((bf16[768,512]{1,0:T(8,128)(2,1)}, bf16[768,512]{1,0:T(8,128)(2,1)S(1)}, u32[]{:S(2)}, u32[]{:S(2)}) %collective-permute-start.5) | collective-permute-done | bytes 786464 | tf_op jit(solution)/shard_map/ppermute | solution.py:994
  178.6 1.8 collective-permute-start.6
  180.4 2.4 %collective-permute-start.13 = (bf16[224,512]{1,0:T(8,128)(2,1)S(1)}, bf16[224,512]{1,0:T(8,128)(2,1)S(1)}, u32[]{:S(2)}, u32[]{:S(2)}) collective-permute-start(bf16[224,512]{1,0:T(8,128)(2,1)S(1)} %add_convert_fusion.10), channel_id=1, source_target_pairs={{0,16},{1,17},{2,18},{3,19},{4,20},{5,21},{6,22},{7,23},{8,24},{9,... | collective-permute-start | bytes 688136 | tf_op jit(solution)/shard_map/ppermute | solution.py:994
  182.9 3.5 %collective-permute-done.6 = bf16[384,512]{1,0:T(8,128)(2,1)S(1)} collective-permute-done((bf16[384,512]{1,0:T(8,128)(2,1)S(1)}, bf16[384,512]{1,0:T(8,128)(2,1)S(1)}, u32[]{:S(2)}, u32[]{:S(2)}) %collective-permute-start.6) | collective-permute-done | bytes 393248 | tf_op jit(solution)/shard_map/ppermute | solution.py:994
  186.5 1.8 collective-permute-start.7
  188.3 5.5 %collective-permute-done.13 = bf16[224,512]{1,0:T(8,128)(2,1)S(1)} collective-permute-done((bf16[224,512]{1,0:T(8,128)(2,1)S(1)}, bf16[224,512]{1,0:T(8,128)(2,1)S(1)}, u32[]{:S(2)}, u32[]{:S(2)}) %collective-permute-start.13) | collective-permute-done | bytes 229408 | tf_op jit(solution)/shard_map/ppermute | solution.py:994
  194.0 1.4 collective-permute-start.14
  195.4 0.7 collective-permute-done.7
  196.2 2.8 %collective-permute-start.8 = (bf16[96,512]{1,0:T(8,128)(2,1)S(1)}, bf16[96,512]{1,0:T(8,128)(2,1)S(1)}, u32[]{:S(2)}, u32[]{:S(2)}) collective-permute-start(bf16[96,512]{1,0:T(8,128)(2,1)S(1)} %add_convert_fusion.16), channel_id=1, source_target_pairs={{0,16},{1,17},{2,18},{3,19},{4,20},{5,21},{6,22},{7,23},{8,24},{9,... | collective-permute-start | bytes 294920 | tf_op jit(solution)/shard_map/ppermute | solution.py:994
  198.9 5.1 %collective-permute-done.8 = bf16[96,512]{1,0:T(8,128)(2,1)S(1)} collective-permute-done((bf16[96,512]{1,0:T(8,128)(2,1)S(1)}, bf16[96,512]{1,0:T(8,128)(2,1)S(1)}, u32[]{:S(2)}, u32[]{:S(2)}) %collective-permute-start.8) | collective-permute-done | bytes 98336 | tf_op jit(solution)/shard_map/ppermute | solution.py:994
  204.1 3.5 %collective-permute-start.9 = (bf16[96,512]{1,0:T(8,128)(2,1)S(1)}, bf16[96,512]{1,0:T(8,128)(2,1)S(1)}, u32[]{:S(2)}, u32[]{:S(2)}) collective-permute-start(bf16[96,512]{1,0:T(8,128)(2,1)S(1)} %add_convert_fusion.15), channel_id=1, source_target_pairs={{0,16},{1,17},{2,18},{3,19},{4,20},{5,21},{6,22},{7,23},{8,24},{9,... | collective-permute-start | bytes 294920 | tf_op jit(solution)/shard_map/ppermute | solution.py:994
  208.0 1.2 collective-permute-start.15
  209.3 1.6 collective-permute-done.9
  210.9 4.3 %collective-permute-start.10 = (bf16[192,512]{1,0:T(8,128)(2,1)S(1)}, bf16[192,512]{1,0:T(8,128)(2,1)S(1)}, u32[]{:S(2)}, u32[]{:S(2)}) collective-permute-start(bf16[192,512]{1,0:T(8,128)(2,1)S(1)} %maximum_select_fusion.3), channel_id=1, source_target_pairs={{0,8},{1,5},{2,10},{3,7},{4,12},{5,1},{6,14},{7,3},{8,0},{9,13},{1... | collective-permute-start | bytes 589832 | tf_op jit(solution)/shard_map/ppermute | solution.py:994
  215.2 5.8 %collective-permute-done.10 = bf16[192,512]{1,0:T(8,128)(2,1)S(1)} collective-permute-done((bf16[192,512]{1,0:T(8,128)(2,1)S(1)}, bf16[192,512]{1,0:T(8,128)(2,1)S(1)}, u32[]{:S(2)}, u32[]{:S(2)}) %collective-permute-start.10) | collective-permute-done | bytes 196640 | tf_op jit(solution)/shard_map/ppermute | solution.py:994
  221.2 0.5 collective-permute-start.11
  221.8 1.4 collective-permute-done.15.refs_2_
  223.1 0.9 copy-done.7
  224.1 4.5 %finish_heads.1 = (f32[1024,512]{1,0:T(8,128)}, f32[128,512]{1,0:T(8,128)}, f32[128,512]{1,0:T(8,128)}, f32[128,1024]{1,0:T(8,128)}, f32[128,1024]{1,0:T(8,128)}) custom-call(s32[2]{0:T(128)S(1)} %pad_add_fusion.refs_0_, bf16[896,512]{1,0:T(8,128)(2,1)} %copy-done.4, bf16[896,512]{1,0:T(8,128)(2,1)} %copy-done.7), custom_call_target="tpu_custom_call" | custom-call | tf_op jit(solution)/shard_map/finish_heads/pallas_call | solution.py:959
  229.0 0.8 copy-done.9
  229.8 3.1 %finish.1 = (f32[128,1536]{1,0:T(8,128)}, f32[256,512]{1,0:T(8,128)}, f32[2,64,192]{2,1,0:T(8,128)}, f32[1,128]{1,0:T(1,128)}, f32[1,128]{1,0:T(1,128)}, /*index...) custom-call(s32[2]{0:T(128)S(1)} %pad_add_fusion.refs_0_, ...), custom_call_target="tpu_custom_call" | custom-call | tf_op jit(solution)/shard_map/finish/pallas_call | solution.py:959
  232.9 1.3 reduce
  234.1 1.3 reduce.1
  (36 shorter events, 3.2 us)
Async XLA Ops:
  0.7 24.3 %copy-start.2 = (s32[2]{0:T(128)S(1)}, s32[2]{0:T(128)}, u32[]{:S(2)}) copy-start(s32[2]{0:T(128)} %refs_0_.1) | copy-start | bytes 28
  37.3 6.9 %collective-permute-start = (bf16[3584,512]{1,0:T(8,128)(2,1)}, bf16[3584,512]{1,0:T(8,128)(2,1)}, u32[]{:S(2)}, u32[]{:S(2)}) collective-permute-start(bf16[3584,512]{1,0:T(8,128)(2,1)} %bitcast.61), channel_id=1, source_target_pairs={{0,1},{1,0},{2,3},{3,2},{4,5},{5,4},{6,7},{7,6},{8,9},{9,8},{10,11... | collective-permute-start | bytes 11010056 | tf_op jit(solution)/shard_map/ppermute | solution.py:994
  49.7 34.0 %collective-permute-start.1 = (bf16[1792,512]{1,0:T(8,128)(2,1)S(1)}, bf16[1792,512]{1,0:T(8,128)(2,1)}, u32[]{:S(2)}, u32[]{:S(2)}) collective-permute-start(bf16[1792,512]{1,0:T(8,128)(2,1)S(1)} %get-tuple-element.143.refs_8_), channel_id=1, source_target_pairs={{0,2},{1,9},{2,0},{3,11},{4,6},{5,13},{6,4},{7,15},{8,10},{9,1},{1... | collective-permute-start | bytes 5505032 | tf_op jit(solution)/shard_map/ppermute | solution.py:994
  52.6 14.1 %all-to-all-start = ((bf16[8,8,1024]{2,1,0:T(8,128)(2,1)}), bf16[8,8,1024]{2,1,0:T(8,128)(2,1)S(1)}, u32[]{:S(2)}, u32[]{:S(2)}) async-start(bf16[8,8,1024]{2,1,0:T(8,128)(2,1)} %bitcast.4), calls=%async_computation | async-start | bytes 262144 | tf_op jit(solution)/shard_map/all_to_all | solution.py:1104
  66.7 0.7 copy-start.6
  67.3 16.3 %copy-start.3 = (bf16[1792,512]{1,0:T(8,128)(2,1)S(1)}, bf16[1792,512]{1,0:T(8,128)(2,1)}, u32[]{:S(2)}) copy-start(bf16[1792,512]{1,0:T(8,128)(2,1)} %get-tuple-element.93) | copy-start | bytes 5505028
  81.1 2.5 %copy-start = (f32[960,1536]{1,0:T(8,128)}, f32[960,1536]{1,0:T(8,128)S(1)}, u32[]{:S(2)}) copy-start(f32[960,1536]{1,0:T(8,128)S(1)} %get-tuple-element.94.refs_2_) | copy-start | bytes 17694724
  85.6 16.1 %collective-permute-start.2 = (bf16[896,512]{1,0:T(8,128)(2,1)S(1)}, bf16[896,512]{1,0:T(8,128)(2,1)S(1)}, u32[]{:S(2)}, u32[]{:S(2)}) collective-permute-start(bf16[896,512]{1,0:T(8,128)(2,1)S(1)} %get-tuple-element.145.refs_8_), channel_id=1, source_target_pairs={{0,4},{1,3},{2,6},{3,1},{4,0},{5,7},{6,2},{7,5},{8,12},{9,11},{10,... | collective-permute-start | bytes 2752520 | tf_op jit(solution)/shard_map/ppermute | solution.py:994
  85.7 2.7 %copy-start.1 = (f32[960,1536]{1,0:T(8,128)S(1)}, f32[960,1536]{1,0:T(8,128)}, u32[]{:S(2)}) copy-start(f32[960,1536]{1,0:T(8,128)} %copy-done) | copy-start | bytes 17694724
  102.0 19.7 %collective-permute-start.3 = (bf16[448,512]{1,0:T(8,128)(2,1)S(1)}, bf16[448,512]{1,0:T(8,128)(2,1)S(1)}, u32[]{:S(2)}, u32[]{:S(2)}) collective-permute-start(bf16[448,512]{1,0:T(8,128)(2,1)S(1)} %get-tuple-element.149.refs_8_), channel_id=1, source_target_pairs={{0,8},{1,5},{2,10},{3,7},{4,12},{5,1},{6,14},{7,3},{8,0},{9,13},{1... | collective-permute-start | bytes 1376264 | tf_op jit(solution)/shard_map/ppermute | solution.py:994
  103.5 25.3 %all-to-all-start.1 = ((bf16[8,8,1024]{2,1,0:T(8,128)(2,1)}), bf16[8,8,1024]{2,1,0:T(8,128)(2,1)S(1)}, u32[]{:S(2)}, u32[]{:S(2)}) async-start(bf16[8,8,1024]{2,1,0:T(8,128)(2,1)} %bitcast.20), calls=%async_computation.1 | async-start | bytes 262144 | tf_op jit(solution)/shard_map/all_to_all | solution.py:1183
  128.8 0.7 copy-start.8
  148.4 15.1 %collective-permute-start.4 = (bf16[1536,512]{1,0:T(8,128)(2,1)}, bf16[1536,512]{1,0:T(8,128)(2,1)S(1)}, u32[]{:S(2)}, u32[]{:S(2)}) collective-permute-start(bf16[1536,512]{1,0:T(8,128)(2,1)} %bitcast.63), channel_id=1, source_target_pairs={{0,1},{1,0},{2,3},{3,2},{4,5},{5,4},{6,7},{7,6},{8,9},{9,8},{10,11... | collective-permute-start | bytes 4718600 | tf_op jit(solution)/shard_map/ppermute | solution.py:994
  166.1 12.2 %collective-permute-start.5 = (bf16[768,512]{1,0:T(8,128)(2,1)}, bf16[768,512]{1,0:T(8,128)(2,1)S(1)}, u32[]{:S(2)}, u32[]{:S(2)}) collective-permute-start(bf16[768,512]{1,0:T(8,128)(2,1)} %get-tuple-element.147), channel_id=1, source_target_pairs={{0,2},{1,9},{2,0},{3,11},{4,6},{5,13},{6,4},{7,15},{8,10},{9,1},{1... | collective-permute-start | bytes 2359304 | tf_op jit(solution)/shard_map/ppermute | solution.py:994
  166.7 13.7 %collective-permute-start.12 = (bf16[224,512]{1,0:T(8,128)(2,1)S(1)}, bf16[224,512]{1,0:T(8,128)(2,1)S(1)}, u32[]{:S(2)}, u32[]{:S(2)}) collective-permute-start(bf16[224,512]{1,0:T(8,128)(2,1)S(1)} %get-tuple-element.153.refs_8_), channel_id=1, source_target_pairs={{0,16},{1,17},{2,18},{3,19},{4,20},{5,21},{6,22},{7,23},{8,24},{9,... | collective-permute-start | bytes 688136 | tf_op jit(solution)/shard_map/ppermute | solution.py:994
  178.6 7.8 %collective-permute-start.6 = (bf16[384,512]{1,0:T(8,128)(2,1)S(1)}, bf16[384,512]{1,0:T(8,128)(2,1)S(1)}, u32[]{:S(2)}, u32[]{:S(2)}) collective-permute-start(bf16[384,512]{1,0:T(8,128)(2,1)S(1)} %get-tuple-element.151), channel_id=1, source_target_pairs={{0,4},{1,3},{2,6},{3,1},{4,0},{5,7},{6,2},{7,5},{8,12},{9,11},{10,... | collective-permute-start | bytes 1179656 | tf_op jit(solution)/shard_map/ppermute | solution.py:994
  180.4 13.4 %collective-permute-start.13 = (bf16[224,512]{1,0:T(8,128)(2,1)S(1)}, bf16[224,512]{1,0:T(8,128)(2,1)S(1)}, u32[]{:S(2)}, u32[]{:S(2)}) collective-permute-start(bf16[224,512]{1,0:T(8,128)(2,1)S(1)} %add_convert_fusion.10), channel_id=1, source_target_pairs={{0,16},{1,17},{2,18},{3,19},{4,20},{5,21},{6,22},{7,23},{8,24},{9,... | collective-permute-start | bytes 688136 | tf_op jit(solution)/shard_map/ppermute | solution.py:994
  186.5 9.6 %collective-permute-start.7 = (bf16[192,512]{1,0:T(8,128)(2,1)S(1)}, bf16[192,512]{1,0:T(8,128)(2,1)S(1)}, u32[]{:S(2)}, u32[]{:S(2)}) collective-permute-start(bf16[192,512]{1,0:T(8,128)(2,1)S(1)} %get-tuple-element.155), channel_id=1, source_target_pairs={{0,8},{1,5},{2,10},{3,7},{4,12},{5,1},{6,14},{7,3},{8,0},{9,13},{1... | collective-permute-start | bytes 589832 | tf_op jit(solution)/shard_map/ppermute | solution.py:994
  194.0 13.6 %collective-permute-start.14 = (bf16[448,512]{1,0:T(8,128)(2,1)S(1)}, bf16[448,512]{1,0:T(8,128)(2,1)S(1)}, u32[]{:S(2)}, u32[]{:S(2)}) collective-permute-start(bf16[448,512]{1,0:T(8,128)(2,1)S(1)} %maximum_select_fusion.1), channel_id=1, source_target_pairs={{0,8},{1,5},{2,10},{3,7},{4,12},{5,1},{6,14},{7,3},{8,0},{9,13},{1... | collective-permute-start | bytes 1376264 | tf_op jit(solution)/shard_map/ppermute | solution.py:994
  196.2 7.9 %collective-permute-start.8 = (bf16[96,512]{1,0:T(8,128)(2,1)S(1)}, bf16[96,512]{1,0:T(8,128)(2,1)S(1)}, u32[]{:S(2)}, u32[]{:S(2)}) collective-permute-start(bf16[96,512]{1,0:T(8,128)(2,1)S(1)} %add_convert_fusion.16), channel_id=1, source_target_pairs={{0,16},{1,17},{2,18},{3,19},{4,20},{5,21},{6,22},{7,23},{8,24},{9,... | collective-permute-start | bytes 294920 | tf_op jit(solution)/shard_map/ppermute | solution.py:994
  204.1 6.8 %collective-permute-start.9 = (bf16[96,512]{1,0:T(8,128)(2,1)S(1)}, bf16[96,512]{1,0:T(8,128)(2,1)S(1)}, u32[]{:S(2)}, u32[]{:S(2)}) collective-permute-start(bf16[96,512]{1,0:T(8,128)(2,1)S(1)} %add_convert_fusion.15), channel_id=1, source_target_pairs={{0,16},{1,17},{2,18},{3,19},{4,20},{5,21},{6,22},{7,23},{8,24},{9,... | collective-permute-start | bytes 294920 | tf_op jit(solution)/shard_map/ppermute | solution.py:994
  208.0 15.1 %copy-start.4 = (bf16[896,512]{1,0:T(8,128)(2,1)}, bf16[896,512]{1,0:T(8,128)(2,1)S(1)}, u32[]{:S(2)}) copy-start(bf16[896,512]{1,0:T(8,128)(2,1)S(1)} %maximum_select_fusion.refs_1_) | copy-start | bytes 2752516
  208.0 15.1 %collective-permute-start.15 = (bf16[896,512]{1,0:T(8,128)(2,1)S(1)}, bf16[896,512]{1,0:T(8,128)(2,1)S(1)}, u32[]{:S(2)}, u32[]{:S(2)}) collective-permute-start(bf16[896,512]{1,0:T(8,128)(2,1)S(1)} %maximum_select_fusion.refs_1_), channel_id=1, source_target_pairs={{0,4},{1,9},{2,6},{3,11},{4,0},{5,13},{6,2},{7,15},{8,12},{9,1},{1... | collective-permute-start | bytes 2752520 | tf_op jit(solution)/shard_map/ppermute | solution.py:994
  210.9 10.1 %collective-permute-start.10 = (bf16[192,512]{1,0:T(8,128)(2,1)S(1)}, bf16[192,512]{1,0:T(8,128)(2,1)S(1)}, u32[]{:S(2)}, u32[]{:S(2)}) collective-permute-start(bf16[192,512]{1,0:T(8,128)(2,1)S(1)} %maximum_select_fusion.3), channel_id=1, source_target_pairs={{0,8},{1,5},{2,10},{3,7},{4,12},{5,1},{6,14},{7,3},{8,0},{9,13},{1... | collective-permute-start | bytes 589832 | tf_op jit(solution)/shard_map/ppermute | solution.py:994
  221.1 7.9 %copy-start.5 = (bf16[384,512]{1,0:T(8,128)(2,1)}, bf16[384,512]{1,0:T(8,128)(2,1)S(1)}, u32[]{:S(2)}) copy-start(bf16[384,512]{1,0:T(8,128)(2,1)S(1)} %maximum_select_fusion.2.refs_1_) | copy-start | bytes 1179652
  221.2 7.8 %collective-permute-start.11 = (bf16[384,512]{1,0:T(8,128)(2,1)S(1)}, bf16[384,512]{1,0:T(8,128)(2,1)S(1)}, u32[]{:S(2)}, u32[]{:S(2)}) collective-permute-start(bf16[384,512]{1,0:T(8,128)(2,1)S(1)} %maximum_select_fusion.2.refs_1_), channel_id=1, source_target_pairs={{0,4},{1,9},{2,6},{3,11},{4,0},{5,13},{6,2},{7,15},{8,12},{9,1},{1... | collective-permute-start | bytes 1179656 | tf_op jit(solution)/shard_map/ppermute | solution.py:994
  223.1 0.9 copy-start.7
  229.0 0.8 copy-start.9

commit v2 on v1

--- a/solution.py
+++ b/solution.py
@@ -51,6 +51,16 @@
     spread = (iota((GROUPS, width), 1) // CLASSES == iota((GROUPS, width), 0)).astype(f32)
     wide = mm(categories, spread.astype(bf16))
     own = (iota((count, width), 1) % CLASSES).astype(f32)
+    return jnp.where(wide == own, 1.0, 0.0).astype(bf16)
+
+
+def hot_columns(columns):
+    categories = jnp.concatenate([part.astype(f32) for part in columns], 1).astype(bf16)
+    count = categories.shape[1]
+    width = GROUPS * CLASSES
+    spread = (iota((width, GROUPS), 0) // CLASSES == iota((width, GROUPS), 1)).astype(f32)
+    wide = mm(spread.astype(bf16), categories)
+    own = (iota((width, count), 0) % CLASSES).astype(f32)
     return jnp.where(wide == own, 1.0, 0.0).astype(bf16)
 
 
@@ -92,14 +102,13 @@
 
 def pair_row(ref, pair):
     half = LANES // 2
-    return jnp.concatenate(
-        [
-            ref[:, pair * GATE + (3 * e + p) * half : pair * GATE + (3 * e + p + 1) * half]
-            for p in range(3)
-            for e in range(2)
-        ],
-        1,
-    )
+    pieces = []
+    for p in range(3):
+        for e in range(2):
+            at = pair * GATE + (3 * e + p) * half
+            line, lane = at // LANES, at % LANES
+            pieces.append(ref[line : line + 1, lane : lane + half])
+    return jnp.concatenate(pieces, 1)
 
 
 def plain_row(row):
@@ -146,9 +155,12 @@
     cell_bias_ref,
     start_ref,
     order_ref,
+    later_cat_ref,
     held_ref,
     taken_ref,
     pre_ref,
+    later_ref,
+    later_pre_ref,
     gates_ref,
     states_ref,
     sent_ref,
@@ -220,7 +232,27 @@
     for ref in (taken_ref, pre_ref, ordered_ref, state_ref, cell_ref):
         ref.flush()
     state = advance(0, start, True)
-    lax.fori_loop(1, length, advance, state, unroll=7)
+    ready(later_cat_ref)
+    steps, _, count = later_cat_ref.shape
+    chunks = steps // 2
+    share = 7
+
+    def several(chunk, state):
+        rows = pl.ds(pl.multiple_of(chunk * 2 * count, 2 * count), 2 * count)
+        later_pre = mm(
+            hot_rows([later_cat_ref[2 * chunk], later_cat_ref[2 * chunk + 1]]), table_ref[...]
+        )
+        later_pre_ref[rows, :] = later_pre
+        later = norm_silu(later_pre, stoch_gain_ref[...], stoch_bias_ref[...])
+        later_ref[rows, :] = later.astype(bf16)
+        for step in range(share):
+            state = advance(1 + chunk * share + step, state)
+        return state
+
+    state = lax.fori_loop(0, chunks, several, state)
+    later_ref.flush()
+    later_pre_ref.flush()
+    lax.fori_loop(1 + chunks * share, length, advance, state, unroll=7)
     gates_ref.flush()
     states_ref.flush()
     for pair in range(PAIRS):
@@ -248,13 +280,13 @@
     core_ref,
     camera_ref,
     held_ref,
-    embed_ref,
-    camera_scale_ref,
     prior_hidden_ref,
     prior_gain_ref,
     prior_bias_ref,
     prior_out_ref,
     prior_shift_ref,
+    embed_ref,
+    camera_scale_ref,
     post_deter_ref,
     post_embed_ref,
     post_gain_ref,
@@ -274,19 +306,19 @@
     features = embed_ref.shape[1]
     length = frames // 2
     held = held_ref[...]
+    split = (GROUPS, CLASSES, frames)
+    prior_pre = mm(held, prior_hidden_ref[...])
+    prior_act = norm_silu(prior_pre, prior_gain_ref[...], prior_bias_ref[...]).astype(bf16)
+    prior_logits = mm(prior_act, prior_out_ref[...]) + prior_shift_ref[...]
+    prior_prob, prior_mix = mixed_probs(prior_logits.T.reshape(split))
     for s in range(2):
         rows = slice(s * length, (s + 1) * length)
         scale = scale_row(camera_ref, camera_scale_ref, s, slice(0, features))
         scaled_ref[rows, :] = (embed_ref[rows, :].astype(f32) * scale).astype(bf16)
     post_pre = mm(held, post_deter_ref[...]) + mm(scaled_ref[...], post_embed_ref[...])
-    prior_pre = mm(held, prior_hidden_ref[...])
     post_act = norm_silu(post_pre, post_gain_ref[...], post_bias_ref[...]).astype(bf16)
-    prior_act = norm_silu(prior_pre, prior_gain_ref[...], prior_bias_ref[...]).astype(bf16)
     post_logits = mm(post_act, post_out_ref[...]) + post_shift_ref[...]
-    prior_logits = mm(prior_act, prior_out_ref[...]) + prior_shift_ref[...]
-    split = (GROUPS, CLASSES, frames)
     post_prob, post_mix = mixed_probs(post_logits.T.reshape(split))
-    prior_prob, prior_mix = mixed_probs(prior_logits.T.reshape(split))
     ratio = jnp.log(post_mix) - jnp.log(prior_mix)
     divergence = jnp.sum(jnp.sum(post_mix * ratio, 0, keepdims=True), 1, keepdims=True)
     slope = sigmoid(divergence - free_bits)
@@ -400,33 +432,29 @@
 
 def rollout_kernel(
     got_ref,
-    cat_ref,
-    table_ref,
-    stoch_gain_ref,
-    stoch_bias_ref,
+    inputs_ref,
     ordered_ref,
     state_ref,
     cell_ref,
+    cot_ref,
     states_ref,
-    inputs_ref,
     held_ref,
-    pre_ref,
+    back_ref,
+    gate_grad_ref,
+    cell_grad_ref,
     unit_ref,
     scale_ref,
+    part_ref,
+    gain_grad_ref,
+    bias_grad_ref,
+    turned_ref,
 ):
     horizon, count, width = states_ref.shape
-    inputs_ref[:count, :] = got_ref[:, width:]
-    for at in range(0, horizon - 1, 2):
-        rows = slice(at * count, (at + 2) * count)
-        pre = mm(hot_rows([cat_ref[at], cat_ref[at + 1]]), table_ref[...])
-        pre_ref[rows, :] = pre
-        inputs_ref[(at + 1) * count : (at + 3) * count, :] = norm_silu(
-            pre, stoch_gain_ref[...], stoch_bias_ref[...]
-        ).astype(bf16)
-    chunk = 3 * count
-    for at in range(0, horizon * count, chunk):
-        rows = slice(at, at + chunk)
-        unit_ref[rows, :] = mm(inputs_ref[rows, :], ordered_ref[...])
+    unit_ref[:count, :] = mm(got_ref[:, width:], ordered_ref[...])
+    chunk = (horizon - 1) * count // 2
+    for at in range(0, (horizon - 1) * count, chunk):
+        rows = slice(count + at, count + at + chunk)
+        unit_ref[rows, :] = mm(inputs_ref[at : at + chunk, :], ordered_ref[...])
     norm = 1.0 / (PAIRS * GATE)
 
     def advance(step, state):
@@ -460,31 +488,13 @@
         states_ref[step] = renewed
         return renewed
 
-    inputs_ref.flush()
-    pre_ref.flush()
     ready(state_ref, cell_ref)
-    lax.fori_loop(0, horizon, advance, got_ref[:, :width].astype(f32))
-
-
-def rollout_back_kernel(
-    got_ref,
-    states_ref,
-    unit_ref,
-    scale_ref,
-    cot_ref,
-    ordered_ref,
-    state_ref,
-    cell_ref,
-    back_ref,
-    gate_grad_ref,
-    cell_grad_ref,
-    part_ref,
-    gain_grad_ref,
-    bias_grad_ref,
-):
-    horizon, count, width = states_ref.shape
-    norm = 1.0 / (PAIRS * GATE)
     first = got_ref[:, :width].astype(f32)
+    lax.fori_loop(0, horizon, advance, first, unroll=5)
+    held_ref.flush()
+    states_ref.flush()
+    turned_ref[...] = state_ref[...].astype(f32).T.astype(bf16)
+    ready(cot_ref)
     gain_grad_ref[...] = jnp.zeros_like(gain_grad_ref)
     bias_grad_ref[...] = jnp.zeros_like(bias_grad_ref)
 
@@ -529,11 +539,10 @@
             units = unit_ref[rows, gates_of(pair)]
             grad = (factor * (part_ref[:, gates_of(pair)] - low - units * high)).astype(bf16)
             gate_grad_ref[rows, gates_of(pair)] = grad
-            carried.append(kept[pair] + mm_nt(grad, state_ref[lanes_of(pair), :]))
+            carried.append(kept[pair] + mm(grad, turned_ref[:, lanes_of(pair)]))
         return jnp.concatenate(carried, 1)
 
-    ready(states_ref, unit_ref, scale_ref, cot_ref, state_ref, cell_ref)
-    carry = lax.fori_loop(0, horizon, retreat, jnp.zeros((count, width), f32))
+    carry = lax.fori_loop(0, horizon, retreat, jnp.zeros((count, width), f32), unroll=5)
     back_ref[:, :width] = carry.astype(bf16)
     back_ref[:, width:] = mm_nt(gate_grad_ref[:count, :], ordered_ref[...]).astype(bf16)
     cell_grad_ref[...] = jnp.concatenate(
@@ -547,6 +556,7 @@
 
 def rollout_grads_kernel(
     gate_grad_ref,
+    got_ref,
     inputs_ref,
     held_ref,
     pre_ref,
@@ -558,26 +568,32 @@
     state_grad_ref,
     table_grad_ref,
     stoch_grad_ref,
+    hot_ref,
+    low_ref,
+    taken_ref,
 ):
+    steps, _, count = cat_ref.shape
+    width = inputs_ref.shape[1]
+    taken_ref[:count, :] = got_ref[:, width:]
+    taken_ref[count:, :] = inputs_ref[...]
+    input_grad_ref[...] = mm_tn(taken_ref[...], gate_grad_ref[...])
+    input_grad_ref.flush()
     for pair in range(PAIRS):
-        grads = gate_grad_ref[:, gates_of(pair)]
-        input_grad_ref[:, gates_of(pair)] = mm_tn(inputs_ref[...], grads)
-        state_grad_ref[pair] = mm_tn(held_ref[:, lanes_of(pair)], grads)
-    steps, _, count = cat_ref.shape
-    table_grad_ref[...] = jnp.zeros(table_grad_ref.shape, f32)
+        state_grad_ref[pair] = mm_tn(held_ref[:, lanes_of(pair)], gate_grad_ref[:, gates_of(pair)])
+    state_grad_ref.flush()
     gain_sum = jnp.zeros(stoch_gain_ref.shape, f32)
     bias_sum = jnp.zeros(stoch_bias_ref.shape, f32)
+    grads = mm_nt(gate_grad_ref[count:, :], ordered_ref[...])
     for at in range(0, steps, 2):
         rows = slice(at * count, (at + 2) * count)
-        grad = mm_nt(gate_grad_ref[(at + 1) * count : (at + 3) * count, :], ordered_ref[...])
         low, gain_grad, bias_grad = norm_silu_back(
-            pre_ref[rows, :], stoch_gain_ref[...], stoch_bias_ref[...], grad
+            pre_ref[rows, :], stoch_gain_ref[...], stoch_bias_ref[...], grads[rows]
         )
         gain_sum = gain_sum + gain_grad
         bias_sum = bias_sum + bias_grad
-        table_grad_ref[...] += mm_tn(
-            hot_rows([cat_ref[at], cat_ref[at + 1]]), low.astype(bf16)
-        )
+        low_ref[rows, :] = low.astype(bf16)
+        hot_ref[:, rows] = hot_columns([cat_ref[at], cat_ref[at + 1]])
+    table_grad_ref[...] = mm(hot_ref[...], low_ref[...])
     stoch_grad_ref[...] = jnp.concatenate([gain_sum, bias_sum], 1)
 
 
@@ -720,7 +736,6 @@
     earlier = jnp.where(frame == 0, 0.0, pltpu.roll(taken_ref[...].astype(f32), 1, 0)).astype(bf16)
     input_grad = jnp.zeros((frames, width), f32)
     gains, biases, inputs = [], [], []
-    order = column_order()
     shares = grads_ref.shape[0]
     unit_rows = width // shares
     for pair in range(PAIRS):
@@ -740,14 +755,13 @@
         columns = ordered_ref[:, gates_of(pair)]
         input_grad = input_grad + mm_nt(gate_low, columns)
         weight_grad = mm_tn(earlier, gate_low) + input_part_ref[:, gates_of(pair)]
-        inputs.append(mm_nt(weight_grad.astype(bf16), order).astype(bf16))
+        inputs.append(weight_grad.astype(bf16))
         state_grad = mm_tn(previous_ref[rows, :].astype(bf16), gate_low) + state_part_ref[pair]
         half = LANES // 2
         upper = iota((half, GATE), 1) % LANES < half
         folded = jnp.where(upper, state_grad[:half], state_grad[half:])
         at = 3 * unit_rows + 2 * unit_rows
         grads_ref[pair, at : at + half, :GATE] = folded.astype(bf16)
-        grads_ref[pair, at : at + half, GATE:] = jnp.zeros((half, width - GATE), bf16)
     weights = jnp.concatenate(inputs, 1)
     for q in range(shares):
         for c in range(3):
@@ -761,10 +775,10 @@
         pre_ref[...], stoch_gain_ref[...], stoch_bias_ref[...], taken_grad
     )
     stoch = jnp.concatenate([gain_grad, bias_grad], 1) + stoch_part_ref[...]
-    hot = hot_rows([cat_ref[s] for s in range(2)])
-    table_grad = mm_tn(hot, low.astype(bf16)) + table_part_ref[...]
+    hot = hot_columns([cat_ref[s] for s in range(2)])
+    table_grad = mm(hot, low.astype(bf16)) + table_part_ref[...]
     rows = table_grad.shape[0] // shares
-    vector_row = 5 * unit_rows + LANES // 2
+    vector_row = 5 * unit_rows
     classes = GROUPS * CLASSES
     wide = camera_grad_ref.shape[1] // shares
     for q in range(shares):
@@ -787,18 +801,15 @@
             plain_row(kind[q] + cell_part_ref[k : k + 1, gates_of(q)])
             for k, kind in enumerate((gains, biases))
         ]
-        pad = jnp.zeros((1, width - GATE), f32)
-        rows_out = [
-            jnp.concatenate(units[:4], 1),
-            jnp.concatenate(units[4:] + logits[:1], 1),
-            jnp.concatenate(logits[1:] + [jnp.zeros((1, width - logits[1].shape[1]), f32)], 1),
+        cameras = [
+            camera_grad_ref[c : c + 1, q * wide : (q + 1) * wide]
+            for c in range(camera_grad_ref.shape[0])
         ]
-        rows_out += [jnp.concatenate([cell, pad], 1) for cell in cells]
-        for c in range(camera_grad_ref.shape[0]):
-            for at in range(q * wide, (q + 1) * wide, width):
-                rows_out.append(camera_grad_ref[c : c + 1, at : at + width])
-        rows_out.append(jnp.zeros((grads_ref.shape[1] - vector_row - len(rows_out), width), f32))
-        grads_ref[q, vector_row:, :] = jnp.concatenate(rows_out, 0).astype(bf16)
+        lines = []
+        for vector in units + logits + cells + cameras:
+            lines += [vector[:, at : at + LANES] for at in range(0, vector.shape[1], LANES)]
+        lines.append(jnp.zeros((LANES // 2 - len(lines), LANES), f32))
+        grads_ref[q, vector_row:, GATE:] = jnp.concatenate(lines, 0).astype(bf16)
     block = keep_ref.shape[1]
     for slot, ref in ((0, keep_ref), (1, send_ref)):
         parity = core_ref[0] ^ slot
@@ -860,8 +871,13 @@
     place_blocks(where_ref, own_ref, got_ref, full_ref)
     input_ref, table_ref, state_ref = outs[:3]
     unit_rows = input_ref.shape[0]
-    for c in range(3):
-        input_ref[:, c * width : (c + 1) * width] = full_ref[c * unit_rows : (c + 1) * unit_rows, :]
+    for pair in range(PAIRS):
+        parts = []
+        for p in range(3):
+            at = pair * GATE + p * LANES
+            line, column = at // width * unit_rows, at % width
+            parts.append(full_ref[line : line + unit_rows, column : column + LANES])
+        input_ref[:, gates_of(pair)] = plain_row(jnp.concatenate(parts, 1))
     at = 3 * unit_rows
     table_ref[...] = full_ref[at : at + table_ref.shape[0], :]
     at += table_ref.shape[0]
@@ -871,23 +887,11 @@
         state_ref[e] = jnp.concatenate(
             [folded[:, (2 * p + e) * half : (2 * p + e + 1) * half] for p in range(3)], 1
         )
-    at += half
-    units = outs[3:9]
-    for k, ref in enumerate(units):
-        ref[...] = full_ref[
-            at + k // 4 : at + k // 4 + 1, k % 4 * unit_rows : (k % 4 + 1) * unit_rows
-        ]
-    size = outs[9].shape[1]
-    outs[9][...] = full_ref[at + 1 : at + 2, size:]
-    outs[10][...] = full_ref[at + 2 : at + 3, :size]
-    outs[11][...] = full_ref[at + 3 : at + 4, :GATE]
-    outs[12][...] = full_ref[at + 4 : at + 5, :GATE]
-    row = at + 5
-    camera_ref = outs[13]
-    for c in range(camera_ref.shape[0]):
-        for column in range(0, camera_ref.shape[1], width):
-            camera_ref[c : c + 1, column : column + width] = full_ref[row : row + 1, :]
-            row += 1
+    for ref in outs[3:14]:
+        for line in range(ref.shape[0]):
+            for column in range(0, ref.shape[1], LANES):
+                ref[line : line + 1, column : column + LANES] = full_ref[at : at + 1, GATE:]
+                at += 1
 
 
 def struct(shape, dtype):
@@ -963,7 +967,7 @@
         ),
         in_specs=[pl.BlockSpec(memory_space=pltpu.SMEM)] * scalars
         + [far if k in far_in else near for k in range(scalars, count)]
-        + [pl.BlockSpec(memory_space=pl.ANY)] * len(after),
+        + [far] * len(after),
         out_specs=tuple(far if k in far_out else near for k in range(len(outs))),
         scratch_shapes=[pltpu.VMEM(ins[k].shape, ins[k].dtype) for k in far_in]
         + [pltpu.VMEM(outs[k].shape, outs[k].dtype) for k in far_out]
@@ -976,7 +980,7 @@
             pltpu.with_memory_space_constraint(member, pltpu.HBM) if k in far_in else member
             for k, member in enumerate(ins)
         ],
-        *after,
+        *[pltpu.with_memory_space_constraint(member, pltpu.HBM) for member in after],
     )
 
 
@@ -996,28 +1000,75 @@
     )
 
 
+class Terms:
+    def __init__(self, member):
+        self.members = [(member, [])]
+
+    def add(self, member):
+        self.members.append((member, []))
+
+    def part(self, *sides):
+        total = 0.0
+        for member, path in self.members:
+            path = path + list(sides)
+            rows = member.shape[0] >> len(path)
+            split = member.reshape((2,) * len(path) + (rows, member.shape[1]))
+            one = (1,) * len(path) + split.shape[-2:]
+            chosen = lax.dynamic_slice(split, path + [0, 0], one)
+            total = total + chosen.reshape(split.shape[-2:]).astype(f32)
+        return total.astype(bf16)
+
+    def fold(self, arrived, bits):
+        self.add(arrived)
+        own = linear_bits(bits).astype(jnp.int32)
+        send = self.part(1 - own)
+        self.members = [(member, path + [own]) for member, path in self.members]
+        return send
+
+
 def added(left, right):
     return (left.astype(f32) + right.astype(f32)).astype(bf16)
 
 
-def folded(keep, got, bits):
-    own = linear_bits(bits)
-    half = keep.shape[0] // 2
-    return [
-        added(
-            lax.dynamic_slice_in_dim(keep, side * half, half, 0),
-            lax.dynamic_slice_in_dim(got, side * half, half, 0),
-        )
-        for side in (1 - own, own)
-    ]
-
-
-def doubled(values, bits):
-    got = swap(values, bits)
+def joined(values, got, bits):
     own = linear_bits(bits)
     return jnp.where(
         own == 0, jnp.concatenate([values, got], 0), jnp.concatenate([got, values], 0)
     )
+
+
+class Chain:
+    def __init__(self, keep, send, stages, merged):
+        self.terms, self.piece = Terms(keep), None
+        self.merged = merged
+        self.folds, self.middle = list(stages), stages[-1]
+        if merged:
+            self.folds.pop()
+        self.joins = list(reversed(stages[2:-1])) + [(stages[1][0], stages[0][1])]
+        self.begin(send, (0, 0))
+
+    def begin(self, send, bits):
+        self.sent, self.last = send, bits
+        self.arrived = swap(send, bits)
+
+    def advance(self, *after):
+        if after:
+            self.arrived = lax.optimization_barrier((self.arrived, *after))[0]
+        if self.folds:
+            bits = self.folds.pop(0)
+            self.begin(self.terms.fold(self.arrived, bits), bits)
+            return
+        if self.piece is None:
+            bits = self.middle
+            self.terms.add(self.arrived)
+            self.piece = self.terms.part()
+        else:
+            bits = self.joins.pop(0)
+            if self.merged and self.last == self.middle:
+                self.piece = added(self.piece, self.arrived)
+            else:
+                self.piece = joined(self.piece, self.arrived, self.last)
+        self.begin(self.piece, bits)
 
 
 def on_device(
@@ -1069,17 +1120,33 @@
     embed_rows = embed.reshape(frames, features)
 
     low_bit, next_bit = rep_bits, rep_bits + 1
-    deeper = [(rep_bits + bit,) * 2 for bit in range(2, seq_bits)]
-    outer, inner = (low_bit, next_bit), (next_bit, low_bit)
-    stages = [(1, next_bit), (low_bit, 1), inner] + deeper
-
-    held, taken, obs_pre, obs_gates, obs_states, sent, ordered, state, cell = call(
+    deeper = [rep_bits + bit for bit in range(2, seq_bits)]
+    outer = (low_bit, next_bit)
+    stages = list(
+        zip([1, low_bit, next_bit] + deeper, [next_bit, 1] + deeper + [low_bit], strict=True)
+    )
+
+    (
+        held,
+        taken,
+        obs_pre,
+        imag_inputs,
+        imag_pre,
+        obs_gates,
+        obs_states,
+        sent,
+        ordered,
+        state,
+        cell,
+    ) = call(
         observe_kernel,
         "observe",
         [
             struct((frames, width), bf16),
             struct((frames, width), bf16),
             struct((frames, width), f32),
+            struct((rows - count, width), bf16),
+            struct((rows - count, width), f32),
             struct((3 * long, LANES), f32),
             struct((long, LANES), f32),
             struct((count, 2 * width), bf16),
@@ -1093,12 +1160,13 @@
             *stoch_rows,
             input_weight,
             state_weight.reshape(width, 3 * half),
-            row(cell_gain),
-            row(cell_bias),
+            cell_gain.reshape(-1, LANES),
+            cell_bias.reshape(-1, LANES),
             start_deter,
             start_order,
+            later_cat,
         ),
-        18,
+        26,
         scratch=[pltpu.VMEM((3 * long, LANES), f32)],
     )
     got = lax.all_to_all(sent, "seq", split_axis=0, concat_axis=0, tiled=True)
@@ -1115,13 +1183,13 @@
             core,
             camera,
             held,
-            embed_rows,
-            camera_scale,
             prior_hidden,
             row(prior_gain),
             row(prior_bias),
             prior_out,
             row(prior_shift),
+            embed_rows,
+            camera_scale,
             post_deter,
             post_embed,
             row(post_gain),
@@ -1138,70 +1206,11 @@
         scalars=2,
     )
     flat = (shares * head_rows // 2, width)
-    arrived = swap(send.reshape(flat), (0, 0))
-    send, keep = folded(keep.reshape(flat), arrived, stages[0])
-    arrived = swap(send, stages[0])
-
-    states, imag_inputs, imag_held, imag_pre, units, scales = call(
-        rollout_kernel,
-        "rollout",
-        [
-            struct((horizon, count, width), f32),
-            struct((rows, width), bf16),
-            struct((rows, width), bf16),
-            struct((rows - count, width), f32),
-            struct((rows, gate_count), f32),
-            struct((rows, LANES), f32),
-        ],
-        (got, later_cat, stoch_table, *stoch_rows, ordered, state, cell),
-        24,
-        near_out=(4, 5),
-        after=(send,),
-    )
-    imag_deter = jnp.swapaxes(states, 0, 1)
-    keep, scales = lax.optimization_barrier((keep, scales))
-    send, keep = folded(keep, arrived, stages[1])
-    arrived = swap(send, stages[1])
-    back, gate_grads, cell_part = call(
-        rollout_back_kernel,
-        "rollout_back",
-        [
-            struct((count, 2 * width), bf16),
-            struct((rows, gate_count), bf16),
-            struct((2, gate_count), f32),
-        ],
-        (got, states, units, scales, jnp.swapaxes(imag_cot, 0, 1), ordered, state, cell),
-        24,
-        scratch=[
-            pltpu.VMEM((count, gate_count), f32),
-            pltpu.VMEM((8, gate_count), f32),
-            pltpu.VMEM((8, gate_count), f32),
-        ],
-        near_in=(2, 3),
-        after=(send,),
-    )
-    returned = lax.all_to_all(back, "seq", split_axis=0, concat_axis=0, tiled=True)
-    keep, cell_part = lax.optimization_barrier((keep, cell_part))
-    send, keep = folded(keep, arrived, stages[2])
-    arrived = swap(send, stages[2])
-
-    input_part, state_part, table_part, stoch_part = call(
-        rollout_grads_kernel,
-        "rollout_grads",
-        [
-            struct((width, gate_count), f32),
-            struct((PAIRS, LANES, GATE), f32),
-            struct(stoch_table.shape, f32),
-            struct((1, 2 * width), f32),
-        ],
-        (gate_grads, imag_inputs, imag_held, imag_pre, later_cat, ordered, *stoch_rows),
-        22,
-        after=(send,),
-    )
-    keep, stoch_part = lax.optimization_barrier((keep, stoch_part))
-    for bits in deeper:
-        send, keep = folded(keep, arrived, bits)
-        arrived = swap(send, bits)
+    send, got = lax.optimization_barrier((send, got))
+    tail_stages = list(
+        zip([1, low_bit, next_bit] + deeper, [next_bit, 1, low_bit] + deeper, strict=True)
+    )
+    head = Chain(keep.reshape(flat), send.reshape(flat), stages, True)
     held_grad, embed_grad, camera_grad = call(
         embed_back_kernel,
         "embed_back",
@@ -1222,16 +1231,63 @@
         ),
         18,
         scalars=1,
-        after=(send,),
-    )
-    keep, camera_grad = lax.optimization_barrier((keep, camera_grad))
-    piece = added(keep, arrived)
-    for bits in reversed(deeper):
-        piece = doubled(piece, bits)
-    head_piece = doubled(piece, inner)
-    head_other = swap(head_piece, outer)
-
-    tail_rows = 768
+        after=(head.sent,),
+    )
+    head.advance(camera_grad)
+
+    states, imag_held, back, gate_grads, cell_part = call(
+        rollout_kernel,
+        "rollout",
+        [
+            struct((horizon, count, width), f32),
+            struct((rows, width), bf16),
+            struct((count, 2 * width), bf16),
+            struct((rows, gate_count), bf16),
+            struct((2, gate_count), f32),
+        ],
+        (
+            got,
+            imag_inputs,
+            ordered,
+            state,
+            cell,
+            jnp.swapaxes(imag_cot, 0, 1),
+        ),
+        36,
+        scratch=[
+            pltpu.VMEM((rows, gate_count), f32),
+            pltpu.VMEM((rows, LANES), f32),
+            pltpu.VMEM((count, gate_count), f32),
+            pltpu.VMEM((8, gate_count), f32),
+            pltpu.VMEM((8, gate_count), f32),
+            pltpu.VMEM((GATE, PAIRS * LANES), bf16),
+        ],
+        after=(head.sent,),
+    )
+    imag_deter = jnp.swapaxes(states, 0, 1)
+    returned = lax.all_to_all(back, "seq", split_axis=0, concat_axis=0, tiled=True)
+    head.advance(cell_part)
+
+    input_part, state_part, table_part, stoch_part = call(
+        rollout_grads_kernel,
+        "rollout_grads",
+        [
+            struct((width, gate_count), f32),
+            struct((PAIRS, LANES, GATE), f32),
+            struct(stoch_table.shape, f32),
+            struct((1, 2 * width), f32),
+        ],
+        (gate_grads, got, imag_inputs, imag_held, imag_pre, later_cat, ordered, *stoch_rows),
+        30,
+        scratch=[
+            pltpu.VMEM((stoch_table.shape[0], rows - count), bf16),
+            pltpu.VMEM((rows - count, width), bf16),
+            pltpu.VMEM((rows, width), bf16),
+        ],
+        after=(head.sent,),
+    )
+    head.advance(stoch_part, returned)
+    tail_rows = 5 * unit_rows + half
     blocks = struct((2 * shares, tail_rows // 4, width), bf16)
     start_grad, tail_keep, tail_send = call(
         observe_back_kernel,
@@ -1261,6 +1317,7 @@
             camera_grad,
         ),
         30,
+        after=(head.sent,),
         scratch=[
             pltpu.VMEM((shares, tail_rows, width), bf16),
             pltpu.VMEM((GATE, PAIRS * LANES), bf16),
@@ -1273,19 +1330,40 @@
         scalars=1,
     )
     full = (2 * tail_rows, width)
-    keep = tail_keep.reshape(full)
-    arrived = swap(tail_send.reshape(full), (0, 0))
-    for bits in stages:
-        send, keep = folded(keep, arrived, bits)
-        arrived = swap(send, bits)
-    piece = added(keep, arrived)
-    for bits in reversed([inner] + deeper):
-        piece = doubled(piece, bits)
-    other = swap(piece, outer)
+    tail_send, head.arrived = lax.optimization_barrier((tail_send, head.arrived))
+    for _ in deeper:
+        head.advance()
+    tail = Chain(tail_keep.reshape(full), tail_send.reshape(full), tail_stages, True)
+    for step in range(2 * len(stages) - 2):
+        if step in (0, 2):
+            head.advance(tail.sent)
+        tail.advance()
+    while head.joins:
+        head.advance(tail.sent)
+    piece, other = tail.piece, tail.arrived
+    head_piece, head_other = head.piece, head.arrived
     where = jnp.concatenate([core, linear_bits(outer).astype(jnp.int32).reshape(1)])
     unit = struct((1, unit_rows), f32)
     logit = struct((1, classes // shares), f32)
-    gate = struct((1, GATE), f32)
+    gate = struct((3, LANES), f32)
+    small_rows = struct((unit_rows, width), f32)
+    wide_rows = struct((unit_rows, classes), f32)
+    post_embed_grad, post_deter_grad, prior_hidden_grad, post_out_grad, prior_out_grad = call(
+        finish_heads_kernel,
+        "finish_heads",
+        [
+            struct((embed_rows_count, width), f32),
+            small_rows,
+            small_rows,
+            wide_rows,
+            wide_rows,
+        ],
+        (where, head_piece, head_other),
+        18,
+        scratch=[pltpu.VMEM((head_rows, width), f32)],
+        scalars=1,
+        near_in=(1, 2),
+    )
     finished = call(
         finish_kernel,
         "finish",
@@ -1304,17 +1382,8 @@
         12,
         scratch=[pltpu.VMEM((tail_rows, width), f32)],
         scalars=1,
-    )
-    small_rows = struct((unit_rows, width), f32)
-    wide_rows = struct((unit_rows, classes), f32)
-    post_embed_grad, post_deter_grad, prior_hidden_grad, post_out_grad, prior_out_grad = call(
-        finish_heads_kernel,
-        "finish_heads",
-        [struct((embed_rows_count, width), f32), small_rows, small_rows, wide_rows, wide_rows],
-        (where, head_piece, head_other),
-        16,
-        scratch=[pltpu.VMEM((head_rows, width), f32)],
-        scalars=1,
+        near_in=(1, 2),
+        after=(post_embed_grad,),
     )
     input_weight_grad, stoch_table_grad, state_weight_grad = finished[:3]
     (

time: 236 us -> 184 us (0.78)
  starting transfers between devices: 49 us -> 31.1 us
  Pallas kernels: 109 us -> 95.8 us
  waiting for transfers between devices: 51.1 us -> 41 us
  local copies, waits for them, and re-layouts: 10.8 us -> 1.14 us
    ppermute x16 -> x14, starting transfers between devices: 39.8 us -> 19.3 us  [swap(): lax.ppermute(values, ('seq', 'rep'), [(i, i ^ 1 << bits[i & 1]) for i in...]
    pallas_call x9 -> x8, Pallas kernels: 109 us -> 95.8 us  [call(): pl.pallas_call(body, out_shape=tuple((pltpu.HBM(out.shape, out.dtype) if...]
    convert_element_type x0 -> x8, other arithmetic: none -> 12.9 us  [part(): return total.astype(bf16)]
    convert_element_type x10 -> x2, other arithmetic: 10.9 us -> 0.16 us  [added(): return (left.astype(f32) + right.astype(f32)).astype(bf16)]
    all_to_all x1, waiting for transfers between devices: 8.29 us -> 0.01 us  [on_device(): got = lax.all_to_all(sent, 'seq', split_axis=0, concat_axis=0, tiled=True)]
    unnamed x20 -> x18, local copies, waits for them, and re-layouts: 8.2 us -> 1.14 us
    reshape x2 -> x0, local copies, waits for them, and re-layouts: 2.59 us -> none  [on_device(): row = lambda vector: vector.reshape(1, -1)]
    pallas_call x2 -> x0, other arithmetic: 2.55 us -> none  [call(): pl.pallas_call(body, out_shape=tuple((pltpu.HBM(out.shape, out.dtype) if...]
  transfers between devices with their start and end apart: 18 -> 16, of which waited for: 12 -> 9; matrix products, arithmetic and copies ran while one was open for 1% -> 3% of each run, Pallas kernels for 23% -> 38%
where the time goes in v2:
time: 184 us
  Pallas kernels  95.8 us (52%)
  waiting for transfers between devices  41 us (22%)
  starting transfers between devices  31.1 us (17%)
  other arithmetic  13.7 us (7%)
    pallas_call x8, Pallas kernels, call(): pl.pallas_call(body, out_shape=tuple((pltpu.HBM(out.shape, out.dtype) if...  95.8 us
    ppermute x14, waiting for transfers between devices, swap(): lax.ppermute(values, ('seq', 'rep'), [(i, i ^ 1 << bits[i & 1]) for i in...  41 us
    ppermute x14, starting transfers between devices, swap(): lax.ppermute(values, ('seq', 'rep'), [(i, i ^ 1 << bits[i & 1]) for i in...  19.3 us
    convert_element_type x8, other arithmetic, part(): return total.astype(bf16)  12.9 us
    all_to_all x1, starting transfers between devices, on_device(): got = lax.all_to_all(sent, 'seq', split_axis=0, concat_axis=0, tiled=True)  7.27 us
    all_to_all x1, starting transfers between devices, on_device(): lax.all_to_all(back, 'seq', split_axis=0, concat_axis=0, tiled=True)  4.53 us
  transfers between devices with their start and end apart: 16, of which 9 were waited for; matrix products, arithmetic and copies ran while one was open for 3% of the time, Pallas kernels for 38%

profile of v2, /device:TPU:0, one launch (start us, length us, event | category | flops | bytes accessed | tf_op | source)
XLA Modules:
  0.0 183.8 jit_solution(5376685573098483349)
XLA Ops:
  0.7 24.4 %observe.1 = (bf16[128,512]{1,0:T(8,128)(2,1)}, bf16[128,512]{1,0:T(8,128)(2,1)}, f32[128,512]{1,0:T(8,128)}, bf16[896,512]{1,0:T(8,128)(2,1)}, f32[896,512]{1,0...) custom-call(s32[2,32,64]{2,1,0:T(8,128)} %bitcast.126, ...), custom_call_target="tpu_custom_call" | custom-call | tf_op jit(solution)/shard_map/observe/pallas_call | solution.py:963
  25.0 7.3 %all-to-all-start = ((bf16[8,8,1024]{2,1,0:T(8,128)(2,1)}), bf16[8,8,1024]{2,1,0:T(8,128)(2,1)S(1)}, u32[]{:S(2)}, u32[]{:S(2)}) async-start(bf16[8,8,1024]{2,1,0:T(8,128)(2,1)} %bitcast.128), calls=%async_computation | async-start | bytes 262144 | tf_op jit(solution)/shard_map/all_to_all | solution.py:1172
  32.3 11.4 %heads.1 = (bf16[128,512]{1,0:T(8,128)(2,1)}, bf16[128,512]{1,0:T(8,128)(2,1)}, f32[1,4096]{1,0:T(1,128)}, bf16[8,448,512]{2,1,0:T(8,128)(2,1)}, bf16[8,448,512]{2,1,0:T(8,128)(2,1)}) custom-call(s32[1]{0:T(128)} %bitcast.refs_0_, s32[2]{0:T(128)S(1)} %copy-done, bf16[128,512]{1,0:T(8,128)(2,1)} %get-tuple-element.81.refs_2_, bf16[512,512]{1,0:T(8,128)(2,1)} %refs_7_.1, ...), custom_call_target="tpu_custom_call" | custom-call | tf_op jit(solution)/shard_map/heads/pallas_call | solution.py:963
  43.8 0.1 collective-permute-start
  43.9 7.2 %embed_back.1 = (f32[128,512]{1,0:T(8,128)}, f32[128,4096]{1,0:T(8,128)}, f32[2,4096]{1,0:T(2,128)}) custom-call(s32[2]{0:T(128)S(1)} %copy-done, bf16[128,4096]{1,0:T(8,128)(2,1)} %bitcast.100, f32[2,4096]{1,0:T(2,128)} %refs_2_.1, bf16[128,512]{1,0:T(8,128)(2,1)} %get-tuple-element.91.refs_3_, bf16[128,512]{1,0:T(8,128)(2,1)} %get-tuple-element.92.refs_4_, ...), custom_call_target="tpu_custom_call" | custom-call | tf_op jit(solution)/shard_map/embed_back/pallas_call | solution.py:963
  51.1 2.1 %fusion.refs_6_ = bf16[1792,512]{1,0:T(8,128)(2,1)S(1)} fusion(bf16[2,1792,512]{2,1,0:T(8,128)(2,1)} %bitcast.20, s32[]{:T(128)S(6)} %select_n.51, bf16[2,1792,512]{2,1,0:T(8,128)(2,1)S(1)} %bitcast.106), kind=kLoop, calls=%fused_computation.1 | loop fusion | flops 3670016 | bytes 5505028 | tf_op jit(solution)/shard_map/convert_element_type | solution.py:1019
  53.1 0.0 copy-start.1
  53.2 1.6 collective-permute-start.1
  54.7 19.1 %rollout.1 = (f32[15,64,512]{2,1,0:T(8,128)}, bf16[960,512]{1,0:T(8,128)(2,1)}, bf16[64,1024]{1,0:T(8,128)(2,1)}, bf16[960,1536]{1,0:T(8,128)(2,1)}, f32[2,1536]{1,0:T(2,128)}) custom-call(bf16[64,1024]{1,0:T(8,128)(2,1)} %bitcast.115, bf16[896,512]{1,0:T(8,128)(2,1)} %get-tuple-element.85.refs_1_.refs_2_, ...), custom_call_target="tpu_custom_call" | custom-call | tf_op jit(solution)/shard_map/rollout/pallas_call | solution.py:963
  73.8 2.7 %collective-permute-done.1 = bf16[1792,512]{1,0:T(8,128)(2,1)} collective-permute-done((bf16[1792,512]{1,0:T(8,128)(2,1)S(1)}, bf16[1792,512]{1,0:T(8,128)(2,1)}, u32[]{:S(2)}, u32[]{:S(2)}) %collective-permute-start.1) | collective-permute-done | bytes 1835040 | tf_op jit(solution)/shard_map/ppermute | solution.py:998
  76.6 2.1 %fusion.1.refs_9_ = bf16[896,512]{1,0:T(8,128)(2,1)S(1)} fusion(bf16[2,896,512]{2,1,0:T(8,128)(2,1)} %bitcast.29, s32[]{:T(128)S(6)} %select_n.54, bf16[2,2,896,512]{3,2,1,0:T(8,128)(2,1)} %bitcast.27, s32[]{:T(128)S(6)} %select_n.52, bf16[2,2,896,512]{3,2,1,0:T(8,128)(2,1)} %bitcast.103), kind=kLoop, calls=%fused_computation.3 | loop fusion | flops 2752512 | bytes 3670024 | tf_op jit(solution)/shard_map/convert_element_type | solution.py:1019
  78.7 2.1 %collective-permute-start.2 = (bf16[896,512]{1,0:T(8,128)(2,1)S(1)}, bf16[896,512]{1,0:T(8,128)(2,1)S(1)}, u32[]{:S(2)}, u32[]{:S(2)}) collective-permute-start(bf16[896,512]{1,0:T(8,128)(2,1)S(1)} %fusion.1.refs_9_), channel_id=1, source_target_pairs={{0,4},{1,3},{2,6},{3,1},{4,0},{5,7},{6,2},{7,5},{8,12},{9,11},{10,... | collective-permute-start | bytes 2752520 | tf_op jit(solution)/shard_map/ppermute | solution.py:998
  80.7 4.5 %all-to-all-start.1 = ((bf16[8,8,1024]{2,1,0:T(8,128)(2,1)}), bf16[8,8,1024]{2,1,0:T(8,128)(2,1)S(1)}, u32[]{:S(2)}, u32[]{:S(2)}) async-start(bf16[8,8,1024]{2,1,0:T(8,128)(2,1)} %bitcast.24), calls=%async_computation.1 | async-start | bytes 262144 | tf_op jit(solution)/shard_map/all_to_all | solution.py:1268
  85.3 11.2 %rollout_grads.1 = (f32[512,1536]{1,0:T(8,128)}, f32[4,128,384]{2,1,0:T(8,128)}, f32[1024,512]{1,0:T(8,128)}, f32[1,1024]{1,0:T(1,128)}) custom-call(bf16[960,1536]{1,0:T(8,128)(2,1)} %get-tuple-element.103.refs_0_, bf16[64,1024]{1,0:T(8,128)(2,1)} %bitcast.116, bf16[896,512]{1,0:T(8,128)(2,1)} %get-tuple-element.85.refs_1_.refs_2_, ...), custom_call_target="tpu_custom_call" | custom-call | tf_op jit(solution)/shard_map/rollout_grads/pallas_call | solution.py:963
  96.5 1.6 fusion.4.refs_22_
  98.1 0.0 copy-start.4
  98.1 2.1 %collective-permute-start.3 = (bf16[448,512]{1,0:T(8,128)(2,1)S(1)}, bf16[448,512]{1,0:T(8,128)(2,1)S(1)}, u32[]{:S(2)}, u32[]{:S(2)}) collective-permute-start(bf16[448,512]{1,0:T(8,128)(2,1)S(1)} %fusion.4.refs_22_), channel_id=1, source_target_pairs={{0,8},{1,17},{2,10},{3,19},{4,12},{5,21},{6,14},{7,23},{8,0},{9,25... | collective-permute-start | bytes 1376264 | tf_op jit(solution)/shard_map/ppermute | solution.py:998
  100.2 17.6 %observe_back.1 = (f32[2,512]{1,0:T(2,128)}, bf16[8,176,512]{2,1,0:T(8,128)(2,1)}, bf16[8,176,512]{2,1,0:T(8,128)(2,1)}) custom-call(s32[1]{0:T(128)} %bitcast.refs_0_, f32[128,512]{1,0:T(8,128)} %get-tuple-element.97.refs_1_, bf16[64,1024]{1,0:T(8,128)(2,1)} %bitcast.122, s32[1,128]{1,0:T(1,128)} %refs_3_.3, s32[2,32,64]{2,1,0:T(8,128)} %bitcast.127, ...), custom_call_target="tpu_custom_call" | custom-call | tf_op jit(solution)/shard_map/observe_back/pallas_call | solution.py:963
  117.7 0.4 collective-permute-start.4
  118.2 3.1 %collective-permute-done.4 = bf16[1408,512]{1,0:T(8,128)(2,1)S(1)} collective-permute-done((bf16[1408,512]{1,0:T(8,128)(2,1)}, bf16[1408,512]{1,0:T(8,128)(2,1)S(1)}, u32[]{:S(2)}, u32[]{:S(2)}) %collective-permute-start.4) | collective-permute-done | bytes 1441824 | tf_op jit(solution)/shard_map/ppermute | solution.py:998
  121.2 1.1 copy-done.6
  122.3 2.2 %fusion.5 = bf16[704,512]{1,0:T(8,128)(2,1)} fusion(bf16[2,704,512]{2,1,0:T(8,128)(2,1)S(1)} %bitcast.111, s32[]{:T(128)S(6)} %select_n.51, bf16[2,704,512]{2,1,0:T(8,128)(2,1)} %bitcast.107), kind=kLoop, calls=%fused_computation.14 | loop fusion | flops 1441792 | bytes 2162692 | tf_op jit(solution)/shard_map/convert_element_type | solution.py:1019
  124.5 1.5 collective-permute-start.5
  126.0 1.6 fusion.3
  127.6 2.4 %collective-permute-start.11 = (bf16[448,512]{1,0:T(8,128)(2,1)S(1)}, bf16[448,512]{1,0:T(8,128)(2,1)S(1)}, u32[]{:S(2)}, u32[]{:S(2)}) collective-permute-start(bf16[448,512]{1,0:T(8,128)(2,1)S(1)} %fusion.3), channel_id=1, source_target_pairs={{0,16},{1,5},{2,18},{3,7},{4,20},{5,1},{6,22},{7,3},{8,24},{9,13},... | collective-permute-start | bytes 1376264 | tf_op jit(solution)/shard_map/ppermute | solution.py:998
  130.0 6.1 %collective-permute-done.5 = bf16[704,512]{1,0:T(8,128)(2,1)} collective-permute-done((bf16[704,512]{1,0:T(8,128)(2,1)}, bf16[704,512]{1,0:T(8,128)(2,1)}, u32[]{:S(2)}, u32[]{:S(2)}) %collective-permute-start.5) | collective-permute-done | bytes 720928 | tf_op jit(solution)/shard_map/ppermute | solution.py:998
  136.1 1.2 fusion.6
  137.3 1.5 collective-permute-start.6
  138.9 2.8 %collective-permute-done.11 = bf16[448,512]{1,0:T(8,128)(2,1)S(1)} collective-permute-done((bf16[448,512]{1,0:T(8,128)(2,1)S(1)}, bf16[448,512]{1,0:T(8,128)(2,1)S(1)}, u32[]{:S(2)}, u32[]{:S(2)}) %collective-permute-start.11) | collective-permute-done | bytes 458784 | tf_op jit(solution)/shard_map/ppermute | solution.py:998
  141.7 0.1 add_convert_fusion.2
  141.8 0.9 collective-permute-start.12
  142.7 2.1 %collective-permute-done.6 = bf16[352,512]{1,0:T(8,128)(2,1)S(1)} collective-permute-done((bf16[352,512]{1,0:T(8,128)(2,1)S(1)}, bf16[352,512]{1,0:T(8,128)(2,1)S(1)}, u32[]{:S(2)}, u32[]{:S(2)}) %collective-permute-start.6) | collective-permute-done | bytes 360480 | tf_op jit(solution)/shard_map/ppermute | solution.py:998
  144.8 1.1 fusion.7
  145.9 1.5 collective-permute-start.7
  147.4 9.8 %collective-permute-done.7 = bf16[176,512]{1,0:T(8,128)(2,1)S(1)} collective-permute-done((bf16[176,512]{1,0:T(8,128)(2,1)S(1)}, bf16[176,512]{1,0:T(8,128)(2,1)S(1)}, u32[]{:S(2)}, u32[]{:S(2)}) %collective-permute-start.7) | collective-permute-done | bytes 180256 | tf_op jit(solution)/shard_map/ppermute | solution.py:998
  157.2 1.1 fusion.9
  158.3 0.8 collective-permute-start.8
  159.2 0.4 maximum_select_fusion.refs_1_
  159.6 1.5 collective-permute-start.13
  161.1 5.3 %collective-permute-done.8 = bf16[176,512]{1,0:T(8,128)(2,1)S(1)} collective-permute-done((bf16[176,512]{1,0:T(8,128)(2,1)S(1)}, bf16[176,512]{1,0:T(8,128)(2,1)S(1)}, u32[]{:S(2)}, u32[]{:S(2)}) %collective-permute-start.8) | collective-permute-done | bytes 180256 | tf_op jit(solution)/shard_map/ppermute | solution.py:998
  166.4 1.3 collective-permute-start.9
  167.7 6.2 %collective-permute-done.9 = bf16[176,512]{1,0:T(8,128)(2,1)S(1)} collective-permute-done((bf16[176,512]{1,0:T(8,128)(2,1)S(1)}, bf16[176,512]{1,0:T(8,128)(2,1)S(1)}, u32[]{:S(2)}, u32[]{:S(2)}) %collective-permute-start.9) | collective-permute-done | bytes 180256 | tf_op jit(solution)/shard_map/ppermute | solution.py:998
  174.0 0.1 maximum_select_fusion.1.refs_1_
  174.1 1.5 collective-permute-start.10
  175.6 0.1 pad_add_fusion.refs_0_
  175.7 3.0 %finish_heads.1 = (f32[1024,512]{1,0:T(8,128)}, f32[128,512]{1,0:T(8,128)}, f32[128,512]{1,0:T(8,128)}, f32[128,1024]{1,0:T(8,128)}, f32[128,1024]{1,0:T(8,128)}) custom-call(s32[2]{0:T(128)S(1)} %pad_add_fusion.refs_0_, bf16[896,512]{1,0:T(8,128)(2,1)S(1)} %maximum_select_fusion.refs_1_, bf16[896,512]{1,0:T(8,128)(2,1)S(1)} %collective-permute-done.13.refs_2_), custom_call_target="tpu_custom_call" | custom-call | tf_op jit(solution)/shard_map/finish_heads/pallas_call | solution.py:963
  178.7 2.9 %collective-permute-done.10.refs_2_ = bf16[352,512]{1,0:T(8,128)(2,1)S(1)} collective-permute-done((bf16[352,512]{1,0:T(8,128)(2,1)S(1)}, bf16[352,512]{1,0:T(8,128)(2,1)S(1)}, u32[]{:S(2)}, u32[]{:S(2)}) %collective-permute-start.10) | collective-permute-done | bytes 360480 | tf_op jit(solution)/shard_map/ppermute | solution.py:998
  181.6 2.1 %finish.1 = (f32[128,1536]{1,0:T(8,128)}, f32[256,512]{1,0:T(8,128)}, f32[2,64,192]{2,1,0:T(8,128)}, f32[1,128]{1,0:T(1,128)}, f32[1,128]{1,0:T(1,128)}, /*index...) custom-call(s32[2]{0:T(128)S(1)} %pad_add_fusion.refs_0_, ...), custom_call_target="tpu_custom_call" | custom-call | tf_op jit(solution)/shard_map/finish/pallas_call | solution.py:963
  (23 shorter events, 0.1 us)
Async XLA Ops:
  0.7 31.6 %copy-start = (s32[2]{0:T(128)S(1)}, s32[2]{0:T(128)}, u32[]{:S(2)}) copy-start(s32[2]{0:T(128)} %refs_0_.1) | copy-start | bytes 28
  25.0 18.7 %all-to-all-start = ((bf16[8,8,1024]{2,1,0:T(8,128)(2,1)}), bf16[8,8,1024]{2,1,0:T(8,128)(2,1)S(1)}, u32[]{:S(2)}, u32[]{:S(2)}) async-start(bf16[8,8,1024]{2,1,0:T(8,128)(2,1)} %bitcast.128), calls=%async_computation | async-start | bytes 262144 | tf_op jit(solution)/shard_map/all_to_all | solution.py:1172
  43.7 7.3 %copy-start.7 = (bf16[8,8,1024]{2,1,0:T(8,128)(2,1)}, bf16[8,8,1024]{2,1,0:T(8,128)(2,1)S(1)}, u32[]{:S(2)}) copy-start(bf16[8,8,1024]{2,1,0:T(8,128)(2,1)S(1)} %all-to-all-done) | copy-start | bytes 393220
  43.8 7.3 %collective-permute-start = (bf16[3584,512]{1,0:T(8,128)(2,1)}, bf16[3584,512]{1,0:T(8,128)(2,1)}, u32[]{:S(2)}, u32[]{:S(2)}) collective-permute-start(bf16[3584,512]{1,0:T(8,128)(2,1)} %bitcast.101), channel_id=1, source_target_pairs={{0,1},{1,0},{2,3},{3,2},{4,5},{5,4},{6,7},{7,6},{8,9},{9,8},{10,11... | collective-permute-start | bytes 11010056 | tf_op jit(solution)/shard_map/ppermute | solution.py:998
  43.8 7.2 %copy-start.3 = (bf16[8,448,512]{2,1,0:T(8,128)(2,1)S(1)}, bf16[8,448,512]{2,1,0:T(8,128)(2,1)}, u32[]{:S(2)}) copy-start(bf16[8,448,512]{2,1,0:T(8,128)(2,1)} %get-tuple-element.89) | copy-start | bytes 11010052
  53.1 1.6 copy-start.1
  53.2 23.4 %collective-permute-start.1 = (bf16[1792,512]{1,0:T(8,128)(2,1)S(1)}, bf16[1792,512]{1,0:T(8,128)(2,1)}, u32[]{:S(2)}, u32[]{:S(2)}) collective-permute-start(bf16[1792,512]{1,0:T(8,128)(2,1)S(1)} %fusion.refs_6_), channel_id=1, source_target_pairs={{0,2},{1,9},{2,0},{3,11},{4,6},{5,13},{6,4},{7,15},{8,10},{9,1},{1... | collective-permute-start | bytes 5505032 | tf_op jit(solution)/shard_map/ppermute | solution.py:998
  78.7 6.6 %copy-start.2 = (bf16[896,512]{1,0:T(8,128)(2,1)}, bf16[896,512]{1,0:T(8,128)(2,1)S(1)}, u32[]{:S(2)}) copy-start(bf16[896,512]{1,0:T(8,128)(2,1)S(1)} %fusion.1.refs_9_) | copy-start | bytes 2752516
  78.7 17.8 %collective-permute-start.2 = (bf16[896,512]{1,0:T(8,128)(2,1)S(1)}, bf16[896,512]{1,0:T(8,128)(2,1)S(1)}, u32[]{:S(2)}, u32[]{:S(2)}) collective-permute-start(bf16[896,512]{1,0:T(8,128)(2,1)S(1)} %fusion.1.refs_9_), channel_id=1, source_target_pairs={{0,4},{1,3},{2,6},{3,1},{4,0},{5,7},{6,2},{7,5},{8,12},{9,11},{10,... | collective-permute-start | bytes 2752520 | tf_op jit(solution)/shard_map/ppermute | solution.py:998
  80.7 15.7 %all-to-all-start.1 = ((bf16[8,8,1024]{2,1,0:T(8,128)(2,1)}), bf16[8,8,1024]{2,1,0:T(8,128)(2,1)S(1)}, u32[]{:S(2)}, u32[]{:S(2)}) async-start(bf16[8,8,1024]{2,1,0:T(8,128)(2,1)} %bitcast.24), calls=%async_computation.1 | async-start | bytes 262144 | tf_op jit(solution)/shard_map/all_to_all | solution.py:1268
  96.5 3.7 %copy-start.8 = (bf16[8,8,1024]{2,1,0:T(8,128)(2,1)}, bf16[8,8,1024]{2,1,0:T(8,128)(2,1)S(1)}, u32[]{:S(2)}) copy-start(bf16[8,8,1024]{2,1,0:T(8,128)(2,1)S(1)} %all-to-all-done.1) | copy-start | bytes 393220
  98.1 2.1 %copy-start.4 = (bf16[448,512]{1,0:T(8,128)(2,1)}, bf16[448,512]{1,0:T(8,128)(2,1)S(1)}, u32[]{:S(2)}) copy-start(bf16[448,512]{1,0:T(8,128)(2,1)S(1)} %fusion.4.refs_22_) | copy-start | bytes 1376260
  98.1 19.7 %collective-permute-start.3 = (bf16[448,512]{1,0:T(8,128)(2,1)S(1)}, bf16[448,512]{1,0:T(8,128)(2,1)S(1)}, u32[]{:S(2)}, u32[]{:S(2)}) collective-permute-start(bf16[448,512]{1,0:T(8,128)(2,1)S(1)} %fusion.4.refs_22_), channel_id=1, source_target_pairs={{0,8},{1,17},{2,10},{3,19},{4,12},{5,21},{6,14},{7,23},{8,0},{9,25... | collective-permute-start | bytes 1376264 | tf_op jit(solution)/shard_map/ppermute | solution.py:998
  117.7 3.5 %collective-permute-start.4 = (bf16[1408,512]{1,0:T(8,128)(2,1)}, bf16[1408,512]{1,0:T(8,128)(2,1)S(1)}, u32[]{:S(2)}, u32[]{:S(2)}) collective-permute-start(bf16[1408,512]{1,0:T(8,128)(2,1)} %bitcast.145), channel_id=1, source_target_pairs={{0,1},{1,0},{2,3},{3,2},{4,5},{5,4},{6,7},{7,6},{8,9},{9,8},{10,11... | collective-permute-start | bytes 4325384 | tf_op jit(solution)/shard_map/ppermute | solution.py:998
  121.2 1.1 copy-start.6
  124.5 11.6 %copy-start.5 = (bf16[8,176,512]{2,1,0:T(8,128)(2,1)S(1)}, bf16[8,176,512]{2,1,0:T(8,128)(2,1)}, u32[]{:S(2)}) copy-start(bf16[8,176,512]{2,1,0:T(8,128)(2,1)} %get-tuple-element.115) | copy-start | bytes 4325380
  124.5 11.6 %collective-permute-start.5 = (bf16[704,512]{1,0:T(8,128)(2,1)}, bf16[704,512]{1,0:T(8,128)(2,1)}, u32[]{:S(2)}, u32[]{:S(2)}) collective-permute-start(bf16[704,512]{1,0:T(8,128)(2,1)} %fusion.5), channel_id=1, source_target_pairs={{0,2},{1,9},{2,0},{3,11},{4,6},{5,13},{6,4},{7,15},{8,10},{9,1},{1... | collective-permute-start | bytes 2162696 | tf_op jit(solution)/shard_map/ppermute | solution.py:998
  127.6 14.1 %collective-permute-start.11 = (bf16[448,512]{1,0:T(8,128)(2,1)S(1)}, bf16[448,512]{1,0:T(8,128)(2,1)S(1)}, u32[]{:S(2)}, u32[]{:S(2)}) collective-permute-start(bf16[448,512]{1,0:T(8,128)(2,1)S(1)} %fusion.3), channel_id=1, source_target_pairs={{0,16},{1,5},{2,18},{3,7},{4,20},{5,1},{6,22},{7,3},{8,24},{9,13},... | collective-permute-start | bytes 1376264 | tf_op jit(solution)/shard_map/ppermute | solution.py:998
  137.3 7.5 %collective-permute-start.6 = (bf16[352,512]{1,0:T(8,128)(2,1)S(1)}, bf16[352,512]{1,0:T(8,128)(2,1)S(1)}, u32[]{:S(2)}, u32[]{:S(2)}) collective-permute-start(bf16[352,512]{1,0:T(8,128)(2,1)S(1)} %fusion.6), channel_id=1, source_target_pairs={{0,4},{1,3},{2,6},{3,1},{4,0},{5,7},{6,2},{7,5},{8,12},{9,11},{10,... | collective-permute-start | bytes 1081352 | tf_op jit(solution)/shard_map/ppermute | solution.py:998
  141.8 17.4 %collective-permute-start.12 = (bf16[448,512]{1,0:T(8,128)(2,1)S(1)}, bf16[448,512]{1,0:T(8,128)(2,1)S(1)}, u32[]{:S(2)}, u32[]{:S(2)}) collective-permute-start(bf16[448,512]{1,0:T(8,128)(2,1)S(1)} %add_convert_fusion.2), channel_id=1, source_target_pairs={{0,8},{1,17},{2,10},{3,19},{4,12},{5,21},{6,14},{7,23},{8,0},{9,25... | collective-permute-start | bytes 1376264 | tf_op jit(solution)/shard_map/ppermute | solution.py:998
  145.9 11.3 %collective-permute-start.7 = (bf16[176,512]{1,0:T(8,128)(2,1)S(1)}, bf16[176,512]{1,0:T(8,128)(2,1)S(1)}, u32[]{:S(2)}, u32[]{:S(2)}) collective-permute-start(bf16[176,512]{1,0:T(8,128)(2,1)S(1)} %fusion.7), channel_id=1, source_target_pairs={{0,8},{1,5},{2,10},{3,7},{4,12},{5,1},{6,14},{7,3},{8,0},{9,13},{1... | collective-permute-start | bytes 540680 | tf_op jit(solution)/shard_map/ppermute | solution.py:998
  158.3 8.0 %collective-permute-start.8 = (bf16[176,512]{1,0:T(8,128)(2,1)S(1)}, bf16[176,512]{1,0:T(8,128)(2,1)S(1)}, u32[]{:S(2)}, u32[]{:S(2)}) collective-permute-start(bf16[176,512]{1,0:T(8,128)(2,1)S(1)} %fusion.9), channel_id=1, source_target_pairs={{0,16},{1,17},{2,18},{3,19},{4,20},{5,21},{6,22},{7,23},{8,24},{9,... | collective-permute-start | bytes 540680 | tf_op jit(solution)/shard_map/ppermute | solution.py:998
  159.6 16.1 %collective-permute-start.13 = (bf16[896,512]{1,0:T(8,128)(2,1)S(1)}, bf16[896,512]{1,0:T(8,128)(2,1)S(1)}, u32[]{:S(2)}, u32[]{:S(2)}) collective-permute-start(bf16[896,512]{1,0:T(8,128)(2,1)S(1)} %maximum_select_fusion.refs_1_), channel_id=1, source_target_pairs={{0,4},{1,9},{2,6},{3,11},{4,0},{5,13},{6,2},{7,15},{8,12},{9,1},{1... | collective-permute-start | bytes 2752520 | tf_op jit(solution)/shard_map/ppermute | solution.py:998
  166.4 7.6 %collective-permute-start.9 = (bf16[176,512]{1,0:T(8,128)(2,1)S(1)}, bf16[176,512]{1,0:T(8,128)(2,1)S(1)}, u32[]{:S(2)}, u32[]{:S(2)}) collective-permute-start(bf16[176,512]{1,0:T(8,128)(2,1)S(1)} %add_convert_fusion.3), channel_id=1, source_target_pairs={{0,8},{1,5},{2,10},{3,7},{4,12},{5,1},{6,14},{7,3},{8,0},{9,13},{1... | collective-permute-start | bytes 540680 | tf_op jit(solution)/shard_map/ppermute | solution.py:998
  174.1 7.5 %collective-permute-start.10 = (bf16[352,512]{1,0:T(8,128)(2,1)S(1)}, bf16[352,512]{1,0:T(8,128)(2,1)S(1)}, u32[]{:S(2)}, u32[]{:S(2)}) collective-permute-start(bf16[352,512]{1,0:T(8,128)(2,1)S(1)} %maximum_select_fusion.1.refs_1_), channel_id=1, source_target_pairs={{0,4},{1,9},{2,6},{3,11},{4,0},{5,13},{6,2},{7,15},{8,12},{9,1},{1... | collective-permute-start | bytes 1081352 | tf_op jit(solution)/shard_map/ppermute | solution.py:998

commit v3 on v2

--- a/solution.py
+++ b/solution.py
@@ -145,6 +145,7 @@
 
 
 def observe_kernel(
+    camera_ref,
     cat_ref,
     table_ref,
     stoch_gain_ref,
@@ -156,6 +157,9 @@
     start_ref,
     order_ref,
     later_cat_ref,
+    embed_ref,
+    camera_scale_ref,
+    post_embed_ref,
     held_ref,
     taken_ref,
     pre_ref,
@@ -167,6 +171,8 @@
     ordered_ref,
     state_ref,
     cell_ref,
+    scaled_ref,
+    embed_part_ref,
     inputs_ref,
 ):
     frames, width = held_ref.shape
@@ -232,26 +238,53 @@
     for ref in (taken_ref, pre_ref, ordered_ref, state_ref, cell_ref):
         ref.flush()
     state = advance(0, start, True)
-    ready(later_cat_ref)
+    ready(later_cat_ref, embed_ref, camera_scale_ref, post_embed_ref)
     steps, _, count = later_cat_ref.shape
     chunks = steps // 2
     share = 7
+    features = embed_ref.shape[1] // (chunks + 1)
+
+    def scale_block(chunk):
+        columns = pl.ds(pl.multiple_of(chunk * features, features), features)
+        for s in range(2):
+            rows = slice(s * length, (s + 1) * length)
+            factor = scale_row(camera_ref, camera_scale_ref, s, columns)
+            scaled_ref[rows, columns] = (embed_ref[rows, columns].astype(f32) * factor).astype(
+                bf16
+            )
+
+    def embed_block(chunk, side):
+        block = features // 2
+        columns = pl.ds(pl.multiple_of(chunk * features + side * block, block), block)
+        return mm(scaled_ref[:, columns], post_embed_ref[columns, :])
+
+    scale_block(chunks)
+    embed_part_ref[...] = embed_block(chunks, 0) + embed_block(chunks, 1)
 
     def several(chunk, state):
         rows = pl.ds(pl.multiple_of(chunk * 2 * count, 2 * count), 2 * count)
-        later_pre = mm(
-            hot_rows([later_cat_ref[2 * chunk], later_cat_ref[2 * chunk + 1]]), table_ref[...]
-        )
-        later_pre_ref[rows, :] = later_pre
-        later = norm_silu(later_pre, stoch_gain_ref[...], stoch_bias_ref[...])
-        later_ref[rows, :] = later.astype(bf16)
+        hot = hot_rows([later_cat_ref[2 * chunk], later_cat_ref[2 * chunk + 1]])
+        later_pre = None
+        block = hot.shape[1] // 4
         for step in range(share):
             state = advance(1 + chunk * share + step, state)
+            if step < 4:
+                columns = slice(step * block, (step + 1) * block)
+                part = mm(hot[:, columns], table_ref[columns, :])
+                later_pre = part if later_pre is None else later_pre + part
+            if step == 3:
+                scale_block(chunk)
+            if step >= 5:
+                embed_part_ref[...] += embed_block(chunk, step - 5)
+            if step == 4:
+                later_pre_ref[rows, :] = later_pre
+                later = norm_silu(later_pre, stoch_gain_ref[...], stoch_bias_ref[...])
+                later_ref[rows, :] = later.astype(bf16)
         return state
 
     state = lax.fori_loop(0, chunks, several, state)
-    later_ref.flush()
-    later_pre_ref.flush()
+    for ref in (later_ref, later_pre_ref, scaled_ref, embed_part_ref):
+        ref.flush()
     lax.fori_loop(1 + chunks * share, length, advance, state, unroll=7)
     gates_ref.flush()
     states_ref.flush()
@@ -278,21 +311,19 @@
 
 def heads_kernel(
     core_ref,
-    camera_ref,
     held_ref,
     prior_hidden_ref,
     prior_gain_ref,
     prior_bias_ref,
     prior_out_ref,
     prior_shift_ref,
-    embed_ref,
-    camera_scale_ref,
     post_deter_ref,
-    post_embed_ref,
+    embed_part_ref,
     post_gain_ref,
     post_bias_ref,
     post_out_ref,
     post_shift_ref,
+    scaled_ref,
     post_low_ref,
     prior_low_ref,
     small_ref,
@@ -300,22 +331,16 @@
     send_ref,
     post_act_ref,
     prior_act_ref,
-    scaled_ref,
 ):
     frames, width = held_ref.shape
-    features = embed_ref.shape[1]
-    length = frames // 2
+    features = scaled_ref.shape[1]
     held = held_ref[...]
     split = (GROUPS, CLASSES, frames)
     prior_pre = mm(held, prior_hidden_ref[...])
     prior_act = norm_silu(prior_pre, prior_gain_ref[...], prior_bias_ref[...]).astype(bf16)
     prior_logits = mm(prior_act, prior_out_ref[...]) + prior_shift_ref[...]
     prior_prob, prior_mix = mixed_probs(prior_logits.T.reshape(split))
-    for s in range(2):
-        rows = slice(s * length, (s + 1) * length)
-        scale = scale_row(camera_ref, camera_scale_ref, s, slice(0, features))
-        scaled_ref[rows, :] = (embed_ref[rows, :].astype(f32) * scale).astype(bf16)
-    post_pre = mm(held, post_deter_ref[...]) + mm(scaled_ref[...], post_embed_ref[...])
+    post_pre = mm(held, post_deter_ref[...]) + embed_part_ref[...]
     post_act = norm_silu(post_pre, post_gain_ref[...], post_bias_ref[...]).astype(bf16)
     post_logits = mm(post_act, post_out_ref[...]) + post_shift_ref[...]
     post_prob, post_mix = mixed_probs(post_logits.T.reshape(split))
@@ -366,10 +391,6 @@
         for y in range(shares // 2):
             share = 2 * y + parity
             places = [block_place(parity, y, block) for block in range(4)]
-            for block in range(4):
-                at = pl.multiple_of(share * embed_rows + block * large, large)
-                grad = mm_tn(scaled_ref[:, pl.ds(at, large)], post_low)
-                ref[places[block], :large, :] = grad.astype(bf16)
             at = pl.multiple_of(share * unit_rows, unit_rows)
             for index, (left, right) in enumerate(products):
                 grad = mm_tn(left[:, pl.ds(at, unit_rows)], right).astype(bf16)
@@ -378,7 +399,18 @@
                     ref[places[block], first : first + small, :] = grad[
                         block * small : (block + 1) * small
                     ]
-        ref.flush()
+            for block in range(4):
+                at = pl.multiple_of(share * embed_rows + block * large, large)
+                grad = mm_tn(scaled_ref[:, pl.ds(at, large)], post_low)
+                ref[places[block], :large, :] = grad.astype(bf16)
+                ref.flush(places[block])
+
+
+def other_place(parity, y, block):
+    low_bit, next_bit = block // 2, block % 2
+    return jnp.where(
+        parity == 0, 4 * low_bit + 2 * y + next_bit, 4 * y + 2 * low_bit + next_bit
+    )
 
 
 def block_place(parity, y, block):
@@ -438,10 +470,11 @@
     cell_ref,
     cot_ref,
     states_ref,
-    held_ref,
     back_ref,
     gate_grad_ref,
     cell_grad_ref,
+    state_grad_ref,
+    held_ref,
     unit_ref,
     scale_ref,
     part_ref,
@@ -491,7 +524,6 @@
     ready(state_ref, cell_ref)
     first = got_ref[:, :width].astype(f32)
     lax.fori_loop(0, horizon, advance, first, unroll=5)
-    held_ref.flush()
     states_ref.flush()
     turned_ref[...] = state_ref[...].astype(f32).T.astype(bf16)
     ready(cot_ref)
@@ -545,6 +577,10 @@
     carry = lax.fori_loop(0, horizon, retreat, jnp.zeros((count, width), f32), unroll=5)
     back_ref[:, :width] = carry.astype(bf16)
     back_ref[:, width:] = mm_nt(gate_grad_ref[:count, :], ordered_ref[...]).astype(bf16)
+    back_ref.flush()
+    gate_grad_ref.flush()
+    for pair in range(PAIRS):
+        state_grad_ref[pair] = mm_tn(held_ref[:, lanes_of(pair)], gate_grad_ref[:, gates_of(pair)])
     cell_grad_ref[...] = jnp.concatenate(
         [
             jnp.sum(gain_grad_ref[...], 0, keepdims=True),
@@ -558,14 +594,12 @@
     gate_grad_ref,
     got_ref,
     inputs_ref,
-    held_ref,
     pre_ref,
     cat_ref,
     ordered_ref,
     stoch_gain_ref,
     stoch_bias_ref,
     input_grad_ref,
-    state_grad_ref,
     table_grad_ref,
     stoch_grad_ref,
     hot_ref,
@@ -578,9 +612,6 @@
     taken_ref[count:, :] = inputs_ref[...]
     input_grad_ref[...] = mm_tn(taken_ref[...], gate_grad_ref[...])
     input_grad_ref.flush()
-    for pair in range(PAIRS):
-        state_grad_ref[pair] = mm_tn(held_ref[:, lanes_of(pair)], gate_grad_ref[:, gates_of(pair)])
-    state_grad_ref.flush()
     gain_sum = jnp.zeros(stoch_gain_ref.shape, f32)
     bias_sum = jnp.zeros(stoch_bias_ref.shape, f32)
     grads = mm_nt(gate_grad_ref[count:, :], ordered_ref[...])
@@ -623,6 +654,8 @@
     start_grad_ref,
     keep_ref,
     send_ref,
+    keep_more_ref,
+    send_more_ref,
     grads_ref,
     turned_ref,
     arriving_ref,
@@ -810,26 +843,27 @@
             lines += [vector[:, at : at + LANES] for at in range(0, vector.shape[1], LANES)]
         lines.append(jnp.zeros((LANES // 2 - len(lines), LANES), f32))
         grads_ref[q, vector_row:, GATE:] = jnp.concatenate(lines, 0).astype(bf16)
-    block = keep_ref.shape[1]
-    for slot, ref in ((0, keep_ref), (1, send_ref)):
+    block, more = keep_ref.shape[1], keep_more_ref.shape[1]
+    for slot, ref, more_ref in ((1, send_ref, send_more_ref), (0, keep_ref, keep_more_ref)):
         parity = core_ref[0] ^ slot
         for y in range(shares // 2):
             for index in range(4):
-                at = index * block
-                ref[block_place(parity, y, index)] = grads_ref[
-                    2 * y + parity, at : at + block, :
-                ]
-
-
-def place_blocks(where_ref, own_ref, got_ref, full_ref):
-    block = own_ref.shape[0] // 2
+                at = index * (block + more)
+                place = block_place(parity, y, index)
+                ref[place] = grads_ref[2 * y + parity, at : at + block, :]
+                place = other_place(parity, y, index)
+                more_ref[place] = grads_ref[2 * y + parity, at + block : at + block + more, :]
+
+
+def place_blocks(where_ref, own_ref, got_ref, full_ref, at=0):
+    block, whole = own_ref.shape[0] // 2, full_ref.shape[0] // 4
     parity, bit = where_ref[0], where_ref[1]
     for side in range(2):
         for inner in range(2):
             rows = slice(inner * block, (inner + 1) * block)
             piece = jnp.where(bit == side, own_ref[rows, :], got_ref[rows, :]).astype(f32)
             place = jnp.where(parity == 0, 2 * side + inner, 2 * inner + side)
-            full_ref[pl.ds(pl.multiple_of(place * block, block), block), :] = piece
+            full_ref[pl.ds(pl.multiple_of(place * whole + at, 16), block), :] = piece
 
 
 def finish_heads_kernel(
@@ -865,10 +899,13 @@
             ref[rows, column : column + width] = full_ref[first : first + small, :]
 
 
-def finish_kernel(where_ref, own_ref, got_ref, *refs):
+def finish_kernel(
+    where_ref, flat_where_ref, own_ref, got_ref, own_more_ref, got_more_ref, *refs
+):
     outs, full_ref = refs[:-1], refs[-1]
     width = own_ref.shape[1]
     place_blocks(where_ref, own_ref, got_ref, full_ref)
+    place_blocks(flat_where_ref, own_more_ref, got_more_ref, full_ref, own_ref.shape[0] // 2)
     input_ref, table_ref, state_ref = outs[:3]
     unit_rows = input_ref.shape[0]
     for pair in range(PAIRS):
@@ -913,9 +950,9 @@
         return self.ref[index]
 
 
-class Outgoing:
-    def __init__(self, ref, copy):
-        self.ref, self.copy, self.shape, self.started = ref, copy, ref.shape, False
+class Near:
+    def __init__(self, ref):
+        self.ref, self.shape = ref, ref.shape
 
     def __getitem__(self, index):
         return self.ref[index]
@@ -924,9 +961,34 @@
         self.ref[index] = value
 
     def flush(self):
-        if not self.started:
-            self.copy.start()
-            self.started = True
+        pass
+
+
+class Outgoing:
+    def __init__(self, ref, target, marks):
+        self.ref, self.target, self.marks = ref, target, marks
+        self.shape, self.copies = ref.shape, []
+
+    def __getitem__(self, index):
+        return self.ref[index]
+
+    def __setitem__(self, index, value):
+        self.ref[index] = value
+
+    def flush(self, part=None):
+        source, target = self.ref, self.target
+        if part is not None:
+            source, target = source.at[part], target.at[part]
+        elif self.copies:
+            return
+        copy = pltpu.make_async_copy(source, target, self.marks[len(self.copies)])
+        copy.start()
+        self.copies.append(copy)
+
+    def finish(self):
+        self.flush()
+        for copy in self.copies:
+            copy.wait()
 
 
 def ready(*refs):
@@ -935,10 +997,23 @@
             ref.ready()
 
 
-def call(kernel, name, outs, ins, mib, scratch=(), scalars=0, after=(), near_in=(), near_out=()):
+def call(
+    kernel,
+    name,
+    outs,
+    ins,
+    mib,
+    scratch=(),
+    scalars=0,
+    after=(),
+    near_in=(),
+    near_out=(),
+    parts=(),
+):
     count, total = len(ins), len(ins) + len(after) + len(outs)
     far_in = [k for k in range(scalars, count) if k not in near_in]
     far_out = [k for k in range(len(outs)) if k not in near_out]
+    pieces = {k: outs[k].shape[0] if k in parts else 1 for k in far_out}
     near = pl.BlockSpec(memory_space=pltpu.VMEM)
     far = pl.BlockSpec(memory_space=pltpu.HBM)
 
@@ -950,15 +1025,19 @@
         for at, k in enumerate(far_in):
             copy = pltpu.make_async_copy(given[k], places[at], marks.at[at])
             given[k] = Incoming(places[at], copy)
-        for at, k in enumerate(far_out, len(far_in)):
-            copy = pltpu.make_async_copy(places[at], made[k], marks.at[at])
-            made[k] = Outgoing(places[at], copy)
+        at = len(far_in)
+        for place, k in zip(places[at:], far_out, strict=True):
+            own = [marks.at[at + part] for part in range(pieces[k])]
+            made[k] = Outgoing(place, made[k], own)
+            at += pieces[k]
+        for k in near_out:
+            made[k] = Near(made[k])
         kernel(*given, *made, *rest)
         ready(*given)
         for k in far_out:
             made[k].flush()
         for k in far_out:
-            made[k].copy.wait()
+            made[k].finish()
 
     return pl.pallas_call(
         body,
@@ -972,7 +1051,7 @@
         scratch_shapes=[pltpu.VMEM(ins[k].shape, ins[k].dtype) for k in far_in]
         + [pltpu.VMEM(outs[k].shape, outs[k].dtype) for k in far_out]
         + list(scratch)
-        + [pltpu.SemaphoreType.DMA((len(far_in) + len(far_out),))],
+        + [pltpu.SemaphoreType.DMA((len(far_in) + sum(pieces.values()),))],
         compiler_params=pltpu.CompilerParams(vmem_limit_bytes=mib * 1024 * 1024),
         name=name,
     )(
@@ -1038,13 +1117,10 @@
 
 
 class Chain:
-    def __init__(self, keep, send, stages, merged):
+    def __init__(self, keep, send, stages, last):
         self.terms, self.piece = Terms(keep), None
-        self.merged = merged
-        self.folds, self.middle = list(stages), stages[-1]
-        if merged:
-            self.folds.pop()
-        self.joins = list(reversed(stages[2:-1])) + [(stages[1][0], stages[0][1])]
+        self.folds, self.middle = list(stages[:-1]), stages[-1]
+        self.joins = list(reversed(stages[2:-1])) + [last]
         self.begin(send, (0, 0))
 
     def begin(self, send, bits):
@@ -1064,7 +1140,7 @@
             self.piece = self.terms.part()
         else:
             bits = self.joins.pop(0)
-            if self.merged and self.last == self.middle:
+            if self.last == self.middle:
                 self.piece = added(self.piece, self.arrived)
             else:
                 self.piece = joined(self.piece, self.arrived, self.last)
@@ -1138,6 +1214,8 @@
         ordered,
         state,
         cell,
+        scaled,
+        embed_part,
     ) = call(
         observe_kernel,
         "observe",
@@ -1153,8 +1231,11 @@
             struct((width, gate_count), bf16),
             struct((width, GATE), bf16),
             struct((2, gate_count), f32),
+            struct((frames, features), bf16),
+            struct((frames, width), f32),
         ],
         (
+            camera,
             cat,
             stoch_table,
             *stoch_rows,
@@ -1165,9 +1246,13 @@
             start_deter,
             start_order,
             later_cat,
+            embed_rows,
+            camera_scale,
+            post_embed,
         ),
-        26,
+        36,
         scratch=[pltpu.VMEM((3 * long, LANES), f32)],
+        scalars=1,
     )
     got = lax.all_to_all(sent, "seq", split_axis=0, concat_axis=0, tiled=True)
 
@@ -1181,36 +1266,34 @@
         [square, square, struct((1, 4 * width + 2 * classes), f32), blocks, blocks],
         (
             core,
-            camera,
             held,
             prior_hidden,
             row(prior_gain),
             row(prior_bias),
             prior_out,
             row(prior_shift),
-            embed_rows,
-            camera_scale,
             post_deter,
-            post_embed,
+            embed_part,
             row(post_gain),
             row(post_bias),
             post_out,
             row(post_shift),
+            scaled,
         ),
         34,
-        scratch=[
-            pltpu.VMEM((frames, width), bf16),
-            pltpu.VMEM((frames, width), bf16),
-            pltpu.VMEM((frames, features), bf16),
-        ],
-        scalars=2,
+        scratch=[pltpu.VMEM((frames, width), bf16), pltpu.VMEM((frames, width), bf16)],
+        scalars=1,
+        parts=(3, 4),
     )
     flat = (shares * head_rows // 2, width)
     send, got = lax.optimization_barrier((send, got))
     tail_stages = list(
         zip([1, low_bit, next_bit] + deeper, [next_bit, 1, low_bit] + deeper, strict=True)
     )
-    head = Chain(keep.reshape(flat), send.reshape(flat), stages, True)
+    more_stages = list(
+        zip([low_bit, 1, next_bit] + deeper, [1, low_bit, next_bit] + deeper, strict=True)
+    )
+    head = Chain(keep.reshape(flat), send.reshape(flat), stages, outer)
     held_grad, embed_grad, camera_grad = call(
         embed_back_kernel,
         "embed_back",
@@ -1235,15 +1318,15 @@
     )
     head.advance(camera_grad)
 
-    states, imag_held, back, gate_grads, cell_part = call(
+    states, back, gate_grads, cell_part, state_part = call(
         rollout_kernel,
         "rollout",
         [
             struct((horizon, count, width), f32),
-            struct((rows, width), bf16),
             struct((count, 2 * width), bf16),
             struct((rows, gate_count), bf16),
             struct((2, gate_count), f32),
+            struct((PAIRS, LANES, GATE), f32),
         ],
         (
             got,
@@ -1255,6 +1338,7 @@
         ),
         36,
         scratch=[
+            pltpu.VMEM((rows, width), bf16),
             pltpu.VMEM((rows, gate_count), f32),
             pltpu.VMEM((rows, LANES), f32),
             pltpu.VMEM((count, gate_count), f32),
@@ -1268,16 +1352,15 @@
     returned = lax.all_to_all(back, "seq", split_axis=0, concat_axis=0, tiled=True)
     head.advance(cell_part)
 
-    input_part, state_part, table_part, stoch_part = call(
+    input_part, table_part, stoch_part = call(
         rollout_grads_kernel,
         "rollout_grads",
         [
             struct((width, gate_count), f32),
-            struct((PAIRS, LANES, GATE), f32),
             struct(stoch_table.shape, f32),
             struct((1, 2 * width), f32),
         ],
-        (gate_grads, got, imag_inputs, imag_held, imag_pre, later_cat, ordered, *stoch_rows),
+        (gate_grads, got, imag_inputs, imag_pre, later_cat, ordered, *stoch_rows),
         30,
         scratch=[
             pltpu.VMEM((stoch_table.shape[0], rows - count), bf16),
@@ -1288,11 +1371,13 @@
     )
     head.advance(stoch_part, returned)
     tail_rows = 5 * unit_rows + half
-    blocks = struct((2 * shares, tail_rows // 4, width), bf16)
-    start_grad, tail_keep, tail_send = call(
+    less = tail_rows // 8 // 16 * 16
+    blocks = struct((2 * shares, tail_rows // 4 - less, width), bf16)
+    more = struct((2 * shares, less, width), bf16)
+    start_grad, tail_keep, tail_send, more_keep, more_send = call(
         observe_back_kernel,
         "observe_back",
-        [struct((seq_count, width), f32), blocks, blocks],
+        [struct((seq_count, width), f32), blocks, blocks, more, more],
         (
             core,
             held_grad,
@@ -1328,21 +1413,28 @@
         ]
         + [pltpu.VMEM((long, LANES), f32)] * 10,
         scalars=1,
-    )
-    full = (2 * tail_rows, width)
+        near_out=(1, 3),
+    )
     tail_send, head.arrived = lax.optimization_barrier((tail_send, head.arrived))
     for _ in deeper:
         head.advance()
-    tail = Chain(tail_keep.reshape(full), tail_send.reshape(full), tail_stages, True)
+    tails = [
+        Chain(keep.reshape(-1, width), send.reshape(-1, width), order, last)
+        for keep, send, order, last in (
+            (tail_keep, tail_send, tail_stages, outer),
+            (more_keep, more_send, more_stages, (low_bit, low_bit)),
+        )
+    ]
     for step in range(2 * len(stages) - 2):
-        if step in (0, 2):
-            head.advance(tail.sent)
-        tail.advance()
+        if step in (1,4):
+            head.advance(tails[0].sent)
+        for tail in tails:
+            tail.advance()
     while head.joins:
-        head.advance(tail.sent)
-    piece, other = tail.piece, tail.arrived
+        head.advance(tails[0].sent)
     head_piece, head_other = head.piece, head.arrived
     where = jnp.concatenate([core, linear_bits(outer).astype(jnp.int32).reshape(1)])
+    flat_where = jnp.stack([0, linear_bits((low_bit, low_bit)).astype(jnp.int32)])
     unit = struct((1, unit_rows), f32)
     logit = struct((1, classes // shares), f32)
     gate = struct((3, LANES), f32)
@@ -1378,11 +1470,11 @@
             gate,
             struct((camera_scale.shape[0], features // shares), f32),
         ],
-        (where, piece, other),
+        (where, flat_where, *[member for tail in tails for member in (tail.piece, tail.arrived)]),
         12,
         scratch=[pltpu.VMEM((tail_rows, width), f32)],
-        scalars=1,
-        near_in=(1, 2),
+        scalars=2,
+        near_in=(2, 3, 4, 5),
         after=(post_embed_grad,),
     )
     input_weight_grad, stoch_table_grad, state_weight_grad = finished[:3]

time: 184 us -> 176 us (0.957)
  waiting for transfers between devices: 41 us -> 26.2 us
  starting transfers between devices: 31.1 us -> 38.2 us
  other arithmetic: 13.7 us -> 17.5 us
  Pallas kernels: 95.8 us -> 92 us
    ppermute x14 -> x21, waiting for transfers between devices: 41 us -> 26.2 us  [swap(): lax.ppermute(values, ('seq', 'rep'), [(i, i ^ 1 << bits[i & 1]) for i in...]
    ppermute x14 -> x21, starting transfers between devices: 19.3 us -> 26.4 us  [swap(): lax.ppermute(values, ('seq', 'rep'), [(i, i ^ 1 << bits[i & 1]) for i in...]
    convert_element_type x8 -> x12, other arithmetic: 12.9 us -> 16.8 us  [part(): return total.astype(bf16)]
    pallas_call x8, Pallas kernels: 95.8 us -> 92 us  [call(): pl.pallas_call(body, out_shape=tuple((pltpu.HBM(out.shape, out.dtype) if...]
  transfers between devices with their start and end apart: 16 -> 23, of which waited for: 9 -> 9; matrix products, arithmetic and copies ran while one was open for 3% -> 7% of each run, Pallas kernels for 38% -> 38%
where the time goes in v3:
time: 176 us
  Pallas kernels  92 us (52%)
  starting transfers between devices  38.2 us (22%)
  waiting for transfers between devices  26.2 us (15%)
  other arithmetic  17.5 us (10%)
    pallas_call x8, Pallas kernels, call(): pl.pallas_call(body, out_shape=tuple((pltpu.HBM(out.shape, out.dtype) if...  92 us
    ppermute x21, starting transfers between devices, swap(): lax.ppermute(values, ('seq', 'rep'), [(i, i ^ 1 << bits[i & 1]) for i in...  26.4 us
    ppermute x21, waiting for transfers between devices, swap(): lax.ppermute(values, ('seq', 'rep'), [(i, i ^ 1 << bits[i & 1]) for i in...  26.2 us
    convert_element_type x12, other arithmetic, part(): return total.astype(bf16)  16.8 us
    all_to_all x1, starting transfers between devices, on_device(): got = lax.all_to_all(sent, 'seq', split_axis=0, concat_axis=0, tiled=True)  7.27 us
    all_to_all x1, starting transfers between devices, on_device(): lax.all_to_all(back, 'seq', split_axis=0, concat_axis=0, tiled=True)  4.53 us
  transfers between devices with their start and end apart: 23, of which 9 were waited for; matrix products, arithmetic and copies ran while one was open for 7% of the time, Pallas kernels for 38%

profile of v3, /device:TPU:0, one launch (start us, length us, event | category | flops | bytes accessed | tf_op | source)
XLA Modules:
  0.0 175.8 jit_solution(4780668954961194174)
XLA Ops:
  1.3 23.9 %observe.1 = (bf16[128,512]{1,0:T(8,128)(2,1)}, bf16[128,512]{1,0:T(8,128)(2,1)}, f32[128,512]{1,0:T(8,128)}, bf16[896,512]{1,0:T(8,128)(2,1)}, f32[896,512]{1,0...) custom-call(s32[2]{0:T(128)S(1)} %copy-done, ...), custom_call_target="tpu_custom_call" | custom-call | tf_op jit(solution)/shard_map/observe/pallas_call | solution.py:1042
  25.3 7.3 %all-to-all-start = ((bf16[8,8,1024]{2,1,0:T(8,128)(2,1)}), bf16[8,8,1024]{2,1,0:T(8,128)(2,1)S(1)}, u32[]{:S(2)}, u32[]{:S(2)}) async-start(bf16[8,8,1024]{2,1,0:T(8,128)(2,1)} %bitcast.164), calls=%async_computation | async-start | bytes 262144 | tf_op jit(solution)/shard_map/all_to_all | solution.py:1257
  32.5 8.6 %heads.1 = (bf16[128,512]{1,0:T(8,128)(2,1)}, bf16[128,512]{1,0:T(8,128)(2,1)}, f32[1,4096]{1,0:T(1,128)}, bf16[8,448,512]{2,1,0:T(8,128)(2,1)}, bf16[8,448,512]{2,1,0:T(8,128)(2,1)}) custom-call(s32[1]{0:T(128)} %bitcast.refs_0_, bf16[128,512]{1,0:T(8,128)(2,1)} %get-tuple-element.84.refs_1_, bf16[512,512]{1,0:T(8,128)(2,1)} %refs_7_.3, ...), custom_call_target="tpu_custom_call" | custom-call | tf_op jit(solution)/shard_map/heads/pallas_call | solution.py:1042
  41.3 7.2 %embed_back.1 = (f32[128,512]{1,0:T(8,128)}, f32[128,4096]{1,0:T(8,128)}, f32[2,4096]{1,0:T(2,128)}) custom-call(s32[2]{0:T(128)S(1)} %copy-done.1, bf16[128,4096]{1,0:T(8,128)(2,1)} %bitcast.142, f32[2,4096]{1,0:T(2,128)} %refs_2_.5, bf16[128,512]{1,0:T(8,128)(2,1)} %get-tuple-element.96.refs_3_, bf16[128,512]{1,0:T(8,128)(2,1)} %get-tuple-element.97.refs_4_, ...), custom_call_target="tpu_custom_call" | custom-call | tf_op jit(solution)/shard_map/embed_back/pallas_call | solution.py:1042
  48.5 2.1 %fusion.refs_6_ = bf16[1792,512]{1,0:T(8,128)(2,1)S(1)} fusion(bf16[2,1792,512]{2,1,0:T(8,128)(2,1)} %bitcast.20, s32[]{:T(128)S(6)} %select_n.67, bf16[2,1792,512]{2,1,0:T(8,128)(2,1)S(1)} %bitcast.148), kind=kLoop, calls=%fused_computation.1 | loop fusion | flops 3670016 | bytes 5505028 | tf_op jit(solution)/shard_map/convert_element_type | solution.py:1098
  50.6 1.6 collective-permute-start.1
  52.2 19.8 %rollout.1 = (f32[15,64,512]{2,1,0:T(8,128)}, bf16[64,1024]{1,0:T(8,128)(2,1)}, bf16[960,1536]{1,0:T(8,128)(2,1)}, f32[2,1536]{1,0:T(2,128)}, f32[4,128,384]{2,1,0:T(8,128)}) custom-call(bf16[64,1024]{1,0:T(8,128)(2,1)} %bitcast.149, bf16[896,512]{1,0:T(8,128)(2,1)} %get-tuple-element.90.refs_1_.refs_2_, ...), custom_call_target="tpu_custom_call" | custom-call | tf_op jit(solution)/shard_map/rollout/pallas_call | solution.py:1042
  72.0 2.0 %collective-permute-done.1 = bf16[1792,512]{1,0:T(8,128)(2,1)} collective-permute-done((bf16[1792,512]{1,0:T(8,128)(2,1)S(1)}, bf16[1792,512]{1,0:T(8,128)(2,1)}, u32[]{:S(2)}, u32[]{:S(2)}) %collective-permute-start.1) | collective-permute-done | bytes 1835040 | tf_op jit(solution)/shard_map/ppermute | solution.py:1077
  74.0 2.1 %fusion.1.refs_8_ = bf16[896,512]{1,0:T(8,128)(2,1)S(1)} fusion(bf16[2,896,512]{2,1,0:T(8,128)(2,1)} %bitcast.29, s32[]{:T(128)S(6)} %select_n.70, bf16[2,2,896,512]{3,2,1,0:T(8,128)(2,1)} %bitcast.27, s32[]{:T(128)S(6)} %select_n.68, bf16[2,2,896,512]{3,2,1,0:T(8,128)(2,1)} %bitcast.145), kind=kLoop, calls=%fused_computation.3 | loop fusion | flops 2752512 | bytes 3670024 | tf_op jit(solution)/shard_map/convert_element_type | solution.py:1098
  76.1 2.1 %collective-permute-start.2 = (bf16[896,512]{1,0:T(8,128)(2,1)S(1)}, bf16[896,512]{1,0:T(8,128)(2,1)S(1)}, u32[]{:S(2)}, u32[]{:S(2)}) collective-permute-start(bf16[896,512]{1,0:T(8,128)(2,1)S(1)} %fusion.1.refs_8_), channel_id=1, source_target_pairs={{0,4},{1,3},{2,6},{3,1},{4,0},{5,7},{6,2},{7,5},{8,12},{9,11},{10,... | collective-permute-start | bytes 2752520 | tf_op jit(solution)/shard_map/ppermute | solution.py:1077
  78.2 4.5 %all-to-all-start.1 = ((bf16[8,8,1024]{2,1,0:T(8,128)(2,1)}), bf16[8,8,1024]{2,1,0:T(8,128)(2,1)S(1)}, u32[]{:S(2)}, u32[]{:S(2)}) async-start(bf16[8,8,1024]{2,1,0:T(8,128)(2,1)} %bitcast.24), calls=%async_computation.1 | async-start | bytes 262144 | tf_op jit(solution)/shard_map/all_to_all | solution.py:1352
  82.7 10.4 %rollout_grads.1 = (f32[512,1536]{1,0:T(8,128)}, f32[1024,512]{1,0:T(8,128)}, f32[1,1024]{1,0:T(1,128)}) custom-call(bf16[960,1536]{1,0:T(8,128)(2,1)} %get-tuple-element.108.refs_0_, bf16[64,1024]{1,0:T(8,128)(2,1)} %bitcast.150, bf16[896,512]{1,0:T(8,128)(2,1)} %get-tuple-element.90.refs_1_.refs_2_, f32[896,512]{1,0:T(8,128)} %get-tuple-element.109.refs_3_, ...), custom_call_target="tpu_custom_call" | custom-call | tf_op jit(solution)/shard_map/rollout_grads/pallas_call | solution.py:1042
  93.1 1.6 fusion.4.refs_22_
  94.7 2.1 %collective-permute-start.3 = (bf16[448,512]{1,0:T(8,128)(2,1)S(1)}, bf16[448,512]{1,0:T(8,128)(2,1)}, u32[]{:S(2)}, u32[]{:S(2)}) collective-permute-start(bf16[448,512]{1,0:T(8,128)(2,1)S(1)} %fusion.4.refs_22_), channel_id=1, source_target_pairs={{0,8},{1,17},{2,10},{3,19},{4,12},{5,21},{6,14},{7,23},{8,0},{9,25... | collective-permute-start | bytes 1376264 | tf_op jit(solution)/shard_map/ppermute | solution.py:1077
  96.8 17.1 %observe_back.1 = (f32[2,512]{1,0:T(2,128)}, bf16[8,96,512]{2,1,0:T(8,128)(2,1)S(1)}, bf16[8,96,512]{2,1,0:T(8,128)(2,1)}, bf16[8,80,512]{2,1,0:T(8,128)(2,1)S(1)}, bf16[8,80,512]{2,1,0:T(8,128)(2,1)}) custom-call(s32[1]{0:T(128)} %bitcast.refs_0_, f32[128,512]{1,0:T(8,128)} %get-tuple-element.102.refs_1_, bf16[64,1024]{1,0:T(8,128)(2,1)} %bitcast.160, ...), custom_call_target="tpu_custom_call" | custom-call | tf_op jit(solution)/shard_map/observe_back/pallas_call | solution.py:1042
  114.5 1.7 fusion.3
  116.2 2.4 %collective-permute-start.18 = (bf16[448,512]{1,0:T(8,128)(2,1)S(1)}, bf16[448,512]{1,0:T(8,128)(2,1)S(1)}, u32[]{:S(2)}, u32[]{:S(2)}) collective-permute-start(bf16[448,512]{1,0:T(8,128)(2,1)S(1)} %fusion.3), channel_id=1, source_target_pairs={{0,16},{1,5},{2,18},{3,7},{4,20},{5,1},{6,22},{7,3},{8,24},{9,13},... | collective-permute-start | bytes 1376264 | tf_op jit(solution)/shard_map/ppermute | solution.py:1077
  118.6 0.8 fusion.7
  119.4 1.5 collective-permute-start.12
  120.9 1.1 fusion.5
  122.0 1.6 collective-permute-start.5
  123.6 4.1 %collective-permute-done.12 = bf16[320,512]{1,0:T(8,128)(2,1)} collective-permute-done((bf16[320,512]{1,0:T(8,128)(2,1)}, bf16[320,512]{1,0:T(8,128)(2,1)}, u32[]{:S(2)}, u32[]{:S(2)}) %collective-permute-start.12) | collective-permute-done | bytes 327712 | tf_op jit(solution)/shard_map/ppermute | solution.py:1077
  127.7 1.6 fusion.8
  129.4 1.3 collective-permute-start.13
  130.7 1.8 %fusion.6 = bf16[192,512]{1,0:T(8,128)(2,1)} fusion(bf16[2,192,512]{2,1,0:T(8,128)(2,1)} %bitcast.52, s32[]{:T(128)S(6)} %select_n.70, bf16[2,2,192,512]{3,2,1,0:T(8,128)(2,1)} %bitcast.50, s32[]{:T(128)S(6)} %select_n.68, bf16[2,2,192,512]{3,2,1,0:T(8,128)(2,1)S(1)} %bitcast.134), kind=kLoop, calls=%fused_computation.17 | loop fusion | flops 589824 | bytes 786440 | tf_op jit(solution)/shard_map/convert_element_type | solution.py:1098
  132.4 1.5 collective-permute-start.6
  134.0 0.7 collective-permute-start.19
  134.8 3.7 %collective-permute-done.6 = bf16[192,512]{1,0:T(8,128)(2,1)} collective-permute-done((bf16[192,512]{1,0:T(8,128)(2,1)}, bf16[192,512]{1,0:T(8,128)(2,1)}, u32[]{:S(2)}, u32[]{:S(2)}) %collective-permute-start.6) | collective-permute-done | bytes 196640 | tf_op jit(solution)/shard_map/ppermute | solution.py:1077
  138.4 1.0 fusion.9
  139.5 0.7 collective-permute-start.7
  140.2 1.0 fusion.12
  141.2 1.4 collective-permute-start.14
  142.6 8.0 %collective-permute-done.7 = bf16[96,512]{1,0:T(8,128)(2,1)S(1)} collective-permute-done((bf16[96,512]{1,0:T(8,128)(2,1)S(1)}, bf16[96,512]{1,0:T(8,128)(2,1)S(1)}, u32[]{:S(2)}, u32[]{:S(2)}) %collective-permute-start.7) | collective-permute-done | bytes 98336 | tf_op jit(solution)/shard_map/ppermute | solution.py:1077
  150.6 1.1 fusion.11
  151.7 0.9 collective-permute-start.8
  153.0 0.8 collective-permute-start.20
  153.8 1.0 fusion.14
  154.8 1.4 collective-permute-start.15
  156.2 2.2 %collective-permute-done.8 = bf16[96,512]{1,0:T(8,128)(2,1)S(1)} collective-permute-done((bf16[96,512]{1,0:T(8,128)(2,1)S(1)}, bf16[96,512]{1,0:T(8,128)(2,1)S(1)}, u32[]{:S(2)}, u32[]{:S(2)}) %collective-permute-start.8) | collective-permute-done | bytes 98336 | tf_op jit(solution)/shard_map/ppermute | solution.py:1077
  158.9 1.4 collective-permute-done.15
  160.4 2.7 %collective-permute-start.16 = (bf16[80,512]{1,0:T(8,128)(2,1)S(1)}, bf16[80,512]{1,0:T(8,128)(2,1)S(1)}, u32[]{:S(2)}, u32[]{:S(2)}) collective-permute-start(bf16[80,512]{1,0:T(8,128)(2,1)S(1)} %add_convert_fusion.5), channel_id=1, source_target_pairs={{0,8},{1,9},{2,10},{3,11},{4,12},{5,13},{6,14},{7,15},{8,0},{9,1},... | collective-permute-start | bytes 245768 | tf_op jit(solution)/shard_map/ppermute | solution.py:1077
  163.0 1.2 collective-permute-done.9
  164.2 0.9 collective-permute-start.10
  165.1 0.8 collective-permute-done.16
  165.9 1.7 collective-permute-start.17
  167.7 3.0 %finish_heads.1 = (f32[1024,512]{1,0:T(8,128)}, f32[128,512]{1,0:T(8,128)}, f32[128,512]{1,0:T(8,128)}, f32[128,1024]{1,0:T(8,128)}, f32[128,1024]{1,0:T(8,128)}) custom-call(s32[2]{0:T(128)S(1)} %get-tuple-element.146.refs_0_, bf16[896,512]{1,0:T(8,128)(2,1)S(1)} %maximum_select_fusion.refs_1_, bf16[896,512]{1,0:T(8,128)(2,1)S(1)} %collective-permute-done.20.refs_2_), custom_call_target="tpu_custom_call" | custom-call | tf_op jit(solution)/shard_map/finish_heads/pallas_call | solution.py:1042
  170.7 2.8 %collective-permute-done.17.refs_5_ = bf16[160,512]{1,0:T(8,128)(2,1)S(1)} collective-permute-done((bf16[160,512]{1,0:T(8,128)(2,1)S(1)}, bf16[160,512]{1,0:T(8,128)(2,1)S(1)}, u32[]{:S(2)}, u32[]{:S(2)}) %collective-permute-start.17) | collective-permute-done | bytes 163872 | tf_op jit(solution)/shard_map/ppermute | solution.py:1077
  173.5 2.1 %finish.1 = (f32[128,1536]{1,0:T(8,128)}, f32[256,512]{1,0:T(8,128)}, f32[2,64,192]{2,1,0:T(8,128)}, f32[1,128]{1,0:T(1,128)}, f32[1,128]{1,0:T(1,128)}, /*index...) custom-call(s32[2]{0:T(128)S(1)} %get-tuple-element.146.refs_0_, ...), custom_call_target="tpu_custom_call" | custom-call | tf_op jit(solution)/shard_map/finish/pallas_call | solution.py:1042
  (41 shorter events, 2.6 us)
Async XLA Ops:
  0.7 0.7 copy-start
  25.3 15.9 %all-to-all-start = ((bf16[8,8,1024]{2,1,0:T(8,128)(2,1)}), bf16[8,8,1024]{2,1,0:T(8,128)(2,1)S(1)}, u32[]{:S(2)}, u32[]{:S(2)}) async-start(bf16[8,8,1024]{2,1,0:T(8,128)(2,1)} %bitcast.164), calls=%async_computation | async-start | bytes 262144 | tf_op jit(solution)/shard_map/all_to_all | solution.py:1257
  32.5 8.7 %copy-start.1 = (s32[2]{0:T(128)S(1)}, s32[2]{0:T(128)}, u32[]{:S(2)}) copy-start(s32[2]{0:T(128)} %refs_0_.3) | copy-start | bytes 28
  41.1 7.3 %copy-start.6 = (bf16[8,8,1024]{2,1,0:T(8,128)(2,1)}, bf16[8,8,1024]{2,1,0:T(8,128)(2,1)S(1)}, u32[]{:S(2)}) copy-start(bf16[8,8,1024]{2,1,0:T(8,128)(2,1)S(1)} %all-to-all-done) | copy-start | bytes 393220
  41.1 7.3 %collective-permute-start = (bf16[3584,512]{1,0:T(8,128)(2,1)}, bf16[3584,512]{1,0:T(8,128)(2,1)}, u32[]{:S(2)}, u32[]{:S(2)}) collective-permute-start(bf16[3584,512]{1,0:T(8,128)(2,1)} %bitcast.143), channel_id=1, source_target_pairs={{0,1},{1,0},{2,3},{3,2},{4,5},{5,4},{6,7},{7,6},{8,9},{9,8},{10,11... | collective-permute-start | bytes 11010056 | tf_op jit(solution)/shard_map/ppermute | solution.py:1077
  41.3 7.2 %copy-start.3 = (bf16[8,448,512]{2,1,0:T(8,128)(2,1)S(1)}, bf16[8,448,512]{2,1,0:T(8,128)(2,1)}, u32[]{:S(2)}) copy-start(bf16[8,448,512]{2,1,0:T(8,128)(2,1)} %get-tuple-element.94) | copy-start | bytes 11010052
  50.6 1.6 copy-start.2
  50.6 23.4 %collective-permute-start.1 = (bf16[1792,512]{1,0:T(8,128)(2,1)S(1)}, bf16[1792,512]{1,0:T(8,128)(2,1)}, u32[]{:S(2)}, u32[]{:S(2)}) collective-permute-start(bf16[1792,512]{1,0:T(8,128)(2,1)S(1)} %fusion.refs_6_), channel_id=1, source_target_pairs={{0,2},{1,9},{2,0},{3,11},{4,6},{5,13},{6,4},{7,15},{8,10},{9,1},{1... | collective-permute-start | bytes 5505032 | tf_op jit(solution)/shard_map/ppermute | solution.py:1077
  76.1 6.6 %copy-start.4 = (bf16[896,512]{1,0:T(8,128)(2,1)}, bf16[896,512]{1,0:T(8,128)(2,1)S(1)}, u32[]{:S(2)}) copy-start(bf16[896,512]{1,0:T(8,128)(2,1)S(1)} %fusion.1.refs_8_) | copy-start | bytes 2752516
  76.1 17.0 %collective-permute-start.2 = (bf16[896,512]{1,0:T(8,128)(2,1)S(1)}, bf16[896,512]{1,0:T(8,128)(2,1)S(1)}, u32[]{:S(2)}, u32[]{:S(2)}) collective-permute-start(bf16[896,512]{1,0:T(8,128)(2,1)S(1)} %fusion.1.refs_8_), channel_id=1, source_target_pairs={{0,4},{1,3},{2,6},{3,1},{4,0},{5,7},{6,2},{7,5},{8,12},{9,11},{10,... | collective-permute-start | bytes 2752520 | tf_op jit(solution)/shard_map/ppermute | solution.py:1077
  78.2 14.9 %all-to-all-start.1 = ((bf16[8,8,1024]{2,1,0:T(8,128)(2,1)}), bf16[8,8,1024]{2,1,0:T(8,128)(2,1)S(1)}, u32[]{:S(2)}, u32[]{:S(2)}) async-start(bf16[8,8,1024]{2,1,0:T(8,128)(2,1)} %bitcast.24), calls=%async_computation.1 | async-start | bytes 262144 | tf_op jit(solution)/shard_map/all_to_all | solution.py:1352
  93.1 3.7 %copy-start.7 = (bf16[8,8,1024]{2,1,0:T(8,128)(2,1)}, bf16[8,8,1024]{2,1,0:T(8,128)(2,1)S(1)}, u32[]{:S(2)}) copy-start(bf16[8,8,1024]{2,1,0:T(8,128)(2,1)S(1)} %all-to-all-done.1) | copy-start | bytes 393220
  94.7 2.1 %copy-start.5 = (bf16[448,512]{1,0:T(8,128)(2,1)}, bf16[448,512]{1,0:T(8,128)(2,1)S(1)}, u32[]{:S(2)}) copy-start(bf16[448,512]{1,0:T(8,128)(2,1)S(1)} %fusion.4.refs_22_) | copy-start | bytes 1376260
  94.7 19.2 %collective-permute-start.3 = (bf16[448,512]{1,0:T(8,128)(2,1)S(1)}, bf16[448,512]{1,0:T(8,128)(2,1)}, u32[]{:S(2)}, u32[]{:S(2)}) collective-permute-start(bf16[448,512]{1,0:T(8,128)(2,1)S(1)} %fusion.4.refs_22_), channel_id=1, source_target_pairs={{0,8},{1,17},{2,10},{3,19},{4,12},{5,21},{6,14},{7,23},{8,0},{9,25... | collective-permute-start | bytes 1376264 | tf_op jit(solution)/shard_map/ppermute | solution.py:1077
  113.9 7.0 %collective-permute-start.4 = (bf16[768,512]{1,0:T(8,128)(2,1)}, bf16[768,512]{1,0:T(8,128)(2,1)}, u32[]{:S(2)}, u32[]{:S(2)}) collective-permute-start(bf16[768,512]{1,0:T(8,128)(2,1)} %bitcast.181), channel_id=1, source_target_pairs={{0,1},{1,0},{2,3},{3,2},{4,5},{5,4},{6,7},{7,6},{8,9},{9,8},{10,11... | collective-permute-start | bytes 2359304 | tf_op jit(solution)/shard_map/ppermute | solution.py:1077
  114.3 4.3 %collective-permute-start.11 = (bf16[640,512]{1,0:T(8,128)(2,1)}, bf16[640,512]{1,0:T(8,128)(2,1)S(1)}, u32[]{:S(2)}, u32[]{:S(2)}) collective-permute-start(bf16[640,512]{1,0:T(8,128)(2,1)} %bitcast.182), channel_id=1, source_target_pairs={{0,1},{1,0},{2,3},{3,2},{4,5},{5,4},{6,7},{7,6},{8,9},{9,8},{10,11... | collective-permute-start | bytes 1966088 | tf_op jit(solution)/shard_map/ppermute | solution.py:1077
  116.2 14.5 %collective-permute-start.18 = (bf16[448,512]{1,0:T(8,128)(2,1)S(1)}, bf16[448,512]{1,0:T(8,128)(2,1)S(1)}, u32[]{:S(2)}, u32[]{:S(2)}) collective-permute-start(bf16[448,512]{1,0:T(8,128)(2,1)S(1)} %fusion.3), channel_id=1, source_target_pairs={{0,16},{1,5},{2,18},{3,7},{4,20},{5,1},{6,22},{7,3},{8,24},{9,13},... | collective-permute-start | bytes 1376264 | tf_op jit(solution)/shard_map/ppermute | solution.py:1077
  119.4 8.3 %collective-permute-start.12 = (bf16[320,512]{1,0:T(8,128)(2,1)}, bf16[320,512]{1,0:T(8,128)(2,1)}, u32[]{:S(2)}, u32[]{:S(2)}) collective-permute-start(bf16[320,512]{1,0:T(8,128)(2,1)} %fusion.7), channel_id=1, source_target_pairs={{0,4},{1,3},{2,6},{3,1},{4,0},{5,7},{6,2},{7,5},{8,12},{9,11},{10,... | collective-permute-start | bytes 983048 | tf_op jit(solution)/shard_map/ppermute | solution.py:1077
  122.0 8.7 %collective-permute-start.5 = (bf16[384,512]{1,0:T(8,128)(2,1)S(1)}, bf16[384,512]{1,0:T(8,128)(2,1)}, u32[]{:S(2)}, u32[]{:S(2)}) collective-permute-start(bf16[384,512]{1,0:T(8,128)(2,1)S(1)} %fusion.5), channel_id=1, source_target_pairs={{0,2},{1,9},{2,0},{3,11},{4,6},{5,13},{6,4},{7,15},{8,10},{9,1},{1... | collective-permute-start | bytes 1179656 | tf_op jit(solution)/shard_map/ppermute | solution.py:1077
  129.4 10.8 %collective-permute-start.13 = (bf16[160,512]{1,0:T(8,128)(2,1)}, bf16[160,512]{1,0:T(8,128)(2,1)}, u32[]{:S(2)}, u32[]{:S(2)}) collective-permute-start(bf16[160,512]{1,0:T(8,128)(2,1)} %fusion.8), channel_id=1, source_target_pairs={{0,2},{1,5},{2,0},{3,7},{4,6},{5,1},{6,4},{7,3},{8,10},{9,13},{10,... | collective-permute-start | bytes 491528 | tf_op jit(solution)/shard_map/ppermute | solution.py:1077
  132.4 6.0 %collective-permute-start.6 = (bf16[192,512]{1,0:T(8,128)(2,1)}, bf16[192,512]{1,0:T(8,128)(2,1)}, u32[]{:S(2)}, u32[]{:S(2)}) collective-permute-start(bf16[192,512]{1,0:T(8,128)(2,1)} %fusion.6), channel_id=1, source_target_pairs={{0,4},{1,3},{2,6},{3,1},{4,0},{5,7},{6,2},{7,5},{8,12},{9,11},{10,... | collective-permute-start | bytes 589832 | tf_op jit(solution)/shard_map/ppermute | solution.py:1077
  134.0 18.6 %collective-permute-start.19 = (bf16[448,512]{1,0:T(8,128)(2,1)S(1)}, bf16[448,512]{1,0:T(8,128)(2,1)S(1)}, u32[]{:S(2)}, u32[]{:S(2)}) collective-permute-start(bf16[448,512]{1,0:T(8,128)(2,1)S(1)} %add_convert_fusion.1), channel_id=1, source_target_pairs={{0,8},{1,17},{2,10},{3,19},{4,12},{5,21},{6,14},{7,23},{8,0},{9,25... | collective-permute-start | bytes 1376264 | tf_op jit(solution)/shard_map/ppermute | solution.py:1077
  139.5 11.2 %collective-permute-start.7 = (bf16[96,512]{1,0:T(8,128)(2,1)S(1)}, bf16[96,512]{1,0:T(8,128)(2,1)S(1)}, u32[]{:S(2)}, u32[]{:S(2)}) collective-permute-start(bf16[96,512]{1,0:T(8,128)(2,1)S(1)} %fusion.9), channel_id=1, source_target_pairs={{0,8},{1,5},{2,10},{3,7},{4,12},{5,1},{6,14},{7,3},{8,0},{9,13},{1... | collective-permute-start | bytes 294920 | tf_op jit(solution)/shard_map/ppermute | solution.py:1077
  141.2 12.7 %collective-permute-start.14 = (bf16[80,512]{1,0:T(8,128)(2,1)S(1)}, bf16[80,512]{1,0:T(8,128)(2,1)S(1)}, u32[]{:S(2)}, u32[]{:S(2)}) collective-permute-start(bf16[80,512]{1,0:T(8,128)(2,1)S(1)} %fusion.12), channel_id=1, source_target_pairs={{0,8},{1,9},{2,10},{3,11},{4,12},{5,13},{6,14},{7,15},{8,0},{9,1},... | collective-permute-start | bytes 245768 | tf_op jit(solution)/shard_map/ppermute | solution.py:1077
  151.7 6.7 %collective-permute-start.8 = (bf16[96,512]{1,0:T(8,128)(2,1)S(1)}, bf16[96,512]{1,0:T(8,128)(2,1)S(1)}, u32[]{:S(2)}, u32[]{:S(2)}) collective-permute-start(bf16[96,512]{1,0:T(8,128)(2,1)S(1)} %fusion.11), channel_id=1, source_target_pairs={{0,16},{1,17},{2,18},{3,19},{4,20},{5,21},{6,22},{7,23},{8,24},{9,... | collective-permute-start | bytes 294920 | tf_op jit(solution)/shard_map/ppermute | solution.py:1077
  153.0 14.7 %collective-permute-start.20 = (bf16[896,512]{1,0:T(8,128)(2,1)S(1)}, bf16[896,512]{1,0:T(8,128)(2,1)S(1)}, u32[]{:S(2)}, u32[]{:S(2)}) collective-permute-start(bf16[896,512]{1,0:T(8,128)(2,1)S(1)} %maximum_select_fusion.refs_1_), channel_id=1, source_target_pairs={{0,4},{1,9},{2,6},{3,11},{4,0},{5,13},{6,2},{7,15},{8,12},{9,1},{1... | collective-permute-start | bytes 2752520 | tf_op jit(solution)/shard_map/ppermute | solution.py:1077
  154.8 5.5 %collective-permute-start.15 = (bf16[80,512]{1,0:T(8,128)(2,1)S(1)}, bf16[80,512]{1,0:T(8,128)(2,1)S(1)}, u32[]{:S(2)}, u32[]{:S(2)}) collective-permute-start(bf16[80,512]{1,0:T(8,128)(2,1)S(1)} %fusion.14), channel_id=1, source_target_pairs={{0,16},{1,17},{2,18},{3,19},{4,20},{5,21},{6,22},{7,23},{8,24},{9,... | collective-permute-start | bytes 245768 | tf_op jit(solution)/shard_map/ppermute | solution.py:1077
  158.4 5.8 %collective-permute-start.9 = (bf16[96,512]{1,0:T(8,128)(2,1)S(1)}, bf16[96,512]{1,0:T(8,128)(2,1)S(1)}, u32[]{:S(2)}, u32[]{:S(2)}) collective-permute-start(bf16[96,512]{1,0:T(8,128)(2,1)S(1)} %add_convert_fusion.4), channel_id=1, source_target_pairs={{0,8},{1,5},{2,10},{3,7},{4,12},{5,1},{6,14},{7,3},{8,0},{9,13},{1... | collective-permute-start | bytes 294920 | tf_op jit(solution)/shard_map/ppermute | solution.py:1077
  160.4 5.5 %collective-permute-start.16 = (bf16[80,512]{1,0:T(8,128)(2,1)S(1)}, bf16[80,512]{1,0:T(8,128)(2,1)S(1)}, u32[]{:S(2)}, u32[]{:S(2)}) collective-permute-start(bf16[80,512]{1,0:T(8,128)(2,1)S(1)} %add_convert_fusion.5), channel_id=1, source_target_pairs={{0,8},{1,9},{2,10},{3,11},{4,12},{5,13},{6,14},{7,15},{8,0},{9,1},... | collective-permute-start | bytes 245768 | tf_op jit(solution)/shard_map/ppermute | solution.py:1077
  164.2 9.2 %collective-permute-start.10 = (bf16[192,512]{1,0:T(8,128)(2,1)S(1)}, bf16[192,512]{1,0:T(8,128)(2,1)S(1)}, u32[]{:S(2)}, u32[]{:S(2)}) collective-permute-start(bf16[192,512]{1,0:T(8,128)(2,1)S(1)} %maximum_select_fusion.1.refs_2_), channel_id=1, source_target_pairs={{0,4},{1,9},{2,6},{3,11},{4,0},{5,13},{6,2},{7,15},{8,12},{9,1},{1... | collective-permute-start | bytes 589832 | tf_op jit(solution)/shard_map/ppermute | solution.py:1077
  165.9 7.6 %collective-permute-start.17 = (bf16[160,512]{1,0:T(8,128)(2,1)S(1)}, bf16[160,512]{1,0:T(8,128)(2,1)S(1)}, u32[]{:S(2)}, u32[]{:S(2)}) collective-permute-start(bf16[160,512]{1,0:T(8,128)(2,1)S(1)} %maximum_select_fusion.2.refs_4_), channel_id=1, source_target_pairs={{0,4},{1,5},{2,6},{3,7},{4,0},{5,1},{6,2},{7,3},{8,12},{9,13},{10,... | collective-permute-start | bytes 491528 | tf_op jit(solution)/shard_map/ppermute | solution.py:1077

commit v4 on v3

--- a/solution.py
+++ b/solution.py
@@ -136,10 +136,14 @@
     return slice(pair * GATE, (pair + 1) * GATE)
 
 
+def camera_of(camera_ref, s):
+    return camera_ref[s] if len(camera_ref.shape) == 1 else camera_ref[:, s : s + 1]
+
+
 def scale_row(camera_ref, camera_scale_ref, s, columns):
     row = None
     for c in range(camera_scale_ref.shape[0]):
-        part = jnp.where(camera_ref[s] == c, camera_scale_ref[c : c + 1, columns], 0.0)
+        part = jnp.where(camera_of(camera_ref, s) == c, camera_scale_ref[c : c + 1, columns], 0.0)
         row = part if row is None else row + part
     return row
 
@@ -178,18 +182,24 @@
     frames, width = held_ref.shape
     length = frames // 2
     half = LANES // 2
+    ready(table_ref)
+    begin(embed_ref, post_embed_ref)
     pre = mm(hot_rows([cat_ref[s] for s in range(2)]), table_ref[...])
     pre_ref[...] = pre
     taken = norm_silu(pre, stoch_gain_ref[...], stoch_bias_ref[...]).astype(bf16)
     taken_ref[...] = taken
     order = column_order()
+    values = []
     for pair in range(PAIRS):
         columns = mm(input_ref[:, gates_of(pair)], order).astype(bf16)
         ordered_ref[:, gates_of(pair)] = columns
-        values = mm(taken, columns)
+        values.append(mm(taken, columns))
+    middle = jnp.sum(values[0] + values[1] + values[2] + values[3], 1, keepdims=True)
+    middle = middle * (1.0 / (PAIRS * GATE))
+    for pair in range(PAIRS):
         for p in range(3):
             at = p * PAIRS * frames + pair * frames
-            inputs_ref[at : at + frames, :] = values[:, lanes_of(p)]
+            inputs_ref[at : at + frames, :] = values[pair][:, lanes_of(p)] - middle
     source, target = iota((3 * half, GATE), 0), iota((3 * half, GATE), 1)
     same = (source // half == target // LANES) & (source % half == target % half)
     weights = mm(weight_ref[...], jnp.where(same, 1.0, 0.0).astype(bf16))
@@ -202,10 +212,9 @@
     )
     row_pair = iota((8, LANES), 0) // 2
     part = iota((8, GATE), 1) // LANES
-    smaller = jnp.where(part == 1, 1.0, 0.5)
-    gain = jnp.concatenate([row for row in gain_rows for _ in range(2)], 0) * smaller
+    gain = jnp.concatenate([row for row in gain_rows for _ in range(2)], 0) * 0.5
     bias = jnp.concatenate([row for row in bias_rows for _ in range(2)], 0)
-    bias = (bias - jnp.where(part == 2, 1.0, 0.0)) * smaller
+    bias = (bias - jnp.where(part == 2, 1.0, 0.0)) * 0.5
     start = jnp.concatenate(
         [start_ref[:, lanes_of(pair)].astype(f32) for pair in range(PAIRS)], 0
     )
@@ -229,19 +238,19 @@
             (parts[p] - mean) * (factor * gain[:, lanes_of(p)]) + bias[:, lanes_of(p)]
             for p in range(3)
         ]
-        reset = 0.5 * jnp.tanh(units[0]) + 0.5
         update = 0.5 * jnp.tanh(units[2]) + 0.5
-        renewed = state + update * (jnp.tanh(reset * units[1]) - state)
+        candidate = jnp.tanh(jnp.tanh(units[0]) * units[1] + units[1])
+        renewed = state + update * (candidate - state)
         states_ref[pl.ds(step, 8, stride=length), :] = renewed
         return renewed
 
     for ref in (taken_ref, pre_ref, ordered_ref, state_ref, cell_ref):
         ref.flush()
     state = advance(0, start, True)
-    ready(later_cat_ref, embed_ref, camera_scale_ref, post_embed_ref)
+    ready(camera_ref, later_cat_ref, embed_ref, camera_scale_ref, post_embed_ref)
     steps, _, count = later_cat_ref.shape
     chunks = steps // 2
-    share = 7
+    share = 8
     features = embed_ref.shape[1] // (chunks + 1)
 
     def scale_block(chunk):
@@ -274,7 +283,7 @@
                 later_pre = part if later_pre is None else later_pre + part
             if step == 3:
                 scale_block(chunk)
-            if step >= 5:
+            if step in (5, 6):
                 embed_part_ref[...] += embed_block(chunk, step - 5)
             if step == 4:
                 later_pre_ref[rows, :] = later_pre
@@ -336,6 +345,8 @@
     features = scaled_ref.shape[1]
     held = held_ref[...]
     split = (GROUPS, CLASSES, frames)
+    ready(prior_hidden_ref)
+    begin(post_out_ref, scaled_ref)
     prior_pre = mm(held, prior_hidden_ref[...])
     prior_act = norm_silu(prior_pre, prior_gain_ref[...], prior_bias_ref[...]).astype(bf16)
     prior_logits = mm(prior_act, prior_out_ref[...]) + prior_shift_ref[...]
@@ -496,23 +507,24 @@
         held_ref[rows, :] = held
         values = []
         total = jnp.zeros((count, LANES), f32)
-        square = jnp.zeros((count, LANES), f32)
         for pair in range(PAIRS):
             value = unit_ref[rows, gates_of(pair)] + mm(
                 held[:, lanes_of(pair)], state_ref[lanes_of(pair), :]
             )
             values.append(value)
             for p in range(3):
-                piece = value[:, lanes_of(p)]
-                total = total + piece
-                square = square + piece * piece
+                total = total + value[:, lanes_of(p)]
         mean = jnp.sum(total, 1, keepdims=True) * norm
-        spread = jnp.sum(square, 1, keepdims=True) * norm - mean * mean
-        factor = lax.rsqrt(jnp.maximum(spread, 0.0) + epsilon)
+        values = [value - mean for value in values]
+        square = jnp.zeros((count, LANES), f32)
+        for value in values:
+            for p in range(3):
+                square = square + value[:, lanes_of(p)] * value[:, lanes_of(p)]
+        factor = lax.rsqrt(jnp.sum(square, 1, keepdims=True) * norm + epsilon)
         scale_ref[rows, :] = jnp.broadcast_to(factor, (count, LANES))
         fresh = []
         for pair in range(PAIRS):
-            units = (values[pair] - mean) * factor
+            units = values[pair] * factor
             unit_ref[rows, gates_of(pair)] = units
             _, _, candidate, update = cell_gates(units, cell_ref, pair)
             old = state[:, lanes_of(pair)]
@@ -610,6 +622,8 @@
     width = inputs_ref.shape[1]
     taken_ref[:count, :] = got_ref[:, width:]
     taken_ref[count:, :] = inputs_ref[...]
+    ready(gate_grad_ref)
+    begin(pre_ref, ordered_ref)
     input_grad_ref[...] = mm_tn(taken_ref[...], gate_grad_ref[...])
     input_grad_ref.flush()
     gain_sum = jnp.zeros(stoch_gain_ref.shape, f32)
@@ -758,10 +772,11 @@
         low_ref[rows, :] = jnp.broadcast_to(low, (8, LANES))
         high_ref[rows, :] = jnp.broadcast_to(high, (8, LANES))
         kept = grad * rest_ref[rows, :] - low * flat_ref[rows, :] - high * lean_ref[rows, :]
-        for pair in range(PAIRS):
-            kept = kept + jnp.where(row_pair == pair, turned[:, lanes_of(pair)], 0.0)
-        return kept
-
+        near = jnp.where(row_pair == 0, turned[:, lanes_of(0)], turned[:, lanes_of(1)])
+        far = jnp.where(row_pair == 2, turned[:, lanes_of(2)], turned[:, lanes_of(3)])
+        return kept + jnp.where(row_pair < 2, near, far)
+
+    begin(ordered_ref, input_part_ref, state_part_ref, table_part_ref)
     carry = lax.fori_loop(0, length, retreat, jnp.zeros((8, LANES), f32), unroll=8)
     for pair in range(PAIRS):
         start_grad_ref[:, lanes_of(pair)] = carry[2 * pair : 2 * pair + 2, :]
@@ -853,6 +868,8 @@
                 ref[place] = grads_ref[2 * y + parity, at : at + block, :]
                 place = other_place(parity, y, index)
                 more_ref[place] = grads_ref[2 * y + parity, at + block : at + block + more, :]
+        ref.flush()
+        more_ref.flush()
 
 
 def place_blocks(where_ref, own_ref, got_ref, full_ref, at=0):
@@ -936,12 +953,19 @@
 
 
 class Incoming:
-    def __init__(self, ref, copy):
-        self.ref, self.copy, self.shape = ref, copy, ref.shape
-        copy.start()
+    def __init__(self, ref, copy, late):
+        self.ref, self.copy, self.shape, self.started = ref, copy, ref.shape, False
+        if not late:
+            self.begin()
+
+    def begin(self):
+        if not self.started:
+            self.copy.start()
+            self.started = True
 
     def ready(self):
         if self.copy is not None:
+            self.begin()
             self.copy.wait()
             self.copy = None
 
@@ -989,6 +1013,12 @@
         self.flush()
         for copy in self.copies:
             copy.wait()
+
+
+def begin(*refs):
+    for ref in refs:
+        if isinstance(ref, Incoming):
+            ref.begin()
 
 
 def ready(*refs):
@@ -1009,6 +1039,7 @@
     near_in=(),
     near_out=(),
     parts=(),
+    late=(),
 ):
     count, total = len(ins), len(ins) + len(after) + len(outs)
     far_in = [k for k in range(scalars, count) if k not in near_in]
@@ -1024,7 +1055,7 @@
         marks = refs[-1]
         for at, k in enumerate(far_in):
             copy = pltpu.make_async_copy(given[k], places[at], marks.at[at])
-            given[k] = Incoming(places[at], copy)
+            given[k] = Incoming(places[at], copy, k in late)
         at = len(far_in)
         for place, k in zip(places[at:], far_out, strict=True):
             own = [marks.at[at + part] for part in range(pieces[k])]
@@ -1235,7 +1266,7 @@
             struct((frames, width), f32),
         ],
         (
-            camera,
+            row(camera),
             cat,
             stoch_table,
             *stoch_rows,
@@ -1252,7 +1283,7 @@
         ),
         36,
         scratch=[pltpu.VMEM((3 * long, LANES), f32)],
-        scalars=1,
+        late=(12, 14),
     )
     got = lax.all_to_all(sent, "seq", split_axis=0, concat_axis=0, tiled=True)
 
@@ -1284,6 +1315,7 @@
         scratch=[pltpu.VMEM((frames, width), bf16), pltpu.VMEM((frames, width), bf16)],
         scalars=1,
         parts=(3, 4),
+        late=(11, 13),
     )
     flat = (shares * head_rows // 2, width)
     send, got = lax.optimization_barrier((send, got))
@@ -1362,6 +1394,7 @@
         ],
         (gate_grads, got, imag_inputs, imag_pre, later_cat, ordered, *stoch_rows),
         30,
+        late=(3, 5),
         scratch=[
             pltpu.VMEM((stoch_table.shape[0], rows - count), bf16),
             pltpu.VMEM((rows - count, width), bf16),
@@ -1414,6 +1447,7 @@
         + [pltpu.VMEM((long, LANES), f32)] * 10,
         scalars=1,
         near_out=(1, 3),
+        late=(12, 15, 16, 17),
     )
     tail_send, head.arrived = lax.optimization_barrier((tail_send, head.arrived))
     for _ in deeper:

time: 176 us -> 175 us (level)
  no operation moved by 1% of the time
where the time goes in v4:
time: 175 us; the launch traced here: 174 us
  Pallas kernels  92.2 us (53%)
  starting transfers between devices  38.2 us (22%)
  waiting for transfers between devices  25.1 us (14%)
  other arithmetic  17.5 us (10%)
    pallas_call x8, Pallas kernels, call(): pl.pallas_call(body, out_shape=tuple((pltpu.HBM(out.shape, out.dtype) if...  92.2 us
    ppermute x21, starting transfers between devices, swap(): lax.ppermute(values, ('seq', 'rep'), [(i, i ^ 1 << bits[i & 1]) for i in...  26.4 us
    ppermute x21, waiting for transfers between devices, swap(): lax.ppermute(values, ('seq', 'rep'), [(i, i ^ 1 << bits[i & 1]) for i in...  25.1 us
    convert_element_type x12, other arithmetic, part(): return total.astype(bf16)  16.8 us
    all_to_all x1, starting transfers between devices, on_device(): got = lax.all_to_all(sent, 'seq', split_axis=0, concat_axis=0, tiled=True)  7.26 us
    all_to_all x1, starting transfers between devices, on_device(): lax.all_to_all(back, 'seq', split_axis=0, concat_axis=0, tiled=True)  4.55 us
  transfers between devices with their start and end apart: 23, of which 9 were waited for; matrix products, arithmetic and copies ran while one was open for 7% of the time, Pallas kernels for 38%

profile of v4, /device:TPU:0, one launch (start us, length us, event | category | flops | bytes accessed | tf_op | source)
XLA Modules:
  0.0 174.2 jit_solution(4406325004177610112)
XLA Ops:
  0.7 23.7 %observe.1 = (bf16[128,512]{1,0:T(8,128)(2,1)}, bf16[128,512]{1,0:T(8,128)(2,1)}, f32[128,512]{1,0:T(8,128)}, bf16[896,512]{1,0:T(8,128)(2,1)}, f32[896,512]{1,0...) custom-call(s32[1,2]{1,0:T(1,128)} %bitcast.142, ...), custom_call_target="tpu_custom_call" | custom-call | tf_op jit(solution)/shard_map/observe/pallas_call | solution.py:1073
  24.3 7.3 %all-to-all-start = ((bf16[8,8,1024]{2,1,0:T(8,128)(2,1)}), bf16[8,8,1024]{2,1,0:T(8,128)(2,1)S(1)}, u32[]{:S(2)}, u32[]{:S(2)}) async-start(bf16[8,8,1024]{2,1,0:T(8,128)(2,1)} %bitcast.166), calls=%async_computation | async-start | bytes 262144 | tf_op jit(solution)/shard_map/all_to_all | solution.py:1288
  31.6 8.6 %heads.1 = (bf16[128,512]{1,0:T(8,128)(2,1)}, bf16[128,512]{1,0:T(8,128)(2,1)}, f32[1,4096]{1,0:T(1,128)}, bf16[8,448,512]{2,1,0:T(8,128)(2,1)}, bf16[8,448,512]{2,1,0:T(8,128)(2,1)}) custom-call(s32[1]{0:T(128)} %bitcast.refs_0_, bf16[128,512]{1,0:T(8,128)(2,1)} %get-tuple-element.84.refs_1_, bf16[512,512]{1,0:T(8,128)(2,1)} %refs_7_.3, ...), custom_call_target="tpu_custom_call" | custom-call | tf_op jit(solution)/shard_map/heads/pallas_call | solution.py:1073
  40.3 7.2 %embed_back.1 = (f32[128,512]{1,0:T(8,128)}, f32[128,4096]{1,0:T(8,128)}, f32[2,4096]{1,0:T(2,128)}) custom-call(s32[2]{0:T(128)S(1)} %copy-done, bf16[128,4096]{1,0:T(8,128)(2,1)} %bitcast.144, f32[2,4096]{1,0:T(2,128)} %refs_2_.5, bf16[128,512]{1,0:T(8,128)(2,1)} %get-tuple-element.96.refs_3_, bf16[128,512]{1,0:T(8,128)(2,1)} %get-tuple-element.97.refs_4_, ...), custom_call_target="tpu_custom_call" | custom-call | tf_op jit(solution)/shard_map/embed_back/pallas_call | solution.py:1073
  47.6 2.1 %fusion.refs_6_ = bf16[1792,512]{1,0:T(8,128)(2,1)S(1)} fusion(bf16[2,1792,512]{2,1,0:T(8,128)(2,1)} %bitcast.21, s32[]{:T(128)S(6)} %select_n.67, bf16[2,1792,512]{2,1,0:T(8,128)(2,1)S(1)} %bitcast.150), kind=kLoop, calls=%fused_computation.1 | loop fusion | flops 3670016 | bytes 5505028 | tf_op jit(solution)/shard_map/convert_element_type | solution.py:1129
  49.6 1.6 collective-permute-start.1
  51.2 20.9 %rollout.1 = (f32[15,64,512]{2,1,0:T(8,128)}, bf16[64,1024]{1,0:T(8,128)(2,1)}, bf16[960,1536]{1,0:T(8,128)(2,1)}, f32[2,1536]{1,0:T(2,128)}, f32[4,128,384]{2,1,0:T(8,128)}) custom-call(bf16[64,1024]{1,0:T(8,128)(2,1)} %bitcast.151, bf16[896,512]{1,0:T(8,128)(2,1)} %get-tuple-element.90.refs_1_.refs_2_, ...), custom_call_target="tpu_custom_call" | custom-call | tf_op jit(solution)/shard_map/rollout/pallas_call | solution.py:1073
  72.1 0.9 collective-permute-done.1
  73.0 2.1 %fusion.1.refs_8_ = bf16[896,512]{1,0:T(8,128)(2,1)S(1)} fusion(bf16[2,896,512]{2,1,0:T(8,128)(2,1)} %bitcast.30, s32[]{:T(128)S(6)} %select_n.70, bf16[2,2,896,512]{3,2,1,0:T(8,128)(2,1)} %bitcast.28, s32[]{:T(128)S(6)} %select_n.68, bf16[2,2,896,512]{3,2,1,0:T(8,128)(2,1)} %bitcast.147), kind=kLoop, calls=%fused_computation.3 | loop fusion | flops 2752512 | bytes 3670024 | tf_op jit(solution)/shard_map/convert_element_type | solution.py:1129
  75.1 2.1 %collective-permute-start.2 = (bf16[896,512]{1,0:T(8,128)(2,1)S(1)}, bf16[896,512]{1,0:T(8,128)(2,1)S(1)}, u32[]{:S(2)}, u32[]{:S(2)}) collective-permute-start(bf16[896,512]{1,0:T(8,128)(2,1)S(1)} %fusion.1.refs_8_), channel_id=1, source_target_pairs={{0,4},{1,3},{2,6},{3,1},{4,0},{5,7},{6,2},{7,5},{8,12},{9,11},{10,... | collective-permute-start | bytes 2752520 | tf_op jit(solution)/shard_map/ppermute | solution.py:1108
  77.2 4.5 %all-to-all-start.1 = ((bf16[8,8,1024]{2,1,0:T(8,128)(2,1)}), bf16[8,8,1024]{2,1,0:T(8,128)(2,1)S(1)}, u32[]{:S(2)}, u32[]{:S(2)}) async-start(bf16[8,8,1024]{2,1,0:T(8,128)(2,1)} %bitcast.25), calls=%async_computation.1 | async-start | bytes 262144 | tf_op jit(solution)/shard_map/all_to_all | solution.py:1384
  81.8 10.4 %rollout_grads.1 = (f32[512,1536]{1,0:T(8,128)}, f32[1024,512]{1,0:T(8,128)}, f32[1,1024]{1,0:T(1,128)}) custom-call(bf16[960,1536]{1,0:T(8,128)(2,1)} %get-tuple-element.108.refs_0_, bf16[64,1024]{1,0:T(8,128)(2,1)} %bitcast.152, bf16[896,512]{1,0:T(8,128)(2,1)} %get-tuple-element.90.refs_1_.refs_2_, f32[896,512]{1,0:T(8,128)} %get-tuple-element.109.refs_3_, ...), custom_call_target="tpu_custom_call" | custom-call | tf_op jit(solution)/shard_map/rollout_grads/pallas_call | solution.py:1073
  92.2 1.6 fusion.4.refs_22_
  93.8 2.1 %collective-permute-start.3 = (bf16[448,512]{1,0:T(8,128)(2,1)S(1)}, bf16[448,512]{1,0:T(8,128)(2,1)}, u32[]{:S(2)}, u32[]{:S(2)}) collective-permute-start(bf16[448,512]{1,0:T(8,128)(2,1)S(1)} %fusion.4.refs_22_), channel_id=1, source_target_pairs={{0,8},{1,17},{2,10},{3,19},{4,12},{5,21},{6,14},{7,23},{8,0},{9,25... | collective-permute-start | bytes 1376264 | tf_op jit(solution)/shard_map/ppermute | solution.py:1108
  95.8 16.5 %observe_back.1 = (f32[2,512]{1,0:T(2,128)}, bf16[8,96,512]{2,1,0:T(8,128)(2,1)S(1)}, bf16[8,96,512]{2,1,0:T(8,128)(2,1)}, bf16[8,80,512]{2,1,0:T(8,128)(2,1)S(1)}, bf16[8,80,512]{2,1,0:T(8,128)(2,1)}) custom-call(s32[1]{0:T(128)} %bitcast.refs_0_, f32[128,512]{1,0:T(8,128)} %get-tuple-element.102.refs_1_, bf16[64,1024]{1,0:T(8,128)(2,1)} %bitcast.162, ...), custom_call_target="tpu_custom_call" | custom-call | tf_op jit(solution)/shard_map/observe_back/pallas_call | solution.py:1073
  112.9 1.7 fusion.3
  114.6 2.4 %collective-permute-start.18 = (bf16[448,512]{1,0:T(8,128)(2,1)S(1)}, bf16[448,512]{1,0:T(8,128)(2,1)S(1)}, u32[]{:S(2)}, u32[]{:S(2)}) collective-permute-start(bf16[448,512]{1,0:T(8,128)(2,1)S(1)} %fusion.3), channel_id=1, source_target_pairs={{0,16},{1,5},{2,18},{3,7},{4,20},{5,1},{6,22},{7,3},{8,24},{9,13},... | collective-permute-start | bytes 1376264 | tf_op jit(solution)/shard_map/ppermute | solution.py:1108
  117.1 0.8 fusion.7
  117.9 1.5 collective-permute-start.12
  119.3 1.1 fusion.5
  120.4 1.6 collective-permute-start.5
  122.0 4.1 %collective-permute-done.12 = bf16[320,512]{1,0:T(8,128)(2,1)} collective-permute-done((bf16[320,512]{1,0:T(8,128)(2,1)}, bf16[320,512]{1,0:T(8,128)(2,1)}, u32[]{:S(2)}, u32[]{:S(2)}) %collective-permute-start.12) | collective-permute-done | bytes 327712 | tf_op jit(solution)/shard_map/ppermute | solution.py:1108
  126.2 1.6 fusion.8
  127.8 1.3 collective-permute-start.13
  129.1 1.8 %fusion.6 = bf16[192,512]{1,0:T(8,128)(2,1)} fusion(bf16[2,192,512]{2,1,0:T(8,128)(2,1)} %bitcast.53, s32[]{:T(128)S(6)} %select_n.70, bf16[2,2,192,512]{3,2,1,0:T(8,128)(2,1)} %bitcast.51, s32[]{:T(128)S(6)} %select_n.68, bf16[2,2,192,512]{3,2,1,0:T(8,128)(2,1)S(1)} %bitcast.135), kind=kLoop, calls=%fused_computation.17 | loop fusion | flops 589824 | bytes 786440 | tf_op jit(solution)/shard_map/convert_element_type | solution.py:1129
  130.9 1.5 collective-permute-start.6
  132.5 0.7 collective-permute-start.19
  133.2 3.7 %collective-permute-done.6 = bf16[192,512]{1,0:T(8,128)(2,1)} collective-permute-done((bf16[192,512]{1,0:T(8,128)(2,1)}, bf16[192,512]{1,0:T(8,128)(2,1)}, u32[]{:S(2)}, u32[]{:S(2)}) %collective-permute-start.6) | collective-permute-done | bytes 196640 | tf_op jit(solution)/shard_map/ppermute | solution.py:1108
  136.9 1.0 fusion.9
  137.9 0.8 collective-permute-start.7
  138.7 1.0 fusion.12
  139.6 1.4 collective-permute-start.14
  141.0 8.0 %collective-permute-done.7 = bf16[96,512]{1,0:T(8,128)(2,1)S(1)} collective-permute-done((bf16[96,512]{1,0:T(8,128)(2,1)S(1)}, bf16[96,512]{1,0:T(8,128)(2,1)S(1)}, u32[]{:S(2)}, u32[]{:S(2)}) %collective-permute-start.7) | collective-permute-done | bytes 98336 | tf_op jit(solution)/shard_map/ppermute | solution.py:1108
  149.1 1.1 fusion.11
  150.1 0.9 collective-permute-start.8
  151.5 0.8 collective-permute-start.20
  152.3 1.0 fusion.14
  153.3 1.4 collective-permute-start.15
  154.7 2.2 %collective-permute-done.8 = bf16[96,512]{1,0:T(8,128)(2,1)S(1)} collective-permute-done((bf16[96,512]{1,0:T(8,128)(2,1)S(1)}, bf16[96,512]{1,0:T(8,128)(2,1)S(1)}, u32[]{:S(2)}, u32[]{:S(2)}) %collective-permute-start.8) | collective-permute-done | bytes 98336 | tf_op jit(solution)/shard_map/ppermute | solution.py:1108
  157.4 1.4 collective-permute-done.15
  158.8 2.7 %collective-permute-start.16 = (bf16[80,512]{1,0:T(8,128)(2,1)S(1)}, bf16[80,512]{1,0:T(8,128)(2,1)S(1)}, u32[]{:S(2)}, u32[]{:S(2)}) collective-permute-start(bf16[80,512]{1,0:T(8,128)(2,1)S(1)} %add_convert_fusion.5), channel_id=1, source_target_pairs={{0,8},{1,9},{2,10},{3,11},{4,12},{5,13},{6,14},{7,15},{8,0},{9,1},... | collective-permute-start | bytes 245768 | tf_op jit(solution)/shard_map/ppermute | solution.py:1108
  161.5 1.2 collective-permute-done.9
  162.7 0.9 collective-permute-start.10
  163.6 0.8 collective-permute-done.16
  164.4 1.7 collective-permute-start.17
  166.1 3.0 %finish_heads.1 = (f32[1024,512]{1,0:T(8,128)}, f32[128,512]{1,0:T(8,128)}, f32[128,512]{1,0:T(8,128)}, f32[128,1024]{1,0:T(8,128)}, f32[128,1024]{1,0:T(8,128)}) custom-call(s32[2]{0:T(128)S(1)} %get-tuple-element.146.refs_0_, bf16[896,512]{1,0:T(8,128)(2,1)S(1)} %maximum_select_fusion.refs_1_, bf16[896,512]{1,0:T(8,128)(2,1)S(1)} %collective-permute-done.20.refs_2_), custom_call_target="tpu_custom_call" | custom-call | tf_op jit(solution)/shard_map/finish_heads/pallas_call | solution.py:1073
  169.1 2.8 %collective-permute-done.17.refs_5_ = bf16[160,512]{1,0:T(8,128)(2,1)S(1)} collective-permute-done((bf16[160,512]{1,0:T(8,128)(2,1)S(1)}, bf16[160,512]{1,0:T(8,128)(2,1)S(1)}, u32[]{:S(2)}, u32[]{:S(2)}) %collective-permute-start.17) | collective-permute-done | bytes 163872 | tf_op jit(solution)/shard_map/ppermute | solution.py:1108
  171.9 2.1 %finish.1 = (f32[128,1536]{1,0:T(8,128)}, f32[256,512]{1,0:T(8,128)}, f32[2,64,192]{2,1,0:T(8,128)}, f32[1,128]{1,0:T(1,128)}, f32[1,128]{1,0:T(1,128)}, /*index...) custom-call(s32[2]{0:T(128)S(1)} %get-tuple-element.146.refs_0_, ...), custom_call_target="tpu_custom_call" | custom-call | tf_op jit(solution)/shard_map/finish/pallas_call | solution.py:1073
  (39 shorter events, 1.9 us)
Async XLA Ops:
  24.3 15.8 %all-to-all-start = ((bf16[8,8,1024]{2,1,0:T(8,128)(2,1)}), bf16[8,8,1024]{2,1,0:T(8,128)(2,1)S(1)}, u32[]{:S(2)}, u32[]{:S(2)}) async-start(bf16[8,8,1024]{2,1,0:T(8,128)(2,1)} %bitcast.166), calls=%async_computation | async-start | bytes 262144 | tf_op jit(solution)/shard_map/all_to_all | solution.py:1288
  31.6 8.7 %copy-start = (s32[2]{0:T(128)S(1)}, s32[2]{0:T(128)}, u32[]{:S(2)}) copy-start(s32[2]{0:T(128)} %refs_0_.1) | copy-start | bytes 28
  40.2 7.3 %copy-start.5 = (bf16[8,8,1024]{2,1,0:T(8,128)(2,1)}, bf16[8,8,1024]{2,1,0:T(8,128)(2,1)S(1)}, u32[]{:S(2)}) copy-start(bf16[8,8,1024]{2,1,0:T(8,128)(2,1)S(1)} %all-to-all-done) | copy-start | bytes 393220
  40.2 7.3 %collective-permute-start = (bf16[3584,512]{1,0:T(8,128)(2,1)}, bf16[3584,512]{1,0:T(8,128)(2,1)}, u32[]{:S(2)}, u32[]{:S(2)}) collective-permute-start(bf16[3584,512]{1,0:T(8,128)(2,1)} %bitcast.145), channel_id=1, source_target_pairs={{0,1},{1,0},{2,3},{3,2},{4,5},{5,4},{6,7},{7,6},{8,9},{9,8},{10,11... | collective-permute-start | bytes 11010056 | tf_op jit(solution)/shard_map/ppermute | solution.py:1108
  40.3 7.2 %copy-start.2 = (bf16[8,448,512]{2,1,0:T(8,128)(2,1)S(1)}, bf16[8,448,512]{2,1,0:T(8,128)(2,1)}, u32[]{:S(2)}) copy-start(bf16[8,448,512]{2,1,0:T(8,128)(2,1)} %get-tuple-element.94) | copy-start | bytes 11010052
  49.6 1.6 copy-start.1
  49.6 23.4 %collective-permute-start.1 = (bf16[1792,512]{1,0:T(8,128)(2,1)S(1)}, bf16[1792,512]{1,0:T(8,128)(2,1)}, u32[]{:S(2)}, u32[]{:S(2)}) collective-permute-start(bf16[1792,512]{1,0:T(8,128)(2,1)S(1)} %fusion.refs_6_), channel_id=1, source_target_pairs={{0,2},{1,9},{2,0},{3,11},{4,6},{5,13},{6,4},{7,15},{8,10},{9,1},{1... | collective-permute-start | bytes 5505032 | tf_op jit(solution)/shard_map/ppermute | solution.py:1108
  75.1 6.6 %copy-start.3 = (bf16[896,512]{1,0:T(8,128)(2,1)}, bf16[896,512]{1,0:T(8,128)(2,1)S(1)}, u32[]{:S(2)}) copy-start(bf16[896,512]{1,0:T(8,128)(2,1)S(1)} %fusion.1.refs_8_) | copy-start | bytes 2752516
  75.1 17.0 %collective-permute-start.2 = (bf16[896,512]{1,0:T(8,128)(2,1)S(1)}, bf16[896,512]{1,0:T(8,128)(2,1)S(1)}, u32[]{:S(2)}, u32[]{:S(2)}) collective-permute-start(bf16[896,512]{1,0:T(8,128)(2,1)S(1)} %fusion.1.refs_8_), channel_id=1, source_target_pairs={{0,4},{1,3},{2,6},{3,1},{4,0},{5,7},{6,2},{7,5},{8,12},{9,11},{10,... | collective-permute-start | bytes 2752520 | tf_op jit(solution)/shard_map/ppermute | solution.py:1108
  77.2 14.9 %all-to-all-start.1 = ((bf16[8,8,1024]{2,1,0:T(8,128)(2,1)}), bf16[8,8,1024]{2,1,0:T(8,128)(2,1)S(1)}, u32[]{:S(2)}, u32[]{:S(2)}) async-start(bf16[8,8,1024]{2,1,0:T(8,128)(2,1)} %bitcast.25), calls=%async_computation.1 | async-start | bytes 262144 | tf_op jit(solution)/shard_map/all_to_all | solution.py:1384
  92.1 3.7 %copy-start.6 = (bf16[8,8,1024]{2,1,0:T(8,128)(2,1)}, bf16[8,8,1024]{2,1,0:T(8,128)(2,1)S(1)}, u32[]{:S(2)}) copy-start(bf16[8,8,1024]{2,1,0:T(8,128)(2,1)S(1)} %all-to-all-done.1) | copy-start | bytes 393220
  93.8 2.1 %copy-start.4 = (bf16[448,512]{1,0:T(8,128)(2,1)}, bf16[448,512]{1,0:T(8,128)(2,1)S(1)}, u32[]{:S(2)}) copy-start(bf16[448,512]{1,0:T(8,128)(2,1)S(1)} %fusion.4.refs_22_) | copy-start | bytes 1376260
  93.8 18.6 %collective-permute-start.3 = (bf16[448,512]{1,0:T(8,128)(2,1)S(1)}, bf16[448,512]{1,0:T(8,128)(2,1)}, u32[]{:S(2)}, u32[]{:S(2)}) collective-permute-start(bf16[448,512]{1,0:T(8,128)(2,1)S(1)} %fusion.4.refs_22_), channel_id=1, source_target_pairs={{0,8},{1,17},{2,10},{3,19},{4,12},{5,21},{6,14},{7,23},{8,0},{9,25... | collective-permute-start | bytes 1376264 | tf_op jit(solution)/shard_map/ppermute | solution.py:1108
  112.3 7.0 %collective-permute-start.4 = (bf16[768,512]{1,0:T(8,128)(2,1)}, bf16[768,512]{1,0:T(8,128)(2,1)}, u32[]{:S(2)}, u32[]{:S(2)}) collective-permute-start(bf16[768,512]{1,0:T(8,128)(2,1)} %bitcast.183), channel_id=1, source_target_pairs={{0,1},{1,0},{2,3},{3,2},{4,5},{5,4},{6,7},{7,6},{8,9},{9,8},{10,11... | collective-permute-start | bytes 2359304 | tf_op jit(solution)/shard_map/ppermute | solution.py:1108
  112.7 4.3 %collective-permute-start.11 = (bf16[640,512]{1,0:T(8,128)(2,1)}, bf16[640,512]{1,0:T(8,128)(2,1)S(1)}, u32[]{:S(2)}, u32[]{:S(2)}) collective-permute-start(bf16[640,512]{1,0:T(8,128)(2,1)} %bitcast.184), channel_id=1, source_target_pairs={{0,1},{1,0},{2,3},{3,2},{4,5},{5,4},{6,7},{7,6},{8,9},{9,8},{10,11... | collective-permute-start | bytes 1966088 | tf_op jit(solution)/shard_map/ppermute | solution.py:1108
  114.6 14.5 %collective-permute-start.18 = (bf16[448,512]{1,0:T(8,128)(2,1)S(1)}, bf16[448,512]{1,0:T(8,128)(2,1)S(1)}, u32[]{:S(2)}, u32[]{:S(2)}) collective-permute-start(bf16[448,512]{1,0:T(8,128)(2,1)S(1)} %fusion.3), channel_id=1, source_target_pairs={{0,16},{1,5},{2,18},{3,7},{4,20},{5,1},{6,22},{7,3},{8,24},{9,13},... | collective-permute-start | bytes 1376264 | tf_op jit(solution)/shard_map/ppermute | solution.py:1108
  117.9 8.3 %collective-permute-start.12 = (bf16[320,512]{1,0:T(8,128)(2,1)}, bf16[320,512]{1,0:T(8,128)(2,1)}, u32[]{:S(2)}, u32[]{:S(2)}) collective-permute-start(bf16[320,512]{1,0:T(8,128)(2,1)} %fusion.7), channel_id=1, source_target_pairs={{0,4},{1,3},{2,6},{3,1},{4,0},{5,7},{6,2},{7,5},{8,12},{9,11},{10,... | collective-permute-start | bytes 983048 | tf_op jit(solution)/shard_map/ppermute | solution.py:1108
  120.4 8.7 %collective-permute-start.5 = (bf16[384,512]{1,0:T(8,128)(2,1)S(1)}, bf16[384,512]{1,0:T(8,128)(2,1)}, u32[]{:S(2)}, u32[]{:S(2)}) collective-permute-start(bf16[384,512]{1,0:T(8,128)(2,1)S(1)} %fusion.5), channel_id=1, source_target_pairs={{0,2},{1,9},{2,0},{3,11},{4,6},{5,13},{6,4},{7,15},{8,10},{9,1},{1... | collective-permute-start | bytes 1179656 | tf_op jit(solution)/shard_map/ppermute | solution.py:1108
  127.8 10.8 %collective-permute-start.13 = (bf16[160,512]{1,0:T(8,128)(2,1)}, bf16[160,512]{1,0:T(8,128)(2,1)}, u32[]{:S(2)}, u32[]{:S(2)}) collective-permute-start(bf16[160,512]{1,0:T(8,128)(2,1)} %fusion.8), channel_id=1, source_target_pairs={{0,2},{1,5},{2,0},{3,7},{4,6},{5,1},{6,4},{7,3},{8,10},{9,13},{10,... | collective-permute-start | bytes 491528 | tf_op jit(solution)/shard_map/ppermute | solution.py:1108
  130.9 6.0 %collective-permute-start.6 = (bf16[192,512]{1,0:T(8,128)(2,1)}, bf16[192,512]{1,0:T(8,128)(2,1)}, u32[]{:S(2)}, u32[]{:S(2)}) collective-permute-start(bf16[192,512]{1,0:T(8,128)(2,1)} %fusion.6), channel_id=1, source_target_pairs={{0,4},{1,3},{2,6},{3,1},{4,0},{5,7},{6,2},{7,5},{8,12},{9,11},{10,... | collective-permute-start | bytes 589832 | tf_op jit(solution)/shard_map/ppermute | solution.py:1108
  132.5 18.6 %collective-permute-start.19 = (bf16[448,512]{1,0:T(8,128)(2,1)S(1)}, bf16[448,512]{1,0:T(8,128)(2,1)S(1)}, u32[]{:S(2)}, u32[]{:S(2)}) collective-permute-start(bf16[448,512]{1,0:T(8,128)(2,1)S(1)} %add_convert_fusion.1), channel_id=1, source_target_pairs={{0,8},{1,17},{2,10},{3,19},{4,12},{5,21},{6,14},{7,23},{8,0},{9,25... | collective-permute-start | bytes 1376264 | tf_op jit(solution)/shard_map/ppermute | solution.py:1108
  137.9 11.2 %collective-permute-start.7 = (bf16[96,512]{1,0:T(8,128)(2,1)S(1)}, bf16[96,512]{1,0:T(8,128)(2,1)S(1)}, u32[]{:S(2)}, u32[]{:S(2)}) collective-permute-start(bf16[96,512]{1,0:T(8,128)(2,1)S(1)} %fusion.9), channel_id=1, source_target_pairs={{0,8},{1,5},{2,10},{3,7},{4,12},{5,1},{6,14},{7,3},{8,0},{9,13},{1... | collective-permute-start | bytes 294920 | tf_op jit(solution)/shard_map/ppermute | solution.py:1108
  139.6 12.7 %collective-permute-start.14 = (bf16[80,512]{1,0:T(8,128)(2,1)S(1)}, bf16[80,512]{1,0:T(8,128)(2,1)S(1)}, u32[]{:S(2)}, u32[]{:S(2)}) collective-permute-start(bf16[80,512]{1,0:T(8,128)(2,1)S(1)} %fusion.12), channel_id=1, source_target_pairs={{0,8},{1,9},{2,10},{3,11},{4,12},{5,13},{6,14},{7,15},{8,0},{9,1},... | collective-permute-start | bytes 245768 | tf_op jit(solution)/shard_map/ppermute | solution.py:1108
  150.1 6.7 %collective-permute-start.8 = (bf16[96,512]{1,0:T(8,128)(2,1)S(1)}, bf16[96,512]{1,0:T(8,128)(2,1)S(1)}, u32[]{:S(2)}, u32[]{:S(2)}) collective-permute-start(bf16[96,512]{1,0:T(8,128)(2,1)S(1)} %fusion.11), channel_id=1, source_target_pairs={{0,16},{1,17},{2,18},{3,19},{4,20},{5,21},{6,22},{7,23},{8,24},{9,... | collective-permute-start | bytes 294920 | tf_op jit(solution)/shard_map/ppermute | solution.py:1108
  151.5 14.7 %collective-permute-start.20 = (bf16[896,512]{1,0:T(8,128)(2,1)S(1)}, bf16[896,512]{1,0:T(8,128)(2,1)S(1)}, u32[]{:S(2)}, u32[]{:S(2)}) collective-permute-start(bf16[896,512]{1,0:T(8,128)(2,1)S(1)} %maximum_select_fusion.refs_1_), channel_id=1, source_target_pairs={{0,4},{1,9},{2,6},{3,11},{4,0},{5,13},{6,2},{7,15},{8,12},{9,1},{1... | collective-permute-start | bytes 2752520 | tf_op jit(solution)/shard_map/ppermute | solution.py:1108
  153.3 5.5 %collective-permute-start.15 = (bf16[80,512]{1,0:T(8,128)(2,1)S(1)}, bf16[80,512]{1,0:T(8,128)(2,1)S(1)}, u32[]{:S(2)}, u32[]{:S(2)}) collective-permute-start(bf16[80,512]{1,0:T(8,128)(2,1)S(1)} %fusion.14), channel_id=1, source_target_pairs={{0,16},{1,17},{2,18},{3,19},{4,20},{5,21},{6,22},{7,23},{8,24},{9,... | collective-permute-start | bytes 245768 | tf_op jit(solution)/shard_map/ppermute | solution.py:1108
  156.9 5.8 %collective-permute-start.9 = (bf16[96,512]{1,0:T(8,128)(2,1)S(1)}, bf16[96,512]{1,0:T(8,128)(2,1)S(1)}, u32[]{:S(2)}, u32[]{:S(2)}) collective-permute-start(bf16[96,512]{1,0:T(8,128)(2,1)S(1)} %add_convert_fusion.4), channel_id=1, source_target_pairs={{0,8},{1,5},{2,10},{3,7},{4,12},{5,1},{6,14},{7,3},{8,0},{9,13},{1... | collective-permute-start | bytes 294920 | tf_op jit(solution)/shard_map/ppermute | solution.py:1108
  158.8 5.5 %collective-permute-start.16 = (bf16[80,512]{1,0:T(8,128)(2,1)S(1)}, bf16[80,512]{1,0:T(8,128)(2,1)S(1)}, u32[]{:S(2)}, u32[]{:S(2)}) collective-permute-start(bf16[80,512]{1,0:T(8,128)(2,1)S(1)} %add_convert_fusion.5), channel_id=1, source_target_pairs={{0,8},{1,9},{2,10},{3,11},{4,12},{5,13},{6,14},{7,15},{8,0},{9,1},... | collective-permute-start | bytes 245768 | tf_op jit(solution)/shard_map/ppermute | solution.py:1108
  162.7 9.2 %collective-permute-start.10 = (bf16[192,512]{1,0:T(8,128)(2,1)S(1)}, bf16[192,512]{1,0:T(8,128)(2,1)S(1)}, u32[]{:S(2)}, u32[]{:S(2)}) collective-permute-start(bf16[192,512]{1,0:T(8,128)(2,1)S(1)} %maximum_select_fusion.1.refs_2_), channel_id=1, source_target_pairs={{0,4},{1,9},{2,6},{3,11},{4,0},{5,13},{6,2},{7,15},{8,12},{9,1},{1... | collective-permute-start | bytes 589832 | tf_op jit(solution)/shard_map/ppermute | solution.py:1108
  164.4 7.6 %collective-permute-start.17 = (bf16[160,512]{1,0:T(8,128)(2,1)S(1)}, bf16[160,512]{1,0:T(8,128)(2,1)S(1)}, u32[]{:S(2)}, u32[]{:S(2)}) collective-permute-start(bf16[160,512]{1,0:T(8,128)(2,1)S(1)} %maximum_select_fusion.2.refs_4_), channel_id=1, source_target_pairs={{0,4},{1,5},{2,6},{3,7},{4,0},{5,1},{6,2},{7,3},{8,12},{9,13},{10,... | collective-permute-start | bytes 491528 | tf_op jit(solution)/shard_map/ppermute | solution.py:1108
